TPU v7x, 32 devices: a whole 2x2x4 slice. The times are simulated.
32 devices in a mesh: vir: 8 (over y, x, core), out: 4 (over z).
Axes of the slice: x: 2, y: 2, z: 4, core: 2. Of those that a mesh axis runs over, the one named last changes fastest.
Arguments:
- factors: bfloat16 [512, 512, 1536], P('out', 'vir'), may hold values from -2.5 to 2.5
- amplitudes: bfloat16 [128, 512, 512], P('out', 'vir'), may hold values from -0.015991211 to 0.015991211
Outputs:
- ladder: float32 [2, 128, 512], P(None, 'vir', 'out')
All inputs are finite; a program needn't handle non-finite values.
Results may differ from a plain program's by a relative error of at most 0.0029.
Values may be sent and summed in bfloat16 or wider, within the bound.
No kernel may reach another device: no remote copies, remote signals or barrier semaphores. Data moves between devices by JAX's collectives and lax.ppermute only.
A program may use at most 128 MiB of HBM per device.

v0:
```python
import functools

import jax
import jax.numpy as jnp
from jax import lax
from jax.experimental import pallas as pl
from jax.experimental.pallas import tpu as pltpu
from jax.sharding import PartitionSpec as P

BB = 2
LANES = 128
NT = (((1,), (1,)), ((), ()))
NN = (((1,), (0,)), ((), ()))
LITTLE = pl.CostEstimate(flops=1024, bytes_accessed=1024, transcendentals=0)


def largest_part(extent, limit):
    part = min(extent, limit)
    while extent % part:
        part -= 1
    return part


def call(kernel, inputs, in_specs, out_shape, out_spec, through, grid=(1,), scratch=(), vmem=28):
    n_in, n_thru = len(inputs), len(through)

    def run(*refs):
        outs = refs[n_in + n_thru :]
        kernel(*refs[:n_in], outs[0], *outs[1 + n_thru :])

    anywhere = pl.BlockSpec(memory_space=pl.ANY)
    out = pl.pallas_call(
        run,
        grid=grid,
        in_specs=list(in_specs) + [anywhere] * n_thru,
        out_specs=[out_spec] + [anywhere] * n_thru,
        out_shape=[out_shape] + [jax.ShapeDtypeStruct(t.shape, t.dtype) for t in through],
        input_output_aliases={n_in + k: 1 + k for k in range(n_thru)},
        scratch_shapes=list(scratch),
        compiler_params=pltpu.CompilerParams(vmem_limit_bytes=vmem * 2**20),
        cost_estimate=LITTLE,
    )(*inputs, *through)
    return out[0], list(out[1:])


def fence(arrays):
    anywhere = [pl.BlockSpec(memory_space=pl.ANY)] * len(arrays)
    return pl.pallas_call(
        lambda *refs: None,
        in_specs=anywhere,
        out_specs=anywhere,
        out_shape=[jax.ShapeDtypeStruct(t.shape, t.dtype) for t in arrays],
        input_output_aliases={k: k for k in range(len(arrays))},
        cost_estimate=LITTLE,
    )(*arrays)


def pack_kernel(*refs):
    for k, slab in enumerate(refs[:-1]):
        refs[-1][k] = slab[...]


def pack(slabs, through):
    vmem = pl.BlockSpec(memory_space=pltpu.VMEM)
    shape = jax.ShapeDtypeStruct((len(slabs),) + slabs[0].shape, slabs[0].dtype)
    return call(pack_kernel, slabs, [vmem] * len(slabs), shape, vmem, through)


def assemble_kernel(*refs):
    place_ref, packs, out_ref, whole_ref = refs[0], refs[1:-2], refs[-2], refs[-1]
    piece = packs[0].shape[2]
    for i, packed in enumerate(packs):
        for k in range(packed.shape[0]):
            start = pl.multiple_of(place_ref[i * packed.shape[0] + k] * piece, piece)
            whole_ref[:, pl.ds(start, piece), :] = packed[k]
    for b in range(out_ref.shape[0]):
        out_ref[b] = whole_ref[b].T


def assemble(packs, places, through):
    count, bb, piece, aux_len = packs[0].shape
    d_len = piece * count * len(packs)
    vmem = pl.BlockSpec(memory_space=pltpu.VMEM)
    return call(
        assemble_kernel,
        [places] + packs,
        [pl.BlockSpec(memory_space=pltpu.SMEM)] + [vmem] * len(packs),
        jax.ShapeDtypeStruct((bb, aux_len, d_len), jnp.bfloat16),
        vmem,
        through,
        scratch=[pltpu.VMEM((bb, d_len, aux_len), jnp.bfloat16)],
    )


def integral_kernel(factor_ref, batch_ref, out_ref):
    a_len, c_len, aux_len = factor_ref.shape
    d_len = out_ref.shape[3]
    rows = factor_ref[...].reshape(a_len * c_len, aux_len)
    wide = largest_part(d_len // LANES, 2) * LANES
    for b in range(out_ref.shape[1]):
        for j in range(0, d_len, wide):
            tile = lax.dot_general(
                rows, batch_ref[b, :, j : j + wide], NN, preferred_element_type=jnp.float32
            )
            turned = jnp.swapaxes(tile.reshape(a_len, c_len, wide), 0, 1)
            out_ref[:, b, :, j : j + wide] = turned.astype(jnp.bfloat16)


def integrals(factors, batch, part, parts, through):
    a_rows, c_rows, aux_len = factors.shape
    bb, _, d_len = batch.shape
    c_len = largest_part(c_rows // parts, 8)
    count = c_rows // parts // c_len
    return call(
        integral_kernel,
        [factors, batch],
        [
            pl.BlockSpec((a_rows, c_len, aux_len), lambda i: (0, part * count + i, 0)),
            pl.BlockSpec((bb, aux_len, d_len), lambda i: (0, 0, 0)),
        ],
        jax.ShapeDtypeStruct((c_rows // parts, bb, a_rows, d_len), jnp.bfloat16),
        pl.BlockSpec((c_len, bb, a_rows, d_len), lambda i: (i, 0, 0, 0)),
        through,
        grid=(count,),
    )


def sums(tau_of, integral_ref, total_ref):
    c_len, bb, a_rows, d_len = integral_ref.shape

    @pl.when(pl.program_id(0) == 0)
    def _():
        total_ref[...] = jnp.zeros_like(total_ref)

    total = total_ref[...]
    for c in range(c_len):
        left = integral_ref[c].reshape(bb * a_rows, d_len)
        total += lax.dot_general(left, tau_of(c), NT, preferred_element_type=jnp.float32)
    total_ref[...] = total


def early_kernel(count, *refs):
    tau_refs, (integral_ref, out_ref, total_ref) = refs[:count], refs[count:]
    sums(
        lambda c: jnp.concatenate([r[c] for r in tau_refs], axis=0),
        integral_ref,
        total_ref,
    )

    @pl.when(pl.program_id(0) == pl.num_programs(0) - 1)
    def _():
        out_ref[...] = total_ref[...].T


def late_kernel(count, *refs):
    (slot_ref, early_ref, added_ref), refs = refs[:3], refs[3:]
    tau_refs, (integral_ref, out_ref, total_ref, all_ref) = refs[:count], refs[count:]
    pairs = tau_refs[0].shape[1]
    sums(
        lambda c: jnp.concatenate([r[c] for r in tau_refs], axis=0),
        integral_ref,
        total_ref,
    )

    @pl.when(pl.program_id(0) == pl.num_programs(0) - 1)
    def _():
        known = early_ref.shape[0]
        all_ref[:known] = early_ref[...]
        all_ref[known:] = added_ref[...] + total_ref[...].T
        for j in range(out_ref.shape[0] // pairs):
            start = pl.multiple_of(slot_ref[j] * pairs, pairs)
            out_ref[j * pairs : (j + 1) * pairs] = all_ref[pl.ds(start, pairs), :]


def ladder_specs(taus, integral, start):
    _, pairs, d_len = taus[0].shape
    c_rows, bb, a_rows, _ = integral.shape
    c_len = largest_part(c_rows, 8)
    first = start // c_len
    specs = [pl.BlockSpec((c_len, pairs, d_len), lambda i: (first + i, 0, 0)) for _ in taus]
    specs.append(pl.BlockSpec((c_len, bb, a_rows, d_len), lambda i: (i, 0, 0, 0)))
    return specs, (bb * a_rows, len(taus) * pairs), (c_rows // c_len,)


def ladder_early(taus, integral, start, through):
    specs, shape, grid = ladder_specs(taus, integral, start)
    return call(
        functools.partial(early_kernel, len(taus)),
        taus + [integral],
        specs,
        jax.ShapeDtypeStruct(shape[::-1], jnp.float32),
        pl.BlockSpec(shape[::-1], lambda i: (0, 0)),
        through,
        grid=grid,
        scratch=[pltpu.VMEM(shape, jnp.float32)],
        vmem=16,
    )


def ladder_late(slots, early, added, taus, integral, start, through):
    specs, shape, grid = ladder_specs(taus, integral, start)
    pairs = taus[0].shape[1]
    out = (slots.shape[0] * pairs, shape[0])
    return call(
        functools.partial(late_kernel, len(taus)),
        [slots, early, added] + taus + [integral],
        [pl.BlockSpec(memory_space=pltpu.SMEM)]
        + [pl.BlockSpec(t.shape, lambda i: (0, 0)) for t in (early, added)]
        + specs,
        jax.ShapeDtypeStruct(out, jnp.float32),
        pl.BlockSpec(out, lambda i: (0, 0)),
        through,
        grid=grid,
        scratch=[
            pltpu.VMEM(shape, jnp.float32),
            pltpu.VMEM((early.shape[0] + shape[1], shape[0]), jnp.float32),
        ],
        vmem=16,
    )


def spread(rows, n, z):
    heres = [lax.ppermute(rows, "out", [(0, k)]) for k in range(n - 1, 0, -1)]
    for k, here in zip(range(n - 1, 0, -1), heres):
        rows = jnp.where(z == k, here, rows)
    return rows


def everywhere(shared, vir, through):
    me = lax.axis_index("vir")

    def swap(array, mask):
        return lax.ppermute(array, "vir", [(k, k ^ mask) for k in range(vir)])

    if vir & (vir - 1) == 0 and 2 < vir <= 8:
        masks = list(range(0, vir, 2))
        slabs = [shared] + [swap(shared, m) for m in masks[1:]]
        packed, through = pack(slabs, through)
        packs = [packed, swap(packed, 1)]
        places = jnp.stack([me ^ m ^ core for core in (0, 1) for m in masks])
    else:
        packs = [lax.all_gather(shared, "vir", axis=1, tiled=True)[None]]
        places = jnp.zeros((1,), jnp.int32)
    return assemble(packs, places.astype(jnp.int32), through)


def body(factors, amplitudes):
    a_rows, c_rows, _ = factors.shape
    n = lax.axis_size("out")
    vir = lax.axis_size("vir")
    z = lax.axis_index("out")

    def send(array, *ways):
        return lax.ppermute(array, "out", ways)

    own = amplitudes.transpose(1, 0, 2)
    token = jnp.zeros((8, LANES), jnp.float32)
    shared = spread(factors[:BB], n, z)
    batch, [token] = everywhere(shared, vir, [token])
    halves = 2 if c_rows % 16 == 0 else 1
    half = c_rows // halves
    made = []

    def make():
        nonlocal token
        part, [token] = integrals(factors, batch, len(made), halves, [token])
        made.append(part)

    make()
    if n == 4:
        far = send(own, (3, 1), (2, 0), (1, 3), (0, 2))
        near = send(own, (1, 0), (2, 3))
        token, far, near, own = fence([token, far, near, own])
        ends = send(far, (1, 0), (2, 3))
        middle = send(own, (2, 1), (1, 2))
        inward = send(own, (3, 2), (0, 1))
        early, late = [own, far, near], [ends, middle, inward]
        slots = jnp.array([[0, 2, 1, 3], [5, 0, 4, 1], [1, 4, 0, 5], [3, 1, 2, 0]], jnp.int32)[z]
    else:
        gathered = lax.all_gather(own, "out")
        early, late = [own], [gathered[k] for k in range(n)]
        slots = jnp.arange(1, n + 1, dtype=jnp.int32)
    while len(made) < halves:
        make()

    known, waiting = None, None
    for k, part in enumerate(made):
        terms, [token] = ladder_early(early, part, k * half, [token])
        known = terms if known is None else known + terms
    for k, part in enumerate(made[:-1]):
        terms, [token] = ladder_early(late, part, k * half, [token])
        waiting = terms if waiting is None else waiting + terms
    if waiting is None:
        waiting = jnp.zeros((sum(t.shape[1] for t in late), BB * a_rows), jnp.float32)
    total, _ = ladder_late(slots, known, waiting, late, made[-1], c_rows - half, [token])

    parts = total.reshape(vir, -1, BB * a_rows)
    swapped = lax.all_to_all(parts, "vir", split_axis=0, concat_axis=0)
    out = jnp.sum(swapped, axis=0)
    return out.reshape(-1, BB, a_rows).transpose(1, 0, 2)


def solution(mesh):
    placed = (P("out", "vir", None), P("out", "vir", None))
    return jax.shard_map(
        body, mesh=mesh, in_specs=placed, out_specs=P(None, "vir", "out"), check_vma=False
    )
```

profile of v0, /device:TPU:16, one launch (start us, length us, event | category | flops | bytes accessed | tf_op | source)
XLA Modules:
  0.0 192.2 jit_solution(2828857642199254813)
XLA Ops:
  0.0 1.0 slice.3
  1.0 0.7 collective-permute-start
  1.7 1.3 collective-permute-start.1
  3.0 1.4 collective-permute-start.2
  4.4 2.8 %copy.20 = bf16[32,64,512]{2,0,1:T(8,128)(2,1)S(1)} copy(bf16[32,64,512]{2,1,0:T(8,128)(2,1)} %param.4) | data formatting | bytes 4194304 | tf_op args[1]
  7.2 0.0 copy-start.1
  7.2 4.6 %collective-permute-start.7 = (bf16[64,32,512]{2,1,0:T(8,128)(2,1)S(1)}, bf16[64,32,512]{2,1,0:T(8,128)(2,1)}, u32[]{:S(2)}, u32[]{:S(2)}) collective-permute-start(bf16[64,32,512]{2,1,0:T(8,128)(2,1)S(1)} %bitcast.17), channel_id=1, source_target_pairs={{3,1},{2,0},{1,3},{0,2},{7,5},{6,4},{5,7},{4,6},{11,9},{10,8},{9,1... | collective-permute-start | bytes 6291464 | tf_op jit(solution)/shard_map/ppermute | solution.py:254
  11.8 2.6 %collective-permute-start.8 = (bf16[64,32,512]{2,1,0:T(8,128)(2,1)S(1)}, bf16[64,32,512]{2,1,0:T(8,128)(2,1)}, u32[]{:S(2)}, u32[]{:S(2)}) collective-permute-start(bf16[64,32,512]{2,1,0:T(8,128)(2,1)S(1)} %bitcast.18), channel_id=1, source_target_pairs={{1,0},{2,3},{5,4},{6,7},{9,8},{10,11},{13,12},{14,15},{17,16},{18,... | collective-permute-start | bytes 6291464 | tf_op jit(solution)/shard_map/ppermute | solution.py:254
  14.4 0.0 collective-permute-done
  14.5 8.9 %collective-permute-done.1 = bf16[2,64,1536]{2,1,0:T(8,128)(2,1)S(1)} collective-permute-done((bf16[2,64,1536]{2,1,0:T(8,128)(2,1)S(1)}, bf16[2,64,1536]{2,1,0:T(8,128)(2,1)S(1)}, u32[]{:S(2)}, u32[]{:S(2)}) %collective-permute-start.1) | collective-permute-done | bytes 393248 | tf_op jit(solution)/shard_map/ppermute | solution.py:223
  23.3 0.0 collective-permute-done.2
  23.3 1.1 select_select_fusion.refs_0_
  24.4 1.6 collective-permute-start.3
  26.0 1.5 collective-permute-start.4
  27.5 0.5 collective-permute-start.5
  28.0 8.6 %collective-permute-done.3.refs_1_ = bf16[2,64,1536]{2,1,0:T(8,128)(2,1)S(1)} collective-permute-done((bf16[2,64,1536]{2,1,0:T(8,128)(2,1)S(1)}, bf16[2,64,1536]{2,1,0:T(8,128)(2,1)S(1)}, u32[]{:S(2)}, u32[]{:S(2)}) %collective-permute-start.3) | collective-permute-done | bytes 393248 | tf_op jit(solution)/shard_map/ppermute | solution.py:233
  36.5 6.4 %collective-permute-done.4.refs_2_ = bf16[2,64,1536]{2,1,0:T(8,128)(2,1)S(1)} collective-permute-done((bf16[2,64,1536]{2,1,0:T(8,128)(2,1)S(1)}, bf16[2,64,1536]{2,1,0:T(8,128)(2,1)S(1)}, u32[]{:S(2)}, u32[]{:S(2)}) %collective-permute-start.4) | collective-permute-done | bytes 393248 | tf_op jit(solution)/shard_map/ppermute | solution.py:233
  42.9 0.0 collective-permute-done.5.refs_3_
  42.9 1.3 shard_map.37
  44.2 0.0 collective-permute-start.6
  44.2 0.1 stack.35.refs_0_
  44.3 3.7 %collective-permute-done.6.refs_2_ = bf16[4,2,64,1536]{3,2,1,0:T(8,128)(2,1)} collective-permute-done((bf16[4,2,64,1536]{3,2,1,0:T(8,128)(2,1)}, bf16[4,2,64,1536]{3,2,1,0:T(8,128)(2,1)}, u32[]{:S(2)}, u32[]{:S(2)}) %collective-permute-start.6) | collective-permute-done | bytes 1572896 | tf_op jit(solution)/shard_map/ppermute | solution.py:233
  47.9 3.0 %shard_map.38 = (bf16[2,1536,512]{2,1,0:T(8,128)(2,1)S(1)}, f32[8,128]{1,0:T(8,128)S(1)}) custom-call(s32[8]{0:T(128)S(1)} %stack.35.refs_0_, bf16[4,2,64,1536]{3,2,1,0:T(8,128)(2,1)} %get-tuple-element.24.refs_1_, bf16[4,2,64,1536]{3,2,1,0:T(8,128)(2,1)} %collective-permute-done.6.refs_2_, ...), custom_call_target="tpu_custom_call", output_to_operand_aliasing={{1}: (3, {})} | custom-call | flops 1024 | bytes 1024 | tf_op jit(solution)/shard_map/pallas_call | solution.py:32
  50.9 0.0 copy-done.1
  50.9 0.0 copy-start.3
  50.9 17.5 %shard_map.39 = (bf16[32,2,128,512]{3,2,1,0:T(8,128)(2,1)S(1)}, f32[8,128]{1,0:T(8,128)S(1)}) custom-call(bf16[128,64,1536]{2,1,0:T(8,128)(2,1)} %refs_0_.3, bf16[2,1536,512]{2,1,0:T(8,128)(2,1)S(1)} %get-tuple-element.26.refs_1_, f32[8,128]{1,0:T(8,128)S(1)} %get-tuple-element.27.refs_2_), custom_call_target="tpu_custom_call", output_to_operand_aliasing={{1}: (2, {})} | custom-call | flops 1024 | bytes 1024 | tf_op jit(solution)/shard_map/pallas_call | solution.py:32
  68.5 0.0 copy-done.3
  68.5 0.0 copy-start
  68.5 3.3 %copy-done = bf16[32,2,128,512]{3,2,1,0:T(8,128)(2,1)} copy-done((bf16[32,2,128,512]{3,2,1,0:T(8,128)(2,1)}, bf16[32,2,128,512]{3,2,1,0:T(8,128)(2,1)S(1)}, u32[]{:S(2)}) %copy-start) | copy-done | bytes 8388632
  71.7 0.0 copy-start.5
  71.7 0.6 copy-done.5
  72.3 26.1 %collective-permute-done.7.refs_1_ = bf16[64,32,512]{2,1,0:T(8,128)(2,1)} collective-permute-done((bf16[64,32,512]{2,1,0:T(8,128)(2,1)S(1)}, bf16[64,32,512]{2,1,0:T(8,128)(2,1)}, u32[]{:S(2)}, u32[]{:S(2)}) %collective-permute-start.7) | collective-permute-done | bytes 2097184 | tf_op jit(solution)/shard_map/ppermute | solution.py:254
  98.5 0.0 collective-permute-done.8.refs_2_
  98.5 0.0 copy-start.4
  98.5 23.3 %collective-permute-start.9 = (bf16[64,32,512]{2,1,0:T(8,128)(2,1)}, bf16[64,32,512]{2,1,0:T(8,128)(2,1)}, u32[]{:S(2)}, u32[]{:S(2)}) collective-permute-start(bf16[64,32,512]{2,1,0:T(8,128)(2,1)} %get-tuple-element.30.refs_1_), channel_id=1, source_target_pairs={{1,0},{2,3},{5,4},{6,7},{9,8},{10,11},{13,12},{14,15},{17,16},{18,... | collective-permute-start | bytes 6291464 | tf_op jit(solution)/shard_map/ppermute | solution.py:254
  121.8 1.9 collective-permute-start.10
  123.7 1.3 collective-permute-start.11
  125.0 0.7 dynamic-slice_bitcast_fusion.refs_0_
  125.7 0.0 slice-start
  125.7 0.0 copy-done.4
  125.7 0.0 copy-start.6
  125.7 0.8 copy-done.6
  126.6 0.0 slice-start.1
  126.6 0.0 copy-start.2
  126.6 16.8 %shard_map.41 = (bf16[32,2,128,512]{3,2,1,0:T(8,128)(2,1)S(1)}, f32[8,128]{1,0:T(8,128)S(1)}) custom-call(bf16[128,64,1536]{2,1,0:T(8,128)(2,1)} %refs_0_.3, bf16[2,1536,512]{2,1,0:T(8,128)(2,1)S(1)} %copy-done.4, f32[8,128]{1,0:T(8,128)S(1)} %copy-done.6), custom_call_target="tpu_custom_call", output_to_operand_aliasing={{1}: (2, {})} | custom-call | flops 1024 | bytes 1024 | tf_op jit(solution)/shard_map/pallas_call | solution.py:32
  143.4 0.0 copy-start.7
  143.4 0.6 copy-done.7
  144.0 0.0 slice-done
  144.0 0.0 slice-done.1
  144.0 0.0 copy-done.2
  144.0 0.0 copy-start.8
  144.0 0.7 copy-done.8
  144.7 4.3 %shard_map.42 = (f32[96,256]{1,0:T(8,128)S(1)}, f32[8,128]{1,0:T(8,128)S(1)}) custom-call(bf16[64,32,512]{2,1,0:T(8,128)(2,1)S(1)} %copy-done.2, bf16[64,32,512]{2,1,0:T(8,128)(2,1)} %get-tuple-element.30.refs_1_, bf16[64,32,512]{2,1,0:T(8,128)(2,1)} %get-tuple-element.31.refs_2_, ...), custom_call_target="tpu_custom_call", output_to_operand_aliasing={{1}: (4, {})} | custom-call | flops 1024 | bytes 1024 | tf_op jit(solution)/shard_map/pallas_call | solution.py:32
  149.0 4.3 %shard_map.43 = (f32[96,256]{1,0:T(8,128)S(1)}, f32[8,128]{1,0:T(8,128)S(1)}) custom-call(bf16[64,32,512]{2,1,0:T(8,128)(2,1)S(1)} %copy-done.2, bf16[64,32,512]{2,1,0:T(8,128)(2,1)} %get-tuple-element.30.refs_1_, bf16[64,32,512]{2,1,0:T(8,128)(2,1)} %get-tuple-element.31.refs_2_, ...), custom_call_target="tpu_custom_call", output_to_operand_aliasing={{1}: (4, {})} | custom-call | flops 1024 | bytes 1024 | tf_op jit(solution)/shard_map/pallas_call | solution.py:32
  153.4 11.4 %collective-permute-done.9.refs_0_.refs_3_ = bf16[64,32,512]{2,1,0:T(8,128)(2,1)} collective-permute-done((bf16[64,32,512]{2,1,0:T(8,128)(2,1)}, bf16[64,32,512]{2,1,0:T(8,128)(2,1)}, u32[]{:S(2)}, u32[]{:S(2)}) %collective-permute-start.9) | collective-permute-done | bytes 2097184 | tf_op jit(solution)/shard_map/ppermute | solution.py:254
  164.8 5.4 %collective-permute-done.10.refs_1_.refs_4_ = bf16[64,32,512]{2,1,0:T(8,128)(2,1)} collective-permute-done((bf16[64,32,512]{2,1,0:T(8,128)(2,1)}, bf16[64,32,512]{2,1,0:T(8,128)(2,1)}, u32[]{:S(2)}, u32[]{:S(2)}) %collective-permute-start.10) | collective-permute-done | bytes 2097184 | tf_op jit(solution)/shard_map/ppermute | solution.py:254
  170.2 1.9 %collective-permute-done.11.refs_2_.refs_5_ = bf16[64,32,512]{2,1,0:T(8,128)(2,1)} collective-permute-done((bf16[64,32,512]{2,1,0:T(8,128)(2,1)}, bf16[64,32,512]{2,1,0:T(8,128)(2,1)}, u32[]{:S(2)}, u32[]{:S(2)}) %collective-permute-start.11) | collective-permute-done | bytes 2097184 | tf_op jit(solution)/shard_map/ppermute | solution.py:254
  172.2 4.5 %shard_map.44 = (f32[96,256]{1,0:T(8,128)S(1)}, f32[8,128]{1,0:T(8,128)S(1)}) custom-call(bf16[64,32,512]{2,1,0:T(8,128)(2,1)} %collective-permute-done.9.refs_0_.refs_3_, bf16[64,32,512]{2,1,0:T(8,128)(2,1)} %collective-permute-done.10.refs_1_.refs_4_, ...), custom_call_target="tpu_custom_call", output_to_operand_aliasing={{1}: (4, {})} | custom-call | flops 1024 | bytes 1024 | tf_op jit(solution)/shard_map/pallas_call | solution.py:32
  176.7 0.0 copy-start.9
  176.7 0.6 copy-done.9
  177.3 0.7 copy-done.10
  178.0 4.6 %shard_map.45 = (f32[128,256]{1,0:T(8,128)S(1)}, f32[8,128]{1,0:T(8,128)S(1)}) custom-call(s32[4]{0:T(128)S(1)} %dynamic-slice_bitcast_fusion.refs_0_, f32[96,256]{1,0:T(8,128)S(1)} %add.7.refs_1_, f32[96,256]{1,0:T(8,128)S(1)} %get-tuple-element.40.refs_2_, ...), custom_call_target="tpu_custom_call", output_to_operand_aliasing={{1}: (7, {})} | custom-call | flops 1024 | bytes 1024 | tf_op jit(solution)/shard_map/pallas_call | solution.py:32
  182.5 9.0 %all_to_all.5 = f32[8,16,256]{2,1,0:T(8,128)S(1)} all-to-all(f32[8,16,256]{2,1,0:T(8,128)S(1)} %bitcast.20), channel_id=1, replica_groups=mesh['vir'=8,'out'=4] {'vir'}, dimensions={0} | all-to-all | bytes 262144 | tf_op jit(solution)/shard_map/all_to_all | solution.py:298
  191.6 0.6 copy.18
  (7 shorter events, 0.0 us)
Async XLA Ops:
  1.0 13.4 %collective-permute-start = (bf16[2,64,1536]{2,1,0:T(8,128)(2,1)S(1)}, bf16[2,64,1536]{2,1,0:T(8,128)(2,1)S(1)}, u32[]{:S(2)}, u32[]{:S(2)}) collective-permute-start(bf16[2,64,1536]{2,1,0:T(8,128)(2,1)S(1)} %slice.3), channel_id=1, source_target_pairs={{0,1},{4,5},{8,9},{12,13},{16,17},{20,21},{24,25},{28,29}} | collective-permute-start | bytes 1179656 | tf_op jit(solution)/shard_map/ppermute | solution.py:223
  1.7 21.6 %collective-permute-start.1 = (bf16[2,64,1536]{2,1,0:T(8,128)(2,1)S(1)}, bf16[2,64,1536]{2,1,0:T(8,128)(2,1)S(1)}, u32[]{:S(2)}, u32[]{:S(2)}) collective-permute-start(bf16[2,64,1536]{2,1,0:T(8,128)(2,1)S(1)} %slice.3), channel_id=1, source_target_pairs={{0,2},{4,6},{8,10},{12,14},{16,18},{20,22},{24,26},{28,30}} | collective-permute-start | bytes 1179656 | tf_op jit(solution)/shard_map/ppermute | solution.py:223
  3.0 20.3 %collective-permute-start.2 = (bf16[2,64,1536]{2,1,0:T(8,128)(2,1)S(1)}, bf16[2,64,1536]{2,1,0:T(8,128)(2,1)}, u32[]{:S(2)}, u32[]{:S(2)}) collective-permute-start(bf16[2,64,1536]{2,1,0:T(8,128)(2,1)S(1)} %slice.3), channel_id=1, source_target_pairs={{0,3},{4,7},{8,11},{12,15},{16,19},{20,23},{24,27},{28,31}} | collective-permute-start | bytes 1179656 | tf_op jit(solution)/shard_map/ppermute | solution.py:223
  7.2 43.7 %copy-start.1 = (bf16[32,64,512]{2,0,1:T(8,128)(2,1)}, bf16[32,64,512]{2,0,1:T(8,128)(2,1)S(1)}, u32[]{:S(2)}) copy-start(bf16[32,64,512]{2,0,1:T(8,128)(2,1)S(1)} %copy.20) | copy-start | bytes 6291460
  7.2 91.3 %collective-permute-start.7 = (bf16[64,32,512]{2,1,0:T(8,128)(2,1)S(1)}, bf16[64,32,512]{2,1,0:T(8,128)(2,1)}, u32[]{:S(2)}, u32[]{:S(2)}) collective-permute-start(bf16[64,32,512]{2,1,0:T(8,128)(2,1)S(1)} %bitcast.17), channel_id=1, source_target_pairs={{3,1},{2,0},{1,3},{0,2},{7,5},{6,4},{5,7},{4,6},{11,9},{10,8},{9,1... | collective-permute-start | bytes 6291464 | tf_op jit(solution)/shard_map/ppermute | solution.py:254
  11.8 86.7 %collective-permute-start.8 = (bf16[64,32,512]{2,1,0:T(8,128)(2,1)S(1)}, bf16[64,32,512]{2,1,0:T(8,128)(2,1)}, u32[]{:S(2)}, u32[]{:S(2)}) collective-permute-start(bf16[64,32,512]{2,1,0:T(8,128)(2,1)S(1)} %bitcast.18), channel_id=1, source_target_pairs={{1,0},{2,3},{5,4},{6,7},{9,8},{10,11},{13,12},{14,15},{17,16},{18,... | collective-permute-start | bytes 6291464 | tf_op jit(solution)/shard_map/ppermute | solution.py:254
  24.4 12.1 %collective-permute-start.3 = (bf16[2,64,1536]{2,1,0:T(8,128)(2,1)S(1)}, bf16[2,64,1536]{2,1,0:T(8,128)(2,1)S(1)}, u32[]{:S(2)}, u32[]{:S(2)}) collective-permute-start(bf16[2,64,1536]{2,1,0:T(8,128)(2,1)S(1)} %select_select_fusion.refs_0_), channel_id=1, source_target_pairs={{0,8},{4,12},{8,0},{12,4},{16,24},{20,28},{24,16},{28,20},{1,9},{5... | collective-permute-start | bytes 1179656 | tf_op jit(solution)/shard_map/ppermute | solution.py:233
  26.0 16.9 %collective-permute-start.4 = (bf16[2,64,1536]{2,1,0:T(8,128)(2,1)S(1)}, bf16[2,64,1536]{2,1,0:T(8,128)(2,1)S(1)}, u32[]{:S(2)}, u32[]{:S(2)}) collective-permute-start(bf16[2,64,1536]{2,1,0:T(8,128)(2,1)S(1)} %select_select_fusion.refs_0_), channel_id=1, source_target_pairs={{0,16},{4,20},{8,24},{12,28},{16,0},{20,4},{24,8},{28,12},{1,17},{... | collective-permute-start | bytes 1179656 | tf_op jit(solution)/shard_map/ppermute | solution.py:233
  27.5 15.4 %collective-permute-start.5 = (bf16[2,64,1536]{2,1,0:T(8,128)(2,1)S(1)}, bf16[2,64,1536]{2,1,0:T(8,128)(2,1)S(1)}, u32[]{:S(2)}, u32[]{:S(2)}) collective-permute-start(bf16[2,64,1536]{2,1,0:T(8,128)(2,1)S(1)} %select_select_fusion.refs_0_), channel_id=1, source_target_pairs={{0,24},{4,28},{8,16},{12,20},{16,8},{20,12},{24,0},{28,4},{1,25},{... | collective-permute-start | bytes 1179656 | tf_op jit(solution)/shard_map/ppermute | solution.py:233
  44.2 3.8 %collective-permute-start.6 = (bf16[4,2,64,1536]{3,2,1,0:T(8,128)(2,1)}, bf16[4,2,64,1536]{3,2,1,0:T(8,128)(2,1)}, u32[]{:S(2)}, u32[]{:S(2)}) collective-permute-start(bf16[4,2,64,1536]{3,2,1,0:T(8,128)(2,1)} %get-tuple-element.24.refs_1_), channel_id=1, source_target_pairs={{0,4},{4,0},{8,12},{12,8},{16,20},{20,16},{24,28},{28,24},{1,5},{5... | collective-permute-start | bytes 4718600 | tf_op jit(solution)/shard_map/ppermute | solution.py:233
  50.9 17.5 %copy-start.3 = (bf16[2,1536,512]{2,1,0:T(8,128)(2,1)}, bf16[2,1536,512]{2,1,0:T(8,128)(2,1)S(1)}, u32[]{:S(2)}) copy-start(bf16[2,1536,512]{2,1,0:T(8,128)(2,1)S(1)} %get-tuple-element.26.refs_1_) | copy-start | bytes 9437188
  68.5 3.3 %copy-start = (bf16[32,2,128,512]{3,2,1,0:T(8,128)(2,1)}, bf16[32,2,128,512]{3,2,1,0:T(8,128)(2,1)S(1)}, u32[]{:S(2)}) copy-start(bf16[32,2,128,512]{3,2,1,0:T(8,128)(2,1)S(1)} %get-tuple-element.32.refs_3_) | copy-start | bytes 25165828
  71.7 0.6 copy-start.5
  98.5 27.2 %copy-start.4 = (bf16[2,1536,512]{2,1,0:T(8,128)(2,1)S(1)}, bf16[2,1536,512]{2,1,0:T(8,128)(2,1)}, u32[]{:S(2)}) copy-start(bf16[2,1536,512]{2,1,0:T(8,128)(2,1)} %copy-done.3) | copy-start | bytes 9437188
  98.5 66.3 %collective-permute-start.9 = (bf16[64,32,512]{2,1,0:T(8,128)(2,1)}, bf16[64,32,512]{2,1,0:T(8,128)(2,1)}, u32[]{:S(2)}, u32[]{:S(2)}) collective-permute-start(bf16[64,32,512]{2,1,0:T(8,128)(2,1)} %get-tuple-element.30.refs_1_), channel_id=1, source_target_pairs={{1,0},{2,3},{5,4},{6,7},{9,8},{10,11},{13,12},{14,15},{17,16},{18,... | collective-permute-start | bytes 6291464 | tf_op jit(solution)/shard_map/ppermute | solution.py:254
  121.8 48.4 %collective-permute-start.10 = (bf16[64,32,512]{2,1,0:T(8,128)(2,1)}, bf16[64,32,512]{2,1,0:T(8,128)(2,1)}, u32[]{:S(2)}, u32[]{:S(2)}) collective-permute-start(bf16[64,32,512]{2,1,0:T(8,128)(2,1)} %get-tuple-element.29.refs_0_), channel_id=1, source_target_pairs={{2,1},{1,2},{6,5},{5,6},{10,9},{9,10},{14,13},{13,14},{18,17},{17,... | collective-permute-start | bytes 6291464 | tf_op jit(solution)/shard_map/ppermute | solution.py:254
  123.7 48.4 %collective-permute-start.11 = (bf16[64,32,512]{2,1,0:T(8,128)(2,1)}, bf16[64,32,512]{2,1,0:T(8,128)(2,1)}, u32[]{:S(2)}, u32[]{:S(2)}) collective-permute-start(bf16[64,32,512]{2,1,0:T(8,128)(2,1)} %get-tuple-element.29.refs_0_), channel_id=1, source_target_pairs={{3,2},{0,1},{7,6},{4,5},{11,10},{8,9},{15,14},{12,13},{19,18},{16,... | collective-permute-start | bytes 6291464 | tf_op jit(solution)/shard_map/ppermute | solution.py:254
  125.7 18.3 %slice-start = ((s8[8388608]{0:T(1024)(128)(4,1)}), s8[4194304]{0:T(1024)(128)(4,1)S(1)}, s32[]{:S(2)}) async-start(s8[8388608]{0:T(1024)(128)(4,1)} %bitcast.15), calls=%async_computation.1 | async-start | bytes 8388608
  125.7 0.8 copy-start.6
  126.6 17.4 %slice-start.1 = ((s8[8388608]{0:T(1024)(128)(4,1)}), s8[4194304]{0:T(1024)(128)(4,1)S(1)}, s32[]{:S(2)}) async-start(s8[8388608]{0:T(1024)(128)(4,1)} %bitcast.15), calls=%async_computation.2 | async-start | bytes 8388608
  126.6 17.4 %copy-start.2 = (bf16[64,32,512]{2,1,0:T(8,128)(2,1)S(1)}, bf16[64,32,512]{2,1,0:T(8,128)(2,1)}, u32[]{:S(2)}) copy-start(bf16[64,32,512]{2,1,0:T(8,128)(2,1)} %get-tuple-element.29.refs_0_) | copy-start | bytes 6291460
  143.4 0.6 copy-start.7
  144.0 0.7 copy-start.8
  176.7 0.6 copy-start.9
  177.3 0.7 copy-start.10
where the time goes:
time: 195 us; the launch traced here: 192 us
  waiting for transfers between devices  72.4 us (37%)
  Pallas kernels  56.3 us (29%)
  starting transfers between devices  40.7 us (21%)
  local copies, waits for them, and re-layouts  12.4 us (6%)
  blocking collectives  9.05 us (5%)
    pallas_call x8, Pallas kernels, call(): pl.pallas_call(run, grid=grid, in_specs=list(in_specs) + [anywhere] * n_t...  56.3 us
    ppermute x5, waiting for transfers between devices, send(): return lax.ppermute(array, 'out', ways)  44.9 us
    ppermute x5, starting transfers between devices, send(): return lax.ppermute(array, 'out', ways)  33.8 us
    ppermute x4, waiting for transfers between devices, swap(): return lax.ppermute(array, 'vir', [(k, k ^ mask) for k in range(vir)])  18.6 us
    unnamed x27, local copies, waits for them, and re-layouts  10 us
    all_to_all x1, blocking collectives, body(): swapped = lax.all_to_all(parts, 'vir', split_axis=0, concat_axis=0)  9.05 us
    ppermute x3, waiting for transfers between devices, spread(): heres = [lax.ppermute(rows, 'out', [(0, k)]) for k in range(n - 1, 0, -1)]  8.89 us
  transfers between devices with their start and end apart: 12, of which 8 were waited for; matrix products, arithmetic and copies ran while one was open for 2% of the time, Pallas kernels for 25%

commit v1 on v0

--- a/solution.py
+++ b/solution.py
@@ -12,6 +12,7 @@
 NT = (((1,), (1,)), ((), ()))
 NN = (((1,), (0,)), ((), ()))
 LITTLE = pl.CostEstimate(flops=1024, bytes_accessed=1024, transcendentals=0)
+MUCH = pl.CostEstimate(flops=2 * 10**10, bytes_accessed=4 * 10**7, transcendentals=0)
 
 
 def largest_part(extent, limit):
@@ -43,7 +44,7 @@
     return out[0], list(out[1:])
 
 
-def fence(arrays):
+def fence(arrays, cost=LITTLE):
     anywhere = [pl.BlockSpec(memory_space=pl.ANY)] * len(arrays)
     return pl.pallas_call(
         lambda *refs: None,
@@ -51,8 +52,32 @@
         out_specs=anywhere,
         out_shape=[jax.ShapeDtypeStruct(t.shape, t.dtype) for t in arrays],
         input_output_aliases={k: k for k in range(len(arrays))},
-        cost_estimate=LITTLE,
+        cost_estimate=cost,
     )(*arrays)
+
+
+def pick_kernel(flag_ref, first_ref, other_ref, out_ref):
+    @pl.when(flag_ref[0] == 1)
+    def _():
+        out_ref[...] = first_ref[...]
+
+    @pl.when(flag_ref[0] == 0)
+    def _():
+        out_ref[...] = other_ref[...]
+
+
+def pick(flag, first, other, through):
+    block = (largest_part(first.shape[0], 16),) + first.shape[1:]
+    spec = pl.BlockSpec(block, lambda i: (i, 0, 0))
+    return call(
+        pick_kernel,
+        [flag.astype(jnp.int32).reshape(1), first, other],
+        [pl.BlockSpec(memory_space=pltpu.SMEM), spec, spec],
+        jax.ShapeDtypeStruct(first.shape, first.dtype),
+        spec,
+        through,
+        grid=(first.shape[0] // block[0],),
+    )
 
 
 def pack_kernel(*refs):
@@ -167,9 +192,12 @@
         known = early_ref.shape[0]
         all_ref[:known] = early_ref[...]
         all_ref[known:] = added_ref[...] + total_ref[...].T
-        for j in range(out_ref.shape[0] // pairs):
-            start = pl.multiple_of(slot_ref[j] * pairs, pairs)
-            out_ref[j * pairs : (j + 1) * pairs] = all_ref[pl.ds(start, pairs), :]
+        owners, bb, rows, a_rows = out_ref.shape
+        each = pairs // rows
+        for j in range(owners):
+            start = pl.multiple_of(slot_ref[j // each] * pairs, pairs) + j % each * rows
+            for b in range(bb):
+                out_ref[j, b] = all_ref[pl.ds(start, rows), b * a_rows : (b + 1) * a_rows]
 
 
 def ladder_specs(taus, integral, start):
@@ -182,7 +210,7 @@
     return specs, (bb * a_rows, len(taus) * pairs), (c_rows // c_len,)
 
 
-def ladder_early(taus, integral, start, through):
+def ladder_early(taus, integral, start):
     specs, shape, grid = ladder_specs(taus, integral, start)
     return call(
         functools.partial(early_kernel, len(taus)),
@@ -190,17 +218,18 @@
         specs,
         jax.ShapeDtypeStruct(shape[::-1], jnp.float32),
         pl.BlockSpec(shape[::-1], lambda i: (0, 0)),
-        through,
+        [],
         grid=grid,
         scratch=[pltpu.VMEM(shape, jnp.float32)],
         vmem=16,
-    )
-
-
-def ladder_late(slots, early, added, taus, integral, start, through):
+    )[0]
+
+
+def ladder_late(slots, early, added, taus, integral, start, owners):
     specs, shape, grid = ladder_specs(taus, integral, start)
     pairs = taus[0].shape[1]
-    out = (slots.shape[0] * pairs, shape[0])
+    _, bb, a_rows, _ = integral.shape
+    out = (owners, bb, slots.shape[0] * pairs // owners, a_rows)
     return call(
         functools.partial(late_kernel, len(taus)),
         [slots, early, added] + taus + [integral],
@@ -208,15 +237,15 @@
         + [pl.BlockSpec(t.shape, lambda i: (0, 0)) for t in (early, added)]
         + specs,
         jax.ShapeDtypeStruct(out, jnp.float32),
-        pl.BlockSpec(out, lambda i: (0, 0)),
-        through,
+        pl.BlockSpec(out, lambda i: (0, 0, 0, 0)),
+        [],
         grid=grid,
         scratch=[
             pltpu.VMEM(shape, jnp.float32),
             pltpu.VMEM((early.shape[0] + shape[1], shape[0]), jnp.float32),
         ],
         vmem=16,
-    )
+    )[0]
 
 
 def spread(rows, n, z):
@@ -268,14 +297,15 @@
 
     make()
     if n == 4:
-        far = send(own, (3, 1), (2, 0), (1, 3), (0, 2))
-        near = send(own, (1, 0), (2, 3))
-        token, far, near, own = fence([token, far, near, own])
-        ends = send(far, (1, 0), (2, 3))
+        inside = (z == 1) | (z == 2)
+        first = send(own, (3, 1), (1, 0), (0, 2), (2, 3))
+        second = send(own, (2, 0), (1, 3))
+        onward, [token] = pick(inside, first, own, [token])
+        sides = send(onward, (1, 0), (0, 1), (2, 3), (3, 2))
+        token, second, own = fence([token, second, own], MUCH)
         middle = send(own, (2, 1), (1, 2))
-        inward = send(own, (3, 2), (0, 1))
-        early, late = [own, far, near], [ends, middle, inward]
-        slots = jnp.array([[0, 2, 1, 3], [5, 0, 4, 1], [1, 4, 0, 5], [3, 1, 2, 0]], jnp.int32)[z]
+        early, late = [own, first, second], [sides, middle]
+        slots = jnp.array([[0, 1, 2, 3], [3, 0, 4, 1], [1, 4, 0, 3], [3, 2, 1, 0]], jnp.int32)[z]
     else:
         gathered = lax.all_gather(own, "out")
         early, late = [own], [gathered[k] for k in range(n)]
@@ -283,21 +313,18 @@
     while len(made) < halves:
         make()
 
-    known, waiting = None, None
+    if n == 4:
+        late[0] = fence(late[:1], MUCH)[0]
+    known, added = None, jnp.zeros((sum(t.shape[1] for t in late), BB * a_rows), jnp.float32)
     for k, part in enumerate(made):
-        terms, [token] = ladder_early(early, part, k * half, [token])
+        terms = ladder_early(early, part, k * half)
         known = terms if known is None else known + terms
     for k, part in enumerate(made[:-1]):
-        terms, [token] = ladder_early(late, part, k * half, [token])
-        waiting = terms if waiting is None else waiting + terms
-    if waiting is None:
-        waiting = jnp.zeros((sum(t.shape[1] for t in late), BB * a_rows), jnp.float32)
-    total, _ = ladder_late(slots, known, waiting, late, made[-1], c_rows - half, [token])
-
-    parts = total.reshape(vir, -1, BB * a_rows)
+        terms = ladder_early(late, part, k * half)
+        added = terms if k == 0 else added + terms
+    parts = ladder_late(slots, known, added, late, made[-1], c_rows - half, vir)
     swapped = lax.all_to_all(parts, "vir", split_axis=0, concat_axis=0)
-    out = jnp.sum(swapped, axis=0)
-    return out.reshape(-1, BB, a_rows).transpose(1, 0, 2)
+    return jnp.sum(swapped, axis=0)
 
 
 def solution(mesh):

time: 195 us -> 186 us (0.954)
  starting transfers between devices: 40.7 us -> 27.6 us
  Pallas kernels: 56.3 us -> 60.7 us
  waiting for transfers between devices: 72.4 us -> 69.9 us
  local copies, waits for them, and re-layouts: 12.4 us -> 14.7 us
    ppermute x5 -> x4, starting transfers between devices: 33.8 us -> 20.6 us  [send(): return lax.ppermute(array, 'out', ways)]
    pallas_call x8 -> x9, Pallas kernels: 56.3 us -> 60.7 us  [call(): pl.pallas_call(run, grid=grid, in_specs=list(in_specs) + [anywhere] * n_t...]
    unnamed x27 -> x25, local copies, waits for them, and re-layouts: 10 us -> 12.9 us
    ppermute x5 -> x4, waiting for transfers between devices: 44.9 us -> 42.4 us  [send(): return lax.ppermute(array, 'out', ways)]
  transfers between devices with their start and end apart: 12 -> 11, of which waited for: 8 -> 9; matrix products, arithmetic and copies ran while one was open for 2% -> 3% of each run, Pallas kernels for 25% -> 28%
where the time goes in v1:
time: 186 us; the launch traced here: 184 us
  waiting for transfers between devices  69.9 us (38%)
  Pallas kernels  60.7 us (33%)
  starting transfers between devices  27.6 us (15%)
  local copies, waits for them, and re-layouts  14.7 us (8%)
  blocking collectives  9.05 us (5%)
    pallas_call x9, Pallas kernels, call(): pl.pallas_call(run, grid=grid, in_specs=list(in_specs) + [anywhere] * n_t...  60.7 us
    ppermute x4, waiting for transfers between devices, send(): return lax.ppermute(array, 'out', ways)  42.4 us
    ppermute x4, starting transfers between devices, send(): return lax.ppermute(array, 'out', ways)  20.6 us
    ppermute x4, waiting for transfers between devices, swap(): return lax.ppermute(array, 'vir', [(k, k ^ mask) for k in range(vir)])  18.4 us
    unnamed x25, local copies, waits for them, and re-layouts  12.9 us
    all_to_all x1, blocking collectives, body(): swapped = lax.all_to_all(parts, 'vir', split_axis=0, concat_axis=0)  9.05 us
    ppermute x3, waiting for transfers between devices, spread(): heres = [lax.ppermute(rows, 'out', [(0, k)]) for k in range(n - 1, 0, -1)]  9.04 us
  transfers between devices with their start and end apart: 11, of which 9 were waited for; matrix products, arithmetic and copies ran while one was open for 3% of the time, Pallas kernels for 28%

profile of v1, /device:TPU:16, one launch (start us, length us, event | category | flops | bytes accessed | tf_op | source)
XLA Modules:
  0.0 183.9 jit_solution(17591844339234249465)
XLA Ops:
  0.0 1.0 slice.3
  1.0 0.7 collective-permute-start.3
  1.7 1.3 collective-permute-start.2
  3.0 1.4 collective-permute-start.1
  4.4 2.8 %copy.15 = bf16[32,64,512]{2,0,1:T(8,128)(2,1)S(1)} copy(bf16[32,64,512]{2,1,0:T(8,128)(2,1)} %param.4) | data formatting | bytes 4194304 | tf_op args[1]
  7.2 0.0 copy-start.4
  7.2 9.1 %collective-permute-start.8 = (bf16[64,32,512]{2,1,0:T(8,128)(2,1)S(1)}, bf16[64,32,512]{2,1,0:T(8,128)(2,1)}, u32[]{:S(2)}, u32[]{:S(2)}) collective-permute-start(bf16[64,32,512]{2,1,0:T(8,128)(2,1)S(1)} %bitcast.16), channel_id=1, source_target_pairs={{2,0},{1,3},{6,4},{5,7},{10,8},{9,11},{14,12},{13,15},{18,16},{17,... | collective-permute-start | bytes 6291464 | tf_op jit(solution)/shard_map/ppermute | solution.py:283
  16.3 0.0 collective-permute-start
  16.3 0.0 collective-permute-done.3
  16.3 9.0 %collective-permute-done.2 = bf16[2,64,1536]{2,1,0:T(8,128)(2,1)S(1)} collective-permute-done((bf16[2,64,1536]{2,1,0:T(8,128)(2,1)S(1)}, bf16[2,64,1536]{2,1,0:T(8,128)(2,1)S(1)}, u32[]{:S(2)}, u32[]{:S(2)}) %collective-permute-start.2) | collective-permute-done | bytes 393248 | tf_op jit(solution)/shard_map/ppermute | solution.py:252
  25.3 0.0 collective-permute-done.1
  25.3 1.1 select_select_fusion.refs_0_
  26.4 2.5 %collective-permute-start.6 = (bf16[2,64,1536]{2,1,0:T(8,128)(2,1)S(1)}, bf16[2,64,1536]{2,1,0:T(8,128)(2,1)S(1)}, u32[]{:S(2)}, u32[]{:S(2)}) collective-permute-start(bf16[2,64,1536]{2,1,0:T(8,128)(2,1)S(1)} %select_select_fusion.refs_0_), channel_id=1, source_target_pairs={{0,24},{4,28},{8,16},{12,20},{16,8},{20,12},{24,0},{28,4},{1,25},{... | collective-permute-start | bytes 1179656 | tf_op jit(solution)/shard_map/ppermute | solution.py:262
  28.9 0.5 collective-permute-start.5
  29.4 0.5 collective-permute-start.4
  29.9 9.5 %collective-permute-done.6.refs_3_ = bf16[2,64,1536]{2,1,0:T(8,128)(2,1)S(1)} collective-permute-done((bf16[2,64,1536]{2,1,0:T(8,128)(2,1)S(1)}, bf16[2,64,1536]{2,1,0:T(8,128)(2,1)S(1)}, u32[]{:S(2)}, u32[]{:S(2)}) %collective-permute-start.6) | collective-permute-done | bytes 393248 | tf_op jit(solution)/shard_map/ppermute | solution.py:262
  39.4 5.2 %collective-permute-done.5.refs_2_ = bf16[2,64,1536]{2,1,0:T(8,128)(2,1)S(1)} collective-permute-done((bf16[2,64,1536]{2,1,0:T(8,128)(2,1)S(1)}, bf16[2,64,1536]{2,1,0:T(8,128)(2,1)S(1)}, u32[]{:S(2)}, u32[]{:S(2)}) %collective-permute-start.5) | collective-permute-done | bytes 393248 | tf_op jit(solution)/shard_map/ppermute | solution.py:262
  44.6 0.1 collective-permute-done.4.refs_1_
  44.7 1.3 shard_map.37
  46.0 0.0 collective-permute-start.7
  46.0 0.1 stack.35.refs_0_
  46.1 3.6 %collective-permute-done.7.refs_2_ = bf16[4,2,64,1536]{3,2,1,0:T(8,128)(2,1)} collective-permute-done((bf16[4,2,64,1536]{3,2,1,0:T(8,128)(2,1)}, bf16[4,2,64,1536]{3,2,1,0:T(8,128)(2,1)}, u32[]{:S(2)}, u32[]{:S(2)}) %collective-permute-start.7) | collective-permute-done | bytes 1572896 | tf_op jit(solution)/shard_map/ppermute | solution.py:262
  49.7 3.0 %shard_map.38 = (bf16[2,1536,512]{2,1,0:T(8,128)(2,1)S(1)}, f32[8,128]{1,0:T(8,128)S(1)}) custom-call(s32[8]{0:T(128)S(1)} %stack.35.refs_0_, bf16[4,2,64,1536]{3,2,1,0:T(8,128)(2,1)} %get-tuple-element.17.refs_1_, bf16[4,2,64,1536]{3,2,1,0:T(8,128)(2,1)} %collective-permute-done.7.refs_2_, ...), custom_call_target="tpu_custom_call", output_to_operand_aliasing={{1}: (3, {})} | custom-call | flops 1024 | bytes 1024 | tf_op jit(solution)/shard_map/pallas_call | solution.py:33
  52.7 0.0 copy-start.6
  52.7 17.5 %shard_map.39 = (bf16[32,2,128,512]{3,2,1,0:T(8,128)(2,1)S(1)}, f32[8,128]{1,0:T(8,128)S(1)}) custom-call(bf16[128,64,1536]{2,1,0:T(8,128)(2,1)} %refs_0_.3, bf16[2,1536,512]{2,1,0:T(8,128)(2,1)S(1)} %get-tuple-element.19.refs_1_, f32[8,128]{1,0:T(8,128)S(1)} %get-tuple-element.20.refs_2_), custom_call_target="tpu_custom_call", output_to_operand_aliasing={{1}: (2, {})} | custom-call | flops 1024 | bytes 1024 | tf_op jit(solution)/shard_map/pallas_call | solution.py:33
  70.2 0.0 copy-done.6
  70.3 0.0 copy-start
  70.3 3.3 %copy-done = bf16[32,2,128,512]{3,2,1,0:T(8,128)(2,1)} copy-done((bf16[32,2,128,512]{3,2,1,0:T(8,128)(2,1)}, bf16[32,2,128,512]{3,2,1,0:T(8,128)(2,1)S(1)}, u32[]{:S(2)}) %copy-start) | copy-done | bytes 8388632
  73.5 4.2 %collective-permute-done.refs_1_ = bf16[64,32,512]{2,1,0:T(8,128)(2,1)} collective-permute-done((bf16[64,32,512]{2,1,0:T(8,128)(2,1)S(1)}, bf16[64,32,512]{2,1,0:T(8,128)(2,1)}, u32[]{:S(2)}, u32[]{:S(2)}) %collective-permute-start) | collective-permute-done | bytes 2097184 | tf_op jit(solution)/shard_map/ppermute | solution.py:283
  77.7 0.0 copy-done.4
  77.7 3.9 %shard_map.40 = (bf16[64,32,512]{2,1,0:T(8,128)(2,1)}, f32[8,128]{1,0:T(8,128)S(1)}) custom-call(s32[1]{0:T(128)} %bitcast.1.refs_0_, bf16[64,32,512]{2,1,0:T(8,128)(2,1)} %collective-permute-done.refs_1_, bf16[64,32,512]{2,1,0:T(8,128)(2,1)S(1)} %bitcast.18, f32[8,128]{1,0:T(8,128)S(1)} %get-tuple-element.21.refs_3_), custom_call_target="tpu_custom_call", output_to_operand_aliasing={{1}: (3, {})} | custom-call | flops 1024 | bytes 1024 | tf_op jit(solution)/shard_map/pallas_call | solution.py:33
  81.6 0.0 copy-start.8
  81.6 0.6 copy-done.8
  82.2 0.0 collective-permute-start.9
  82.2 21.7 %collective-permute-done.8.refs_1_ = bf16[64,32,512]{2,1,0:T(8,128)(2,1)} collective-permute-done((bf16[64,32,512]{2,1,0:T(8,128)(2,1)S(1)}, bf16[64,32,512]{2,1,0:T(8,128)(2,1)}, u32[]{:S(2)}, u32[]{:S(2)}) %collective-permute-start.8) | collective-permute-done | bytes 2097184 | tf_op jit(solution)/shard_map/ppermute | solution.py:283
  104.0 11.6 %collective-permute-start.10 = (bf16[64,32,512]{2,1,0:T(8,128)(2,1)}, bf16[64,32,512]{2,1,0:T(8,128)(2,1)}, u32[]{:S(2)}, u32[]{:S(2)}) collective-permute-start(bf16[64,32,512]{2,1,0:T(8,128)(2,1)} %get-tuple-element.23.refs_0_), channel_id=1, source_target_pairs={{2,1},{1,2},{6,5},{5,6},{10,9},{9,10},{14,13},{13,14},{18,17},{17,... | collective-permute-start | bytes 6291464 | tf_op jit(solution)/shard_map/ppermute | solution.py:283
  115.5 0.7 dynamic-slice_bitcast_fusion.refs_0_
  116.2 0.0 slice-start
  116.2 0.0 copy-start.7
  116.2 2.0 %copy-done.7 = bf16[2,1536,512]{2,1,0:T(8,128)(2,1)S(1)} copy-done((bf16[2,1536,512]{2,1,0:T(8,128)(2,1)S(1)}, bf16[2,1536,512]{2,1,0:T(8,128)(2,1)}, u32[]{:S(2)}) %copy-start.7) | copy-done | bytes 3145752
  118.3 0.0 copy-start.9
  118.3 0.8 copy-done.9
  119.1 0.0 slice-start.1
  119.1 0.0 copy-start.5
  119.1 16.5 %shard_map.43 = (bf16[32,2,128,512]{3,2,1,0:T(8,128)(2,1)S(1)}, f32[8,128]{1,0:T(8,128)S(1)}) custom-call(bf16[128,64,1536]{2,1,0:T(8,128)(2,1)} %refs_0_.3, bf16[2,1536,512]{2,1,0:T(8,128)(2,1)S(1)} %copy-done.7, f32[8,128]{1,0:T(8,128)S(1)} %copy-done.9), custom_call_target="tpu_custom_call", output_to_operand_aliasing={{1}: (2, {})} | custom-call | flops 1024 | bytes 1024 | tf_op jit(solution)/shard_map/pallas_call | solution.py:33
  135.7 0.0 copy-start.2
  135.7 0.0 slice-done
  135.7 0.0 slice-done.1
  135.7 0.0 copy-done.5
  135.7 5.1 %shard_map.42 = f32[96,256]{1,0:T(8,128)S(1)} custom-call(bf16[64,32,512]{2,1,0:T(8,128)(2,1)S(1)} %copy-done.5, bf16[64,32,512]{2,1,0:T(8,128)(2,1)} %collective-permute-done.refs_1_, bf16[64,32,512]{2,1,0:T(8,128)(2,1)} %get-tuple-element.24.refs_2_, bf16[32,2,128,512]{3,2,1,0:T(8,128)(2,1)S(1)} %bitcast.15), custom_call_target="tpu_custom_call" | custom-call | flops 1024 | bytes 1024 | tf_op jit(solution)/shard_map/pallas_call | solution.py:33
  140.8 0.0 copy-done.2
  140.8 4.3 %shard_map.44 = f32[96,256]{1,0:T(8,128)S(1)} custom-call(bf16[64,32,512]{2,1,0:T(8,128)(2,1)S(1)} %copy-done.5, bf16[64,32,512]{2,1,0:T(8,128)(2,1)} %collective-permute-done.refs_1_, bf16[64,32,512]{2,1,0:T(8,128)(2,1)} %get-tuple-element.24.refs_2_, bf16[32,2,128,512]{3,2,1,0:T(8,128)(2,1)S(1)} %get-tuple-element.27.refs_3_.refs_5_), custom_call_target="tpu_custom_call" | custom-call | flops 1024 | bytes 1024 | tf_op jit(solution)/shard_map/pallas_call | solution.py:33
  145.2 12.9 %collective-permute-done.9.refs_0_ = bf16[64,32,512]{2,1,0:T(8,128)(2,1)} collective-permute-done((bf16[64,32,512]{2,1,0:T(8,128)(2,1)}, bf16[64,32,512]{2,1,0:T(8,128)(2,1)}, u32[]{:S(2)}, u32[]{:S(2)}) %collective-permute-start.9) | collective-permute-done | bytes 2097184 | tf_op jit(solution)/shard_map/ppermute | solution.py:283
  158.1 3.6 %collective-permute-done.10.refs_1_.refs_4_ = bf16[64,32,512]{2,1,0:T(8,128)(2,1)} collective-permute-done((bf16[64,32,512]{2,1,0:T(8,128)(2,1)}, bf16[64,32,512]{2,1,0:T(8,128)(2,1)}, u32[]{:S(2)}, u32[]{:S(2)}) %collective-permute-start.10) | collective-permute-done | bytes 2097184 | tf_op jit(solution)/shard_map/ppermute | solution.py:283
  161.7 0.0 copy-start.1
  161.7 3.4 %copy-done.1 = bf16[32,2,128,512]{3,2,1,0:T(8,128)(2,1)S(1)} copy-done((bf16[32,2,128,512]{3,2,1,0:T(8,128)(2,1)S(1)}, bf16[32,2,128,512]{3,2,1,0:T(8,128)(2,1)}, u32[]{:S(2)}) %copy-start.1) | copy-done | bytes 8388632
  165.0 0.0 copy-start.3
  165.0 4.8 %shard_map.46.refs_2_ = f32[64,256]{1,0:T(8,128)S(1)} custom-call(bf16[64,32,512]{2,1,0:T(8,128)(2,1)} %shard_map.45.refs_0_.refs_3_, bf16[64,32,512]{2,1,0:T(8,128)(2,1)} %collective-permute-done.10.refs_1_.refs_4_, bf16[32,2,128,512]{3,2,1,0:T(8,128)(2,1)S(1)} %copy-done.1), custom_call_target="tpu_custom_call" | custom-call | flops 1024 | bytes 1024 | tf_op jit(solution)/shard_map/pallas_call | solution.py:33
  169.9 0.0 copy-done.3
  169.9 4.3 %shard_map.47 = f32[8,2,16,128]{3,2,1,0:T(8,128)S(1)} custom-call(s32[4]{0:T(128)S(1)} %dynamic-slice_bitcast_fusion.refs_0_, f32[96,256]{1,0:T(8,128)S(1)} %add.7.refs_1_, f32[64,256]{1,0:T(8,128)S(1)} %shard_map.46.refs_2_, bf16[64,32,512]{2,1,0:T(8,128)(2,1)} %shard_map.45.refs_0_.refs_3_, bf16[64,32,512]{2,1,0:T(8,128)(2,1)} %collective-permute-done.10.refs_1_.refs_4_, ...), custom_call_target="tpu_custom_call" | custom-call | flops 1024 | bytes 1024 | tf_op jit(solution)/shard_map/pallas_call | solution.py:33
  174.2 9.0 %all_to_all.5 = f32[8,2,16,128]{3,2,1,0:T(8,128)S(1)} all-to-all(f32[8,2,16,128]{3,2,1,0:T(8,128)S(1)} %shard_map.47), channel_id=1, replica_groups=mesh['vir'=8,'out'=4] {'vir'}, dimensions={0} | all-to-all | bytes 262144 | tf_op jit(solution)/shard_map/all_to_all | solution.py:326
  183.3 0.6 reduce_sum.9
  (5 shorter events, 0.0 us)
Async XLA Ops:
  1.0 15.2 %collective-permute-start.3 = (bf16[2,64,1536]{2,1,0:T(8,128)(2,1)S(1)}, bf16[2,64,1536]{2,1,0:T(8,128)(2,1)S(1)}, u32[]{:S(2)}, u32[]{:S(2)}) collective-permute-start(bf16[2,64,1536]{2,1,0:T(8,128)(2,1)S(1)} %slice.3), channel_id=1, source_target_pairs={{0,3},{4,7},{8,11},{12,15},{16,19},{20,23},{24,27},{28,31}} | collective-permute-start | bytes 1179656 | tf_op jit(solution)/shard_map/ppermute | solution.py:252
  1.7 23.6 %collective-permute-start.2 = (bf16[2,64,1536]{2,1,0:T(8,128)(2,1)S(1)}, bf16[2,64,1536]{2,1,0:T(8,128)(2,1)S(1)}, u32[]{:S(2)}, u32[]{:S(2)}) collective-permute-start(bf16[2,64,1536]{2,1,0:T(8,128)(2,1)S(1)} %slice.3), channel_id=1, source_target_pairs={{0,2},{4,6},{8,10},{12,14},{16,18},{20,22},{24,26},{28,30}} | collective-permute-start | bytes 1179656 | tf_op jit(solution)/shard_map/ppermute | solution.py:252
  3.0 22.3 %collective-permute-start.1 = (bf16[2,64,1536]{2,1,0:T(8,128)(2,1)S(1)}, bf16[2,64,1536]{2,1,0:T(8,128)(2,1)}, u32[]{:S(2)}, u32[]{:S(2)}) collective-permute-start(bf16[2,64,1536]{2,1,0:T(8,128)(2,1)S(1)} %slice.3), channel_id=1, source_target_pairs={{0,1},{4,5},{8,9},{12,13},{16,17},{20,21},{24,25},{28,29}} | collective-permute-start | bytes 1179656 | tf_op jit(solution)/shard_map/ppermute | solution.py:252
  7.2 70.5 %copy-start.4 = (bf16[32,64,512]{2,0,1:T(8,128)(2,1)}, bf16[32,64,512]{2,0,1:T(8,128)(2,1)S(1)}, u32[]{:S(2)}) copy-start(bf16[32,64,512]{2,0,1:T(8,128)(2,1)S(1)} %copy.15) | copy-start | bytes 6291460
  7.2 96.8 %collective-permute-start.8 = (bf16[64,32,512]{2,1,0:T(8,128)(2,1)S(1)}, bf16[64,32,512]{2,1,0:T(8,128)(2,1)}, u32[]{:S(2)}, u32[]{:S(2)}) collective-permute-start(bf16[64,32,512]{2,1,0:T(8,128)(2,1)S(1)} %bitcast.16), channel_id=1, source_target_pairs={{2,0},{1,3},{6,4},{5,7},{10,8},{9,11},{14,12},{13,15},{18,16},{17,... | collective-permute-start | bytes 6291464 | tf_op jit(solution)/shard_map/ppermute | solution.py:283
  16.3 61.5 %collective-permute-start = (bf16[64,32,512]{2,1,0:T(8,128)(2,1)S(1)}, bf16[64,32,512]{2,1,0:T(8,128)(2,1)}, u32[]{:S(2)}, u32[]{:S(2)}) collective-permute-start(bf16[64,32,512]{2,1,0:T(8,128)(2,1)S(1)} %bitcast.17), channel_id=1, source_target_pairs={{3,1},{1,0},{0,2},{2,3},{7,5},{5,4},{4,6},{6,7},{11,9},{9,8},{8,10... | collective-permute-start | bytes 6291464 | tf_op jit(solution)/shard_map/ppermute | solution.py:283
  26.4 13.0 %collective-permute-start.6 = (bf16[2,64,1536]{2,1,0:T(8,128)(2,1)S(1)}, bf16[2,64,1536]{2,1,0:T(8,128)(2,1)S(1)}, u32[]{:S(2)}, u32[]{:S(2)}) collective-permute-start(bf16[2,64,1536]{2,1,0:T(8,128)(2,1)S(1)} %select_select_fusion.refs_0_), channel_id=1, source_target_pairs={{0,24},{4,28},{8,16},{12,20},{16,8},{20,12},{24,0},{28,4},{1,25},{... | collective-permute-start | bytes 1179656 | tf_op jit(solution)/shard_map/ppermute | solution.py:262
  28.9 15.7 %collective-permute-start.5 = (bf16[2,64,1536]{2,1,0:T(8,128)(2,1)S(1)}, bf16[2,64,1536]{2,1,0:T(8,128)(2,1)S(1)}, u32[]{:S(2)}, u32[]{:S(2)}) collective-permute-start(bf16[2,64,1536]{2,1,0:T(8,128)(2,1)S(1)} %select_select_fusion.refs_0_), channel_id=1, source_target_pairs={{0,16},{4,20},{8,24},{12,28},{16,0},{20,4},{24,8},{28,12},{1,17},{... | collective-permute-start | bytes 1179656 | tf_op jit(solution)/shard_map/ppermute | solution.py:262
  29.4 15.3 %collective-permute-start.4 = (bf16[2,64,1536]{2,1,0:T(8,128)(2,1)S(1)}, bf16[2,64,1536]{2,1,0:T(8,128)(2,1)S(1)}, u32[]{:S(2)}, u32[]{:S(2)}) collective-permute-start(bf16[2,64,1536]{2,1,0:T(8,128)(2,1)S(1)} %select_select_fusion.refs_0_), channel_id=1, source_target_pairs={{0,8},{4,12},{8,0},{12,4},{16,24},{20,28},{24,16},{28,20},{1,9},{5... | collective-permute-start | bytes 1179656 | tf_op jit(solution)/shard_map/ppermute | solution.py:262
  46.0 3.8 %collective-permute-start.7 = (bf16[4,2,64,1536]{3,2,1,0:T(8,128)(2,1)}, bf16[4,2,64,1536]{3,2,1,0:T(8,128)(2,1)}, u32[]{:S(2)}, u32[]{:S(2)}) collective-permute-start(bf16[4,2,64,1536]{3,2,1,0:T(8,128)(2,1)} %get-tuple-element.17.refs_1_), channel_id=1, source_target_pairs={{0,4},{4,0},{8,12},{12,8},{16,20},{20,16},{24,28},{28,24},{1,5},{5... | collective-permute-start | bytes 4718600 | tf_op jit(solution)/shard_map/ppermute | solution.py:262
  52.7 17.5 %copy-start.6 = (bf16[2,1536,512]{2,1,0:T(8,128)(2,1)}, bf16[2,1536,512]{2,1,0:T(8,128)(2,1)S(1)}, u32[]{:S(2)}) copy-start(bf16[2,1536,512]{2,1,0:T(8,128)(2,1)S(1)} %get-tuple-element.19.refs_1_) | copy-start | bytes 9437188
  70.3 3.3 %copy-start = (bf16[32,2,128,512]{3,2,1,0:T(8,128)(2,1)}, bf16[32,2,128,512]{3,2,1,0:T(8,128)(2,1)S(1)}, u32[]{:S(2)}) copy-start(bf16[32,2,128,512]{3,2,1,0:T(8,128)(2,1)S(1)} %get-tuple-element.25.refs_3_.refs_2_) | copy-start | bytes 25165828
  81.6 0.6 copy-start.8
  82.2 75.9 %collective-permute-start.9 = (bf16[64,32,512]{2,1,0:T(8,128)(2,1)}, bf16[64,32,512]{2,1,0:T(8,128)(2,1)}, u32[]{:S(2)}, u32[]{:S(2)}) collective-permute-start(bf16[64,32,512]{2,1,0:T(8,128)(2,1)} %get-tuple-element.28), channel_id=1, source_target_pairs={{1,0},{0,1},{2,3},{3,2},{5,4},{4,5},{6,7},{7,6},{9,8},{8,9},{10,11... | collective-permute-start | bytes 6291464 | tf_op jit(solution)/shard_map/ppermute | solution.py:283
  104.0 57.7 %collective-permute-start.10 = (bf16[64,32,512]{2,1,0:T(8,128)(2,1)}, bf16[64,32,512]{2,1,0:T(8,128)(2,1)}, u32[]{:S(2)}, u32[]{:S(2)}) collective-permute-start(bf16[64,32,512]{2,1,0:T(8,128)(2,1)} %get-tuple-element.23.refs_0_), channel_id=1, source_target_pairs={{2,1},{1,2},{6,5},{5,6},{10,9},{9,10},{14,13},{13,14},{18,17},{17,... | collective-permute-start | bytes 6291464 | tf_op jit(solution)/shard_map/ppermute | solution.py:283
  116.2 19.4 %slice-start = ((s8[8388608]{0:T(1024)(128)(4,1)}), s8[4194304]{0:T(1024)(128)(4,1)S(1)}, s32[]{:S(2)}) async-start(s8[8388608]{0:T(1024)(128)(4,1)} %bitcast.14), calls=%async_computation.1 | async-start | bytes 8388608
  116.2 2.0 %copy-start.7 = (bf16[2,1536,512]{2,1,0:T(8,128)(2,1)S(1)}, bf16[2,1536,512]{2,1,0:T(8,128)(2,1)}, u32[]{:S(2)}) copy-start(bf16[2,1536,512]{2,1,0:T(8,128)(2,1)} %copy-done.6) | copy-start | bytes 9437188
  118.3 0.9 copy-start.9
  119.1 16.6 %slice-start.1 = ((s8[8388608]{0:T(1024)(128)(4,1)}), s8[4194304]{0:T(1024)(128)(4,1)S(1)}, s32[]{:S(2)}) async-start(s8[8388608]{0:T(1024)(128)(4,1)} %bitcast.14), calls=%async_computation.2 | async-start | bytes 8388608
  119.1 16.6 %copy-start.5 = (bf16[64,32,512]{2,1,0:T(8,128)(2,1)S(1)}, bf16[64,32,512]{2,1,0:T(8,128)(2,1)}, u32[]{:S(2)}) copy-start(bf16[64,32,512]{2,1,0:T(8,128)(2,1)} %get-tuple-element.23.refs_0_) | copy-start | bytes 6291460
  135.7 5.2 %copy-start.2 = (bf16[32,2,128,512]{3,2,1,0:T(8,128)(2,1)}, bf16[32,2,128,512]{3,2,1,0:T(8,128)(2,1)S(1)}, u32[]{:S(2)}) copy-start(bf16[32,2,128,512]{3,2,1,0:T(8,128)(2,1)S(1)} %get-tuple-element.27.refs_3_.refs_5_) | copy-start | bytes 25165828
  161.7 3.4 %copy-start.1 = (bf16[32,2,128,512]{3,2,1,0:T(8,128)(2,1)S(1)}, bf16[32,2,128,512]{3,2,1,0:T(8,128)(2,1)}, u32[]{:S(2)}) copy-start(bf16[32,2,128,512]{3,2,1,0:T(8,128)(2,1)} %copy-done) | copy-start | bytes 25165828
  165.0 4.8 %copy-start.3 = (bf16[32,2,128,512]{3,2,1,0:T(8,128)(2,1)S(1)}, bf16[32,2,128,512]{3,2,1,0:T(8,128)(2,1)}, u32[]{:S(2)}) copy-start(bf16[32,2,128,512]{3,2,1,0:T(8,128)(2,1)} %copy-done.2) | copy-start | bytes 25165828

commit v2 on v1

--- a/solution.py
+++ b/solution.py
@@ -22,7 +22,7 @@
     return part
 
 
-def call(kernel, inputs, in_specs, out_shape, out_spec, through, grid=(1,), scratch=(), vmem=28):
+def call(kernel, inputs, in_specs, out_shape, out_spec, through, grid=(1,), scratch=(), vmem=20):
     n_in, n_thru = len(inputs), len(through)
 
     def run(*refs):
@@ -157,11 +157,14 @@
     def _():
         total_ref[...] = jnp.zeros_like(total_ref)
 
-    total = total_ref[...]
-    for c in range(c_len):
-        left = integral_ref[c].reshape(bb * a_rows, d_len)
-        total += lax.dot_general(left, tau_of(c), NT, preferred_element_type=jnp.float32)
-    total_ref[...] = total
+    left = [integral_ref[c].reshape(bb * a_rows, d_len) for c in range(c_len)]
+    right = [tau_of(c) for c in range(c_len)]
+    total_ref[...] += lax.dot_general(
+        jnp.concatenate(left, axis=1),
+        jnp.concatenate(right, axis=1),
+        NT,
+        preferred_element_type=jnp.float32,
+    )
 
 
 def early_kernel(count, *refs):
@@ -221,7 +224,7 @@
         [],
         grid=grid,
         scratch=[pltpu.VMEM(shape, jnp.float32)],
-        vmem=16,
+        vmem=10,
     )[0]
 
 
@@ -244,7 +247,7 @@
             pltpu.VMEM(shape, jnp.float32),
             pltpu.VMEM((early.shape[0] + shape[1], shape[0]), jnp.float32),
         ],
-        vmem=16,
+        vmem=10,
     )[0]
 
 

time: 186 us -> 186 us (level)
  no operation moved by 1% of the time
where the time goes in v2:
time: 186 us; the launch traced here: 184 us
  waiting for transfers between devices  69.8 us (38%)
  Pallas kernels  60.8 us (33%)
  starting transfers between devices  27.6 us (15%)
  local copies, waits for them, and re-layouts  14.7 us (8%)
  blocking collectives  9.05 us (5%)
    pallas_call x9, Pallas kernels, call(): pl.pallas_call(run, grid=grid, in_specs=list(in_specs) + [anywhere] * n_t...  60.8 us
    ppermute x4, waiting for transfers between devices, send(): return lax.ppermute(array, 'out', ways)  42.4 us
    ppermute x4, starting transfers between devices, send(): return lax.ppermute(array, 'out', ways)  20.6 us
    ppermute x4, waiting for transfers between devices, swap(): return lax.ppermute(array, 'vir', [(k, k ^ mask) for k in range(vir)])  18.4 us
    unnamed x25, local copies, waits for them, and re-layouts  12.9 us
    all_to_all x1, blocking collectives, body(): swapped = lax.all_to_all(parts, 'vir', split_axis=0, concat_axis=0)  9.05 us
    ppermute x3, waiting for transfers between devices, spread(): heres = [lax.ppermute(rows, 'out', [(0, k)]) for k in range(n - 1, 0, -1)]  9.04 us
  transfers between devices with their start and end apart: 11, of which 9 were waited for; matrix products, arithmetic and copies ran while one was open for 3% of the time, Pallas kernels for 28%

profile of v2, /device:TPU:16, one launch (start us, length us, event | category | flops | bytes accessed | tf_op | source)
XLA Modules:
  0.0 183.9 jit_solution(5554774162185285146)
XLA Ops:
  0.0 1.0 slice.3
  1.0 0.7 collective-permute-start.3
  1.7 1.3 collective-permute-start.2
  3.0 1.4 collective-permute-start.1
  4.4 2.8 %copy.15 = bf16[32,64,512]{2,0,1:T(8,128)(2,1)S(1)} copy(bf16[32,64,512]{2,1,0:T(8,128)(2,1)} %param.4) | data formatting | bytes 4194304 | tf_op args[1]
  7.2 0.0 copy-start.4
  7.2 9.1 %collective-permute-start.8 = (bf16[64,32,512]{2,1,0:T(8,128)(2,1)S(1)}, bf16[64,32,512]{2,1,0:T(8,128)(2,1)}, u32[]{:S(2)}, u32[]{:S(2)}) collective-permute-start(bf16[64,32,512]{2,1,0:T(8,128)(2,1)S(1)} %bitcast.16), channel_id=1, source_target_pairs={{2,0},{1,3},{6,4},{5,7},{10,8},{9,11},{14,12},{13,15},{18,16},{17,... | collective-permute-start | bytes 6291464 | tf_op jit(solution)/shard_map/ppermute | solution.py:286
  16.3 0.0 collective-permute-start
  16.3 0.0 collective-permute-done.3
  16.3 9.0 %collective-permute-done.2 = bf16[2,64,1536]{2,1,0:T(8,128)(2,1)S(1)} collective-permute-done((bf16[2,64,1536]{2,1,0:T(8,128)(2,1)S(1)}, bf16[2,64,1536]{2,1,0:T(8,128)(2,1)S(1)}, u32[]{:S(2)}, u32[]{:S(2)}) %collective-permute-start.2) | collective-permute-done | bytes 393248 | tf_op jit(solution)/shard_map/ppermute | solution.py:255
  25.3 0.0 collective-permute-done.1
  25.3 1.1 select_select_fusion.refs_0_
  26.4 2.5 %collective-permute-start.6 = (bf16[2,64,1536]{2,1,0:T(8,128)(2,1)S(1)}, bf16[2,64,1536]{2,1,0:T(8,128)(2,1)S(1)}, u32[]{:S(2)}, u32[]{:S(2)}) collective-permute-start(bf16[2,64,1536]{2,1,0:T(8,128)(2,1)S(1)} %select_select_fusion.refs_0_), channel_id=1, source_target_pairs={{0,24},{4,28},{8,16},{12,20},{16,8},{20,12},{24,0},{28,4},{1,25},{... | collective-permute-start | bytes 1179656 | tf_op jit(solution)/shard_map/ppermute | solution.py:265
  28.9 0.5 collective-permute-start.5
  29.4 0.5 collective-permute-start.4
  29.9 9.5 %collective-permute-done.6.refs_3_ = bf16[2,64,1536]{2,1,0:T(8,128)(2,1)S(1)} collective-permute-done((bf16[2,64,1536]{2,1,0:T(8,128)(2,1)S(1)}, bf16[2,64,1536]{2,1,0:T(8,128)(2,1)S(1)}, u32[]{:S(2)}, u32[]{:S(2)}) %collective-permute-start.6) | collective-permute-done | bytes 393248 | tf_op jit(solution)/shard_map/ppermute | solution.py:265
  39.4 5.2 %collective-permute-done.5.refs_2_ = bf16[2,64,1536]{2,1,0:T(8,128)(2,1)S(1)} collective-permute-done((bf16[2,64,1536]{2,1,0:T(8,128)(2,1)S(1)}, bf16[2,64,1536]{2,1,0:T(8,128)(2,1)S(1)}, u32[]{:S(2)}, u32[]{:S(2)}) %collective-permute-start.5) | collective-permute-done | bytes 393248 | tf_op jit(solution)/shard_map/ppermute | solution.py:265
  44.6 0.1 collective-permute-done.4.refs_1_
  44.7 1.3 shard_map.37
  46.0 0.0 collective-permute-start.7
  46.0 0.1 stack.35.refs_0_
  46.1 3.6 %collective-permute-done.7.refs_2_ = bf16[4,2,64,1536]{3,2,1,0:T(8,128)(2,1)} collective-permute-done((bf16[4,2,64,1536]{3,2,1,0:T(8,128)(2,1)}, bf16[4,2,64,1536]{3,2,1,0:T(8,128)(2,1)}, u32[]{:S(2)}, u32[]{:S(2)}) %collective-permute-start.7) | collective-permute-done | bytes 1572896 | tf_op jit(solution)/shard_map/ppermute | solution.py:265
  49.7 3.0 %shard_map.38 = (bf16[2,1536,512]{2,1,0:T(8,128)(2,1)S(1)}, f32[8,128]{1,0:T(8,128)S(1)}) custom-call(s32[8]{0:T(128)S(1)} %stack.35.refs_0_, bf16[4,2,64,1536]{3,2,1,0:T(8,128)(2,1)} %get-tuple-element.17.refs_1_, bf16[4,2,64,1536]{3,2,1,0:T(8,128)(2,1)} %collective-permute-done.7.refs_2_, ...), custom_call_target="tpu_custom_call", output_to_operand_aliasing={{1}: (3, {})} | custom-call | flops 1024 | bytes 1024 | tf_op jit(solution)/shard_map/pallas_call | solution.py:33
  52.7 0.0 copy-start.6
  52.7 17.5 %shard_map.39 = (bf16[32,2,128,512]{3,2,1,0:T(8,128)(2,1)S(1)}, f32[8,128]{1,0:T(8,128)S(1)}) custom-call(bf16[128,64,1536]{2,1,0:T(8,128)(2,1)} %refs_0_.3, bf16[2,1536,512]{2,1,0:T(8,128)(2,1)S(1)} %get-tuple-element.19.refs_1_, f32[8,128]{1,0:T(8,128)S(1)} %get-tuple-element.20.refs_2_), custom_call_target="tpu_custom_call", output_to_operand_aliasing={{1}: (2, {})} | custom-call | flops 1024 | bytes 1024 | tf_op jit(solution)/shard_map/pallas_call | solution.py:33
  70.2 0.0 copy-done.6
  70.3 0.0 copy-start
  70.3 3.3 %copy-done = bf16[32,2,128,512]{3,2,1,0:T(8,128)(2,1)} copy-done((bf16[32,2,128,512]{3,2,1,0:T(8,128)(2,1)}, bf16[32,2,128,512]{3,2,1,0:T(8,128)(2,1)S(1)}, u32[]{:S(2)}) %copy-start) | copy-done | bytes 8388632
  73.5 4.2 %collective-permute-done.refs_1_ = bf16[64,32,512]{2,1,0:T(8,128)(2,1)} collective-permute-done((bf16[64,32,512]{2,1,0:T(8,128)(2,1)S(1)}, bf16[64,32,512]{2,1,0:T(8,128)(2,1)}, u32[]{:S(2)}, u32[]{:S(2)}) %collective-permute-start) | collective-permute-done | bytes 2097184 | tf_op jit(solution)/shard_map/ppermute | solution.py:286
  77.7 0.0 copy-done.4
  77.7 3.9 %shard_map.40 = (bf16[64,32,512]{2,1,0:T(8,128)(2,1)}, f32[8,128]{1,0:T(8,128)S(1)}) custom-call(s32[1]{0:T(128)} %bitcast.1.refs_0_, bf16[64,32,512]{2,1,0:T(8,128)(2,1)} %collective-permute-done.refs_1_, bf16[64,32,512]{2,1,0:T(8,128)(2,1)S(1)} %bitcast.18, f32[8,128]{1,0:T(8,128)S(1)} %get-tuple-element.21.refs_3_), custom_call_target="tpu_custom_call", output_to_operand_aliasing={{1}: (3, {})} | custom-call | flops 1024 | bytes 1024 | tf_op jit(solution)/shard_map/pallas_call | solution.py:33
  81.6 0.0 copy-start.8
  81.6 0.6 copy-done.8
  82.2 0.0 collective-permute-start.9
  82.2 21.7 %collective-permute-done.8.refs_1_ = bf16[64,32,512]{2,1,0:T(8,128)(2,1)} collective-permute-done((bf16[64,32,512]{2,1,0:T(8,128)(2,1)S(1)}, bf16[64,32,512]{2,1,0:T(8,128)(2,1)}, u32[]{:S(2)}, u32[]{:S(2)}) %collective-permute-start.8) | collective-permute-done | bytes 2097184 | tf_op jit(solution)/shard_map/ppermute | solution.py:286
  104.0 11.6 %collective-permute-start.10 = (bf16[64,32,512]{2,1,0:T(8,128)(2,1)}, bf16[64,32,512]{2,1,0:T(8,128)(2,1)}, u32[]{:S(2)}, u32[]{:S(2)}) collective-permute-start(bf16[64,32,512]{2,1,0:T(8,128)(2,1)} %get-tuple-element.23.refs_0_), channel_id=1, source_target_pairs={{2,1},{1,2},{6,5},{5,6},{10,9},{9,10},{14,13},{13,14},{18,17},{17,... | collective-permute-start | bytes 6291464 | tf_op jit(solution)/shard_map/ppermute | solution.py:286
  115.5 0.7 dynamic-slice_bitcast_fusion.refs_0_
  116.2 0.0 slice-start
  116.2 0.0 copy-start.7
  116.2 2.0 %copy-done.7 = bf16[2,1536,512]{2,1,0:T(8,128)(2,1)S(1)} copy-done((bf16[2,1536,512]{2,1,0:T(8,128)(2,1)S(1)}, bf16[2,1536,512]{2,1,0:T(8,128)(2,1)}, u32[]{:S(2)}) %copy-start.7) | copy-done | bytes 3145752
  118.3 0.0 copy-start.9
  118.3 0.8 copy-done.9
  119.1 0.0 slice-start.1
  119.1 0.0 copy-start.5
  119.1 16.5 %shard_map.43 = (bf16[32,2,128,512]{3,2,1,0:T(8,128)(2,1)S(1)}, f32[8,128]{1,0:T(8,128)S(1)}) custom-call(bf16[128,64,1536]{2,1,0:T(8,128)(2,1)} %refs_0_.3, bf16[2,1536,512]{2,1,0:T(8,128)(2,1)S(1)} %copy-done.7, f32[8,128]{1,0:T(8,128)S(1)} %copy-done.9), custom_call_target="tpu_custom_call", output_to_operand_aliasing={{1}: (2, {})} | custom-call | flops 1024 | bytes 1024 | tf_op jit(solution)/shard_map/pallas_call | solution.py:33
  135.7 0.0 copy-start.2
  135.7 0.0 slice-done
  135.7 0.0 slice-done.1
  135.7 0.0 copy-done.5
  135.7 5.1 %shard_map.42 = f32[96,256]{1,0:T(8,128)S(1)} custom-call(bf16[64,32,512]{2,1,0:T(8,128)(2,1)S(1)} %copy-done.5, bf16[64,32,512]{2,1,0:T(8,128)(2,1)} %collective-permute-done.refs_1_, bf16[64,32,512]{2,1,0:T(8,128)(2,1)} %get-tuple-element.24.refs_2_, bf16[32,2,128,512]{3,2,1,0:T(8,128)(2,1)S(1)} %bitcast.15), custom_call_target="tpu_custom_call" | custom-call | flops 1024 | bytes 1024 | tf_op jit(solution)/shard_map/pallas_call | solution.py:33
  140.8 0.0 copy-done.2
  140.8 4.3 %shard_map.44 = f32[96,256]{1,0:T(8,128)S(1)} custom-call(bf16[64,32,512]{2,1,0:T(8,128)(2,1)S(1)} %copy-done.5, bf16[64,32,512]{2,1,0:T(8,128)(2,1)} %collective-permute-done.refs_1_, bf16[64,32,512]{2,1,0:T(8,128)(2,1)} %get-tuple-element.24.refs_2_, bf16[32,2,128,512]{3,2,1,0:T(8,128)(2,1)S(1)} %get-tuple-element.27.refs_3_.refs_5_), custom_call_target="tpu_custom_call" | custom-call | flops 1024 | bytes 1024 | tf_op jit(solution)/shard_map/pallas_call | solution.py:33
  145.2 12.8 %collective-permute-done.9.refs_0_ = bf16[64,32,512]{2,1,0:T(8,128)(2,1)} collective-permute-done((bf16[64,32,512]{2,1,0:T(8,128)(2,1)}, bf16[64,32,512]{2,1,0:T(8,128)(2,1)}, u32[]{:S(2)}, u32[]{:S(2)}) %collective-permute-start.9) | collective-permute-done | bytes 2097184 | tf_op jit(solution)/shard_map/ppermute | solution.py:286
  158.1 3.6 %collective-permute-done.10.refs_1_.refs_4_ = bf16[64,32,512]{2,1,0:T(8,128)(2,1)} collective-permute-done((bf16[64,32,512]{2,1,0:T(8,128)(2,1)}, bf16[64,32,512]{2,1,0:T(8,128)(2,1)}, u32[]{:S(2)}, u32[]{:S(2)}) %collective-permute-start.10) | collective-permute-done | bytes 2097184 | tf_op jit(solution)/shard_map/ppermute | solution.py:286
  161.7 0.0 copy-start.1
  161.7 3.4 %copy-done.1 = bf16[32,2,128,512]{3,2,1,0:T(8,128)(2,1)S(1)} copy-done((bf16[32,2,128,512]{3,2,1,0:T(8,128)(2,1)S(1)}, bf16[32,2,128,512]{3,2,1,0:T(8,128)(2,1)}, u32[]{:S(2)}) %copy-start.1) | copy-done | bytes 8388632
  165.0 0.0 copy-start.3
  165.0 4.8 %shard_map.46.refs_2_ = f32[64,256]{1,0:T(8,128)S(1)} custom-call(bf16[64,32,512]{2,1,0:T(8,128)(2,1)} %shard_map.45.refs_0_.refs_3_, bf16[64,32,512]{2,1,0:T(8,128)(2,1)} %collective-permute-done.10.refs_1_.refs_4_, bf16[32,2,128,512]{3,2,1,0:T(8,128)(2,1)S(1)} %copy-done.1), custom_call_target="tpu_custom_call" | custom-call | flops 1024 | bytes 1024 | tf_op jit(solution)/shard_map/pallas_call | solution.py:33
  169.9 0.0 copy-done.3
  169.9 4.4 %shard_map.47 = f32[8,2,16,128]{3,2,1,0:T(8,128)S(1)} custom-call(s32[4]{0:T(128)S(1)} %dynamic-slice_bitcast_fusion.refs_0_, f32[96,256]{1,0:T(8,128)S(1)} %add.7.refs_1_, f32[64,256]{1,0:T(8,128)S(1)} %shard_map.46.refs_2_, bf16[64,32,512]{2,1,0:T(8,128)(2,1)} %shard_map.45.refs_0_.refs_3_, bf16[64,32,512]{2,1,0:T(8,128)(2,1)} %collective-permute-done.10.refs_1_.refs_4_, ...), custom_call_target="tpu_custom_call" | custom-call | flops 1024 | bytes 1024 | tf_op jit(solution)/shard_map/pallas_call | solution.py:33
  174.3 9.1 %all_to_all.5 = f32[8,2,16,128]{3,2,1,0:T(8,128)S(1)} all-to-all(f32[8,2,16,128]{3,2,1,0:T(8,128)S(1)} %shard_map.47), channel_id=1, replica_groups=mesh['vir'=8,'out'=4] {'vir'}, dimensions={0} | all-to-all | bytes 262144 | tf_op jit(solution)/shard_map/all_to_all | solution.py:329
  183.3 0.6 reduce_sum.9
  (5 shorter events, 0.0 us)
Async XLA Ops:
  1.0 15.2 %collective-permute-start.3 = (bf16[2,64,1536]{2,1,0:T(8,128)(2,1)S(1)}, bf16[2,64,1536]{2,1,0:T(8,128)(2,1)S(1)}, u32[]{:S(2)}, u32[]{:S(2)}) collective-permute-start(bf16[2,64,1536]{2,1,0:T(8,128)(2,1)S(1)} %slice.3), channel_id=1, source_target_pairs={{0,3},{4,7},{8,11},{12,15},{16,19},{20,23},{24,27},{28,31}} | collective-permute-start | bytes 1179656 | tf_op jit(solution)/shard_map/ppermute | solution.py:255
  1.7 23.6 %collective-permute-start.2 = (bf16[2,64,1536]{2,1,0:T(8,128)(2,1)S(1)}, bf16[2,64,1536]{2,1,0:T(8,128)(2,1)S(1)}, u32[]{:S(2)}, u32[]{:S(2)}) collective-permute-start(bf16[2,64,1536]{2,1,0:T(8,128)(2,1)S(1)} %slice.3), channel_id=1, source_target_pairs={{0,2},{4,6},{8,10},{12,14},{16,18},{20,22},{24,26},{28,30}} | collective-permute-start | bytes 1179656 | tf_op jit(solution)/shard_map/ppermute | solution.py:255
  3.0 22.3 %collective-permute-start.1 = (bf16[2,64,1536]{2,1,0:T(8,128)(2,1)S(1)}, bf16[2,64,1536]{2,1,0:T(8,128)(2,1)}, u32[]{:S(2)}, u32[]{:S(2)}) collective-permute-start(bf16[2,64,1536]{2,1,0:T(8,128)(2,1)S(1)} %slice.3), channel_id=1, source_target_pairs={{0,1},{4,5},{8,9},{12,13},{16,17},{20,21},{24,25},{28,29}} | collective-permute-start | bytes 1179656 | tf_op jit(solution)/shard_map/ppermute | solution.py:255
  7.2 70.5 %copy-start.4 = (bf16[32,64,512]{2,0,1:T(8,128)(2,1)}, bf16[32,64,512]{2,0,1:T(8,128)(2,1)S(1)}, u32[]{:S(2)}) copy-start(bf16[32,64,512]{2,0,1:T(8,128)(2,1)S(1)} %copy.15) | copy-start | bytes 6291460
  7.2 96.8 %collective-permute-start.8 = (bf16[64,32,512]{2,1,0:T(8,128)(2,1)S(1)}, bf16[64,32,512]{2,1,0:T(8,128)(2,1)}, u32[]{:S(2)}, u32[]{:S(2)}) collective-permute-start(bf16[64,32,512]{2,1,0:T(8,128)(2,1)S(1)} %bitcast.16), channel_id=1, source_target_pairs={{2,0},{1,3},{6,4},{5,7},{10,8},{9,11},{14,12},{13,15},{18,16},{17,... | collective-permute-start | bytes 6291464 | tf_op jit(solution)/shard_map/ppermute | solution.py:286
  16.3 61.5 %collective-permute-start = (bf16[64,32,512]{2,1,0:T(8,128)(2,1)S(1)}, bf16[64,32,512]{2,1,0:T(8,128)(2,1)}, u32[]{:S(2)}, u32[]{:S(2)}) collective-permute-start(bf16[64,32,512]{2,1,0:T(8,128)(2,1)S(1)} %bitcast.17), channel_id=1, source_target_pairs={{3,1},{1,0},{0,2},{2,3},{7,5},{5,4},{4,6},{6,7},{11,9},{9,8},{8,10... | collective-permute-start | bytes 6291464 | tf_op jit(solution)/shard_map/ppermute | solution.py:286
  26.4 13.0 %collective-permute-start.6 = (bf16[2,64,1536]{2,1,0:T(8,128)(2,1)S(1)}, bf16[2,64,1536]{2,1,0:T(8,128)(2,1)S(1)}, u32[]{:S(2)}, u32[]{:S(2)}) collective-permute-start(bf16[2,64,1536]{2,1,0:T(8,128)(2,1)S(1)} %select_select_fusion.refs_0_), channel_id=1, source_target_pairs={{0,24},{4,28},{8,16},{12,20},{16,8},{20,12},{24,0},{28,4},{1,25},{... | collective-permute-start | bytes 1179656 | tf_op jit(solution)/shard_map/ppermute | solution.py:265
  28.9 15.7 %collective-permute-start.5 = (bf16[2,64,1536]{2,1,0:T(8,128)(2,1)S(1)}, bf16[2,64,1536]{2,1,0:T(8,128)(2,1)S(1)}, u32[]{:S(2)}, u32[]{:S(2)}) collective-permute-start(bf16[2,64,1536]{2,1,0:T(8,128)(2,1)S(1)} %select_select_fusion.refs_0_), channel_id=1, source_target_pairs={{0,16},{4,20},{8,24},{12,28},{16,0},{20,4},{24,8},{28,12},{1,17},{... | collective-permute-start | bytes 1179656 | tf_op jit(solution)/shard_map/ppermute | solution.py:265
  29.4 15.3 %collective-permute-start.4 = (bf16[2,64,1536]{2,1,0:T(8,128)(2,1)S(1)}, bf16[2,64,1536]{2,1,0:T(8,128)(2,1)S(1)}, u32[]{:S(2)}, u32[]{:S(2)}) collective-permute-start(bf16[2,64,1536]{2,1,0:T(8,128)(2,1)S(1)} %select_select_fusion.refs_0_), channel_id=1, source_target_pairs={{0,8},{4,12},{8,0},{12,4},{16,24},{20,28},{24,16},{28,20},{1,9},{5... | collective-permute-start | bytes 1179656 | tf_op jit(solution)/shard_map/ppermute | solution.py:265
  46.0 3.8 %collective-permute-start.7 = (bf16[4,2,64,1536]{3,2,1,0:T(8,128)(2,1)}, bf16[4,2,64,1536]{3,2,1,0:T(8,128)(2,1)}, u32[]{:S(2)}, u32[]{:S(2)}) collective-permute-start(bf16[4,2,64,1536]{3,2,1,0:T(8,128)(2,1)} %get-tuple-element.17.refs_1_), channel_id=1, source_target_pairs={{0,4},{4,0},{8,12},{12,8},{16,20},{20,16},{24,28},{28,24},{1,5},{5... | collective-permute-start | bytes 4718600 | tf_op jit(solution)/shard_map/ppermute | solution.py:265
  52.7 17.5 %copy-start.6 = (bf16[2,1536,512]{2,1,0:T(8,128)(2,1)}, bf16[2,1536,512]{2,1,0:T(8,128)(2,1)S(1)}, u32[]{:S(2)}) copy-start(bf16[2,1536,512]{2,1,0:T(8,128)(2,1)S(1)} %get-tuple-element.19.refs_1_) | copy-start | bytes 9437188
  70.3 3.3 %copy-start = (bf16[32,2,128,512]{3,2,1,0:T(8,128)(2,1)}, bf16[32,2,128,512]{3,2,1,0:T(8,128)(2,1)S(1)}, u32[]{:S(2)}) copy-start(bf16[32,2,128,512]{3,2,1,0:T(8,128)(2,1)S(1)} %get-tuple-element.25.refs_3_.refs_2_) | copy-start | bytes 25165828
  81.6 0.6 copy-start.8
  82.2 75.9 %collective-permute-start.9 = (bf16[64,32,512]{2,1,0:T(8,128)(2,1)}, bf16[64,32,512]{2,1,0:T(8,128)(2,1)}, u32[]{:S(2)}, u32[]{:S(2)}) collective-permute-start(bf16[64,32,512]{2,1,0:T(8,128)(2,1)} %get-tuple-element.28), channel_id=1, source_target_pairs={{1,0},{0,1},{2,3},{3,2},{5,4},{4,5},{6,7},{7,6},{9,8},{8,9},{10,11... | collective-permute-start | bytes 6291464 | tf_op jit(solution)/shard_map/ppermute | solution.py:286
  104.0 57.7 %collective-permute-start.10 = (bf16[64,32,512]{2,1,0:T(8,128)(2,1)}, bf16[64,32,512]{2,1,0:T(8,128)(2,1)}, u32[]{:S(2)}, u32[]{:S(2)}) collective-permute-start(bf16[64,32,512]{2,1,0:T(8,128)(2,1)} %get-tuple-element.23.refs_0_), channel_id=1, source_target_pairs={{2,1},{1,2},{6,5},{5,6},{10,9},{9,10},{14,13},{13,14},{18,17},{17,... | collective-permute-start | bytes 6291464 | tf_op jit(solution)/shard_map/ppermute | solution.py:286
  116.2 19.4 %slice-start = ((s8[8388608]{0:T(1024)(128)(4,1)}), s8[4194304]{0:T(1024)(128)(4,1)S(1)}, s32[]{:S(2)}) async-start(s8[8388608]{0:T(1024)(128)(4,1)} %bitcast.14), calls=%async_computation.1 | async-start | bytes 8388608
  116.2 2.0 %copy-start.7 = (bf16[2,1536,512]{2,1,0:T(8,128)(2,1)S(1)}, bf16[2,1536,512]{2,1,0:T(8,128)(2,1)}, u32[]{:S(2)}) copy-start(bf16[2,1536,512]{2,1,0:T(8,128)(2,1)} %copy-done.6) | copy-start | bytes 9437188
  118.3 0.9 copy-start.9
  119.1 16.6 %slice-start.1 = ((s8[8388608]{0:T(1024)(128)(4,1)}), s8[4194304]{0:T(1024)(128)(4,1)S(1)}, s32[]{:S(2)}) async-start(s8[8388608]{0:T(1024)(128)(4,1)} %bitcast.14), calls=%async_computation.2 | async-start | bytes 8388608
  119.1 16.6 %copy-start.5 = (bf16[64,32,512]{2,1,0:T(8,128)(2,1)S(1)}, bf16[64,32,512]{2,1,0:T(8,128)(2,1)}, u32[]{:S(2)}) copy-start(bf16[64,32,512]{2,1,0:T(8,128)(2,1)} %get-tuple-element.23.refs_0_) | copy-start | bytes 6291460
  135.7 5.2 %copy-start.2 = (bf16[32,2,128,512]{3,2,1,0:T(8,128)(2,1)}, bf16[32,2,128,512]{3,2,1,0:T(8,128)(2,1)S(1)}, u32[]{:S(2)}) copy-start(bf16[32,2,128,512]{3,2,1,0:T(8,128)(2,1)S(1)} %get-tuple-element.27.refs_3_.refs_5_) | copy-start | bytes 25165828
  161.7 3.4 %copy-start.1 = (bf16[32,2,128,512]{3,2,1,0:T(8,128)(2,1)S(1)}, bf16[32,2,128,512]{3,2,1,0:T(8,128)(2,1)}, u32[]{:S(2)}) copy-start(bf16[32,2,128,512]{3,2,1,0:T(8,128)(2,1)} %copy-done) | copy-start | bytes 25165828
  165.0 4.9 %copy-start.3 = (bf16[32,2,128,512]{3,2,1,0:T(8,128)(2,1)S(1)}, bf16[32,2,128,512]{3,2,1,0:T(8,128)(2,1)}, u32[]{:S(2)}) copy-start(bf16[32,2,128,512]{3,2,1,0:T(8,128)(2,1)} %copy-done.2) | copy-start | bytes 25165828

commit v3 on v2

--- a/solution.py
+++ b/solution.py
@@ -22,7 +22,7 @@
     return part
 
 
-def call(kernel, inputs, in_specs, out_shape, out_spec, through, grid=(1,), scratch=(), vmem=20):
+def call(kernel, inputs, in_specs, out_shape, out_spec, through, grid=(1,), scratch=(), vmem=52):
     n_in, n_thru = len(inputs), len(through)
 
     def run(*refs):
@@ -66,17 +66,19 @@
         out_ref[...] = other_ref[...]
 
 
-def pick(flag, first, other, through):
-    block = (largest_part(first.shape[0], 16),) + first.shape[1:]
-    spec = pl.BlockSpec(block, lambda i: (i, 0, 0))
+def pick(flag, first, other, start, stop, through):
+    c_len = largest_part(stop - start, 16)
+    begin = start // c_len
+    block = (c_len,) + first.shape[1:]
+    spec = pl.BlockSpec(block, lambda i: (begin + i, 0, 0))
     return call(
         pick_kernel,
         [flag.astype(jnp.int32).reshape(1), first, other],
         [pl.BlockSpec(memory_space=pltpu.SMEM), spec, spec],
-        jax.ShapeDtypeStruct(first.shape, first.dtype),
-        spec,
+        jax.ShapeDtypeStruct((stop - start,) + first.shape[1:], first.dtype),
+        pl.BlockSpec(block, lambda i: (i, 0, 0)),
         through,
-        grid=(first.shape[0] // block[0],),
+        grid=((stop - start) // c_len,),
     )
 
 
@@ -131,22 +133,22 @@
             out_ref[:, b, :, j : j + wide] = turned.astype(jnp.bfloat16)
 
 
-def integrals(factors, batch, part, parts, through):
+def integrals(factors, batch, start, stop, through):
     a_rows, c_rows, aux_len = factors.shape
     bb, _, d_len = batch.shape
-    c_len = largest_part(c_rows // parts, 8)
-    count = c_rows // parts // c_len
+    c_len = largest_part(c_rows, 8)
+    first = start // c_len
     return call(
         integral_kernel,
         [factors, batch],
         [
-            pl.BlockSpec((a_rows, c_len, aux_len), lambda i: (0, part * count + i, 0)),
+            pl.BlockSpec((a_rows, c_len, aux_len), lambda i: (0, first + i, 0)),
             pl.BlockSpec((bb, aux_len, d_len), lambda i: (0, 0, 0)),
         ],
-        jax.ShapeDtypeStruct((c_rows // parts, bb, a_rows, d_len), jnp.bfloat16),
+        jax.ShapeDtypeStruct((stop - start, bb, a_rows, d_len), jnp.bfloat16),
         pl.BlockSpec((c_len, bb, a_rows, d_len), lambda i: (i, 0, 0, 0)),
         through,
-        grid=(count,),
+        grid=((stop - start) // c_len,),
     )
 
 
@@ -224,7 +226,7 @@
         [],
         grid=grid,
         scratch=[pltpu.VMEM(shape, jnp.float32)],
-        vmem=10,
+        vmem=52,
     )[0]
 
 
@@ -247,7 +249,7 @@
             pltpu.VMEM(shape, jnp.float32),
             pltpu.VMEM((early.shape[0] + shape[1], shape[0]), jnp.float32),
         ],
-        vmem=10,
+        vmem=52,
     )[0]
 
 
@@ -289,13 +291,13 @@
     token = jnp.zeros((8, LANES), jnp.float32)
     shared = spread(factors[:BB], n, z)
     batch, [token] = everywhere(shared, vir, [token])
-    halves = 2 if c_rows % 16 == 0 else 1
-    half = c_rows // halves
+    cut = 3 * c_rows // 4 if c_rows % 64 == 0 else c_rows
+    spans = [(0, cut), (cut, c_rows)] if cut < c_rows else [(0, c_rows)]
     made = []
 
     def make():
         nonlocal token
-        part, [token] = integrals(factors, batch, len(made), halves, [token])
+        part, [token] = integrals(factors, batch, *spans[len(made)], [token])
         made.append(part)
 
     make()
@@ -303,29 +305,33 @@
         inside = (z == 1) | (z == 2)
         first = send(own, (3, 1), (1, 0), (0, 2), (2, 3))
         second = send(own, (2, 0), (1, 3))
-        onward, [token] = pick(inside, first, own, [token])
-        sides = send(onward, (1, 0), (0, 1), (2, 3), (3, 2))
-        token, second, own = fence([token, second, own], MUCH)
-        middle = send(own, (2, 1), (1, 2))
-        early, late = [own, first, second], [sides, middle]
+        onward = []
+        for span in spans:
+            part, [token] = pick(inside, first, own, *span, [token])
+            onward.append(part)
+        token, second, *kept = fence([token, second] + [own[i:j] for i, j in spans], MUCH)
+        late = []
+        for part, mine in zip(onward, kept):
+            middle = send(mine, (2, 1), (1, 2))
+            late.append([send(part, (1, 0), (0, 1), (2, 3), (3, 2)), middle])
+        early = [own, first, second]
         slots = jnp.array([[0, 1, 2, 3], [3, 0, 4, 1], [1, 4, 0, 3], [3, 2, 1, 0]], jnp.int32)[z]
     else:
         gathered = lax.all_gather(own, "out")
-        early, late = [own], [gathered[k] for k in range(n)]
+        early, late = [own], [[gathered[k, i:j] for k in range(n)] for i, j in spans]
         slots = jnp.arange(1, n + 1, dtype=jnp.int32)
-    while len(made) < halves:
+    while len(made) < len(spans):
         make()
 
-    if n == 4:
-        late[0] = fence(late[:1], MUCH)[0]
-    known, added = None, jnp.zeros((sum(t.shape[1] for t in late), BB * a_rows), jnp.float32)
-    for k, part in enumerate(made):
-        terms = ladder_early(early, part, k * half)
+    known, added = None, None
+    for part, (start, _) in zip(made, spans):
+        terms = ladder_early(early, part, start)
         known = terms if known is None else known + terms
-    for k, part in enumerate(made[:-1]):
-        terms = ladder_early(late, part, k * half)
-        added = terms if k == 0 else added + terms
-    parts = ladder_late(slots, known, added, late, made[-1], c_rows - half, vir)
+    for part, taus in zip(made[:-1], late):
+        added = ladder_early(taus, part, 0)
+    if added is None:
+        added = jnp.zeros((sum(t.shape[1] for t in late[-1]), BB * a_rows), jnp.float32)
+    parts = ladder_late(slots, known, added, late[-1], made[-1], 0, vir)
     swapped = lax.all_to_all(parts, "vir", split_axis=0, concat_axis=0)
     return jnp.sum(swapped, axis=0)
 

time: 186 us -> 184 us (0.989)
  waiting for transfers between devices: 69.8 us -> 46.3 us
  starting transfers between devices: 27.6 us -> 40.4 us
  Pallas kernels: 60.8 us -> 71.7 us
    ppermute x4 -> x6, waiting for transfers between devices: 42.4 us -> 23.8 us  [send(): return lax.ppermute(array, 'out', ways)]
    ppermute x4 -> x6, starting transfers between devices: 20.6 us -> 34.2 us  [send(): return lax.ppermute(array, 'out', ways)]
    pallas_call x9 -> x10, Pallas kernels: 60.8 us -> 71.7 us  [call(): pl.pallas_call(run, grid=grid, in_specs=list(in_specs) + [anywhere] * n_t...]
    unnamed x25 -> x9, local copies, waits for them, and re-layouts: 12.9 us -> 6.53 us
    slice x0 -> x2, local copies, waits for them, and re-layouts: none -> 4.74 us  [body(): own[i:j]]
    ppermute x4, waiting for transfers between devices: 18.4 us -> 14.9 us  [swap(): return lax.ppermute(array, 'vir', [(k, k ^ mask) for k in range(vir)])]
  transfers between devices with their start and end apart: 11 -> 13, of which waited for: 9 -> 7; matrix products, arithmetic and copies ran while one was open for 3% -> 6% of each run, Pallas kernels for 28% -> 38%
where the time goes in v3:
time: 184 us; the launch traced here: 182 us
  Pallas kernels  71.7 us (39%)
  waiting for transfers between devices  46.3 us (25%)
  starting transfers between devices  40.4 us (22%)
  local copies, waits for them, and re-layouts  13.1 us (7%)
  blocking collectives  9.05 us (5%)
    pallas_call x10, Pallas kernels, call(): pl.pallas_call(run, grid=grid, in_specs=list(in_specs) + [anywhere] * n_t...  71.7 us
    ppermute x6, starting transfers between devices, send(): return lax.ppermute(array, 'out', ways)  34.2 us
    ppermute x6, waiting for transfers between devices, send(): return lax.ppermute(array, 'out', ways)  23.8 us
    ppermute x4, waiting for transfers between devices, swap(): return lax.ppermute(array, 'vir', [(k, k ^ mask) for k in range(vir)])  14.9 us
    all_to_all x1, blocking collectives, body(): swapped = lax.all_to_all(parts, 'vir', split_axis=0, concat_axis=0)  9.05 us
    ppermute x3, waiting for transfers between devices, spread(): heres = [lax.ppermute(rows, 'out', [(0, k)]) for k in range(n - 1, 0, -1)]  7.62 us
    unnamed x9, local copies, waits for them, and re-layouts  6.53 us
    slice x2, local copies, waits for them, and re-layouts, body(): own[i:j]  4.74 us
  transfers between devices with their start and end apart: 13, of which 7 were waited for; matrix products, arithmetic and copies ran while one was open for 6% of the time, Pallas kernels for 38%

profile of v3, /device:TPU:16, one launch (start us, length us, event | category | flops | bytes accessed | tf_op | source)
XLA Modules:
  0.0 182.5 jit_solution(9086014470956539880)
XLA Ops:
  0.0 1.0 slice.9
  1.0 0.7 collective-permute-start.1
  1.7 1.3 collective-permute-start.2
  3.0 0.7 collective-permute-start.3
  3.7 4.1 %copy.16 = bf16[32,64,512]{2,0,1:T(8,128)(2,1)} copy(bf16[32,64,512]{2,1,0:T(8,128)(2,1)} %param.4) | data formatting | bytes 4194304 | tf_op args[1]
  7.8 1.6 collective-permute-start
  9.4 6.3 %collective-permute-start.8 = (bf16[64,32,512]{2,1,0:T(8,128)(2,1)}, bf16[64,32,512]{2,1,0:T(8,128)(2,1)}, u32[]{:S(2)}, u32[]{:S(2)}) collective-permute-start(bf16[64,32,512]{2,1,0:T(8,128)(2,1)} %bitcast.13.refs_2_.refs_0_), channel_id=1, source_target_pairs={{2,0},{1,3},{6,4},{5,7},{10,8},{9,11},{14,12},{13,15},{18,16},{17,... | collective-permute-start | bytes 6291464 | tf_op jit(solution)/shard_map/ppermute | solution.py:288
  15.7 0.0 collective-permute-done.1
  15.7 7.6 %collective-permute-done.2 = bf16[2,64,1536]{2,1,0:T(8,128)(2,1)S(1)} collective-permute-done((bf16[2,64,1536]{2,1,0:T(8,128)(2,1)S(1)}, bf16[2,64,1536]{2,1,0:T(8,128)(2,1)S(1)}, u32[]{:S(2)}, u32[]{:S(2)}) %collective-permute-start.2) | collective-permute-done | bytes 393248 | tf_op jit(solution)/shard_map/ppermute | solution.py:257
  23.3 0.0 collective-permute-done.3
  23.3 1.1 select_select_fusion.refs_0_
  24.4 1.6 collective-permute-start.4
  26.0 1.5 collective-permute-start.5
  27.5 0.5 collective-permute-start.6
  28.0 8.6 %collective-permute-done.4.refs_1_ = bf16[2,64,1536]{2,1,0:T(8,128)(2,1)S(1)} collective-permute-done((bf16[2,64,1536]{2,1,0:T(8,128)(2,1)S(1)}, bf16[2,64,1536]{2,1,0:T(8,128)(2,1)S(1)}, u32[]{:S(2)}, u32[]{:S(2)}) %collective-permute-start.4) | collective-permute-done | bytes 393248 | tf_op jit(solution)/shard_map/ppermute | solution.py:267
  36.5 6.4 %collective-permute-done.5.refs_2_ = bf16[2,64,1536]{2,1,0:T(8,128)(2,1)S(1)} collective-permute-done((bf16[2,64,1536]{2,1,0:T(8,128)(2,1)S(1)}, bf16[2,64,1536]{2,1,0:T(8,128)(2,1)S(1)}, u32[]{:S(2)}, u32[]{:S(2)}) %collective-permute-start.5) | collective-permute-done | bytes 393248 | tf_op jit(solution)/shard_map/ppermute | solution.py:267
  42.9 0.0 collective-permute-done.6.refs_3_
  42.9 1.3 shard_map.37
  44.2 0.0 collective-permute-start.7
  44.2 0.0 copy-start
  44.2 2.9 %slice.12.refs_2_ = bf16[48,32,512]{2,1,0:T(8,128)(2,1)} slice(bf16[64,32,512]{2,1,0:T(8,128)(2,1)} %bitcast.13.refs_2_.refs_0_), slice={[0:48], [0:32], [0:512]} | slice | bytes 3145728 | tf_op jit(solution)/shard_map/slice | solution.py:312
  47.0 1.9 %slice.13.refs_3_ = bf16[16,32,512]{2,1,0:T(8,128)(2,1)} slice(bf16[64,32,512]{2,1,0:T(8,128)(2,1)} %bitcast.13.refs_2_.refs_0_), slice={[48:64], [0:32], [0:512]} | slice | bytes 1048576 | tf_op jit(solution)/shard_map/slice | solution.py:312
  48.9 0.1 stack.35.refs_0_
  49.0 0.0 collective-permute-done.7.refs_2_
  49.0 0.0 copy-start.3
  49.0 1.1 copy-done.3
  50.1 0.0 copy-done
  50.2 4.1 %shard_map.38 = (bf16[2,1536,512]{2,1,0:T(8,128)(2,1)}, f32[8,128]{1,0:T(8,128)S(1)}) custom-call(s32[8]{0:T(128)S(1)} %stack.35.refs_0_, bf16[4,2,64,1536]{3,2,1,0:T(8,128)(2,1)S(1)} %copy-done, bf16[4,2,64,1536]{3,2,1,0:T(8,128)(2,1)} %copy-done.3, f32[8,128]{1,0:T(8,128)S(1)} %get-tuple-element.21.refs_3_), custom_call_target="tpu_custom_call", output_to_operand_aliasing={{1}: (3, {})} | custom-call | flops 1024 | bytes 1024 | tf_op jit(solution)/shard_map/pallas_call | solution.py:33
  54.3 25.9 %shard_map.39 = (bf16[48,2,128,512]{3,2,1,0:T(8,128)(2,1)}, f32[8,128]{1,0:T(8,128)S(1)}) custom-call(bf16[128,64,1536]{2,1,0:T(8,128)(2,1)} %refs_0_.3, bf16[2,1536,512]{2,1,0:T(8,128)(2,1)} %get-tuple-element.22.refs_1_, f32[8,128]{1,0:T(8,128)S(1)} %get-tuple-element.23.refs_2_), custom_call_target="tpu_custom_call", output_to_operand_aliasing={{1}: (2, {})} | custom-call | flops 1024 | bytes 1024 | tf_op jit(solution)/shard_map/pallas_call | solution.py:33
  80.2 0.0 collective-permute-done.refs_1_
  80.2 3.8 %shard_map.40 = (bf16[48,32,512]{2,1,0:T(8,128)(2,1)}, f32[8,128]{1,0:T(8,128)S(1)}) custom-call(s32[1]{0:T(128)} %bitcast.2.refs_0_, bf16[64,32,512]{2,1,0:T(8,128)(2,1)} %collective-permute-done.refs_1_, bf16[64,32,512]{2,1,0:T(8,128)(2,1)} %bitcast.13.refs_2_.refs_0_, f32[8,128]{1,0:T(8,128)S(1)} %get-tuple-element.24.refs_3_), custom_call_target="tpu_custom_call", output_to_operand_aliasing={{1}: (3, {})} | custom-call | flops 1024 | bytes 1024 | tf_op jit(solution)/shard_map/pallas_call | solution.py:33
  84.0 1.2 shard_map.41
  85.2 0.0 copy-start.1
  85.2 0.6 copy-done.1
  85.8 13.6 %collective-permute-done.8.refs_1_ = bf16[64,32,512]{2,1,0:T(8,128)(2,1)} collective-permute-done((bf16[64,32,512]{2,1,0:T(8,128)(2,1)}, bf16[64,32,512]{2,1,0:T(8,128)(2,1)}, u32[]{:S(2)}, u32[]{:S(2)}) %collective-permute-start.8) | collective-permute-done | bytes 2097184 | tf_op jit(solution)/shard_map/ppermute | solution.py:288
  99.4 22.5 %collective-permute-start.10 = (bf16[48,32,512]{2,1,0:T(8,128)(2,1)}, bf16[48,32,512]{2,1,0:T(8,128)(2,1)}, u32[]{:S(2)}, u32[]{:S(2)}) collective-permute-start(bf16[48,32,512]{2,1,0:T(8,128)(2,1)} %get-tuple-element.32), channel_id=1, source_target_pairs={{2,1},{1,2},{6,5},{5,6},{10,9},{9,10},{14,13},{13,14},{18,17},{17,... | collective-permute-start | bytes 4718600 | tf_op jit(solution)/shard_map/ppermute | solution.py:288
  121.9 1.8 %collective-permute-start.9 = (bf16[48,32,512]{2,1,0:T(8,128)(2,1)}, bf16[48,32,512]{2,1,0:T(8,128)(2,1)S(1)}, u32[]{:S(2)}, u32[]{:S(2)}) collective-permute-start(bf16[48,32,512]{2,1,0:T(8,128)(2,1)} %get-tuple-element.31), channel_id=1, source_target_pairs={{1,0},{0,1},{2,3},{3,2},{5,4},{4,5},{6,7},{7,6},{9,8},{8,9},{10,11... | collective-permute-start | bytes 4718600 | tf_op jit(solution)/shard_map/ppermute | solution.py:288
  123.7 1.9 %collective-permute-start.12 = (bf16[16,32,512]{2,1,0:T(8,128)(2,1)}, bf16[16,32,512]{2,1,0:T(8,128)(2,1)S(1)}, u32[]{:S(2)}, u32[]{:S(2)}) collective-permute-start(bf16[16,32,512]{2,1,0:T(8,128)(2,1)} %get-tuple-element.34), channel_id=1, source_target_pairs={{2,1},{1,2},{6,5},{5,6},{10,9},{9,10},{14,13},{13,14},{18,17},{17,... | collective-permute-start | bytes 1572872 | tf_op jit(solution)/shard_map/ppermute | solution.py:288
  125.6 0.1 collective-permute-start.11
  125.7 0.7 dynamic-slice_bitcast_fusion.refs_0_
  126.4 0.0 copy-start.2
  126.4 0.7 copy-done.2
  127.1 11.4 %shard_map.44 = (bf16[16,2,128,512]{3,2,1,0:T(8,128)(2,1)}, f32[8,128]{1,0:T(8,128)S(1)}) custom-call(bf16[128,64,1536]{2,1,0:T(8,128)(2,1)} %refs_0_.3, bf16[2,1536,512]{2,1,0:T(8,128)(2,1)} %get-tuple-element.22.refs_1_, f32[8,128]{1,0:T(8,128)S(1)} %copy-done.2), custom_call_target="tpu_custom_call", output_to_operand_aliasing={{1}: (2, {})} | custom-call | flops 1024 | bytes 1024 | tf_op jit(solution)/shard_map/pallas_call | solution.py:33
  138.5 3.5 %shard_map.45 = f32[96,256]{1,0:T(8,128)S(1)} custom-call(bf16[64,32,512]{2,1,0:T(8,128)(2,1)} %bitcast.13.refs_2_.refs_0_, bf16[64,32,512]{2,1,0:T(8,128)(2,1)} %collective-permute-done.refs_1_, bf16[64,32,512]{2,1,0:T(8,128)(2,1)} %get-tuple-element.27.refs_2_, bf16[16,2,128,512]{3,2,1,0:T(8,128)(2,1)} %get-tuple-element.30.refs_3_.refs_5_), custom_call_target="tpu_custom_call" | custom-call | flops 1024 | bytes 1024 | tf_op jit(solution)/shard_map/pallas_call | solution.py:33
  142.1 9.0 %shard_map.43 = f32[96,256]{1,0:T(8,128)S(1)} custom-call(bf16[64,32,512]{2,1,0:T(8,128)(2,1)} %bitcast.13.refs_2_.refs_0_, bf16[64,32,512]{2,1,0:T(8,128)(2,1)} %collective-permute-done.refs_1_, bf16[64,32,512]{2,1,0:T(8,128)(2,1)} %get-tuple-element.27.refs_2_, bf16[48,2,128,512]{3,2,1,0:T(8,128)(2,1)} %get-tuple-element.28.refs_3_.refs_2_), custom_call_target="tpu_custom_call" | custom-call | flops 1024 | bytes 1024 | tf_op jit(solution)/shard_map/pallas_call | solution.py:33
  151.1 6.3 %collective-permute-done.10.refs_1_ = bf16[48,32,512]{2,1,0:T(8,128)(2,1)} collective-permute-done((bf16[48,32,512]{2,1,0:T(8,128)(2,1)}, bf16[48,32,512]{2,1,0:T(8,128)(2,1)}, u32[]{:S(2)}, u32[]{:S(2)}) %collective-permute-start.10) | collective-permute-done | bytes 1572896 | tf_op jit(solution)/shard_map/ppermute | solution.py:288
  157.4 2.0 %collective-permute-done.9.refs_0_ = bf16[48,32,512]{2,1,0:T(8,128)(2,1)S(1)} collective-permute-done((bf16[48,32,512]{2,1,0:T(8,128)(2,1)}, bf16[48,32,512]{2,1,0:T(8,128)(2,1)S(1)}, u32[]{:S(2)}, u32[]{:S(2)}) %collective-permute-start.9) | collective-permute-done | bytes 1572896 | tf_op jit(solution)/shard_map/ppermute | solution.py:288
  159.4 8.3 %shard_map.46.refs_2_ = f32[64,256]{1,0:T(8,128)S(1)} custom-call(bf16[48,32,512]{2,1,0:T(8,128)(2,1)S(1)} %collective-permute-done.9.refs_0_, bf16[48,32,512]{2,1,0:T(8,128)(2,1)} %collective-permute-done.10.refs_1_, bf16[48,2,128,512]{3,2,1,0:T(8,128)(2,1)} %get-tuple-element.28.refs_3_.refs_2_), custom_call_target="tpu_custom_call" | custom-call | flops 1024 | bytes 1024 | tf_op jit(solution)/shard_map/pallas_call | solution.py:33
  167.7 0.0 collective-permute-done.12.refs_4_
  167.8 1.9 %collective-permute-done.11.refs_3_ = bf16[16,32,512]{2,1,0:T(8,128)(2,1)S(1)} collective-permute-done((bf16[16,32,512]{2,1,0:T(8,128)(2,1)S(1)}, bf16[16,32,512]{2,1,0:T(8,128)(2,1)S(1)}, u32[]{:S(2)}, u32[]{:S(2)}) %collective-permute-start.11) | collective-permute-done | bytes 524320 | tf_op jit(solution)/shard_map/ppermute | solution.py:288
  169.6 3.1 %shard_map.47 = f32[8,2,16,128]{3,2,1,0:T(8,128)S(1)} custom-call(s32[4]{0:T(128)S(1)} %dynamic-slice_bitcast_fusion.refs_0_, f32[96,256]{1,0:T(8,128)S(1)} %add.7.refs_1_, f32[64,256]{1,0:T(8,128)S(1)} %shard_map.46.refs_2_, bf16[16,32,512]{2,1,0:T(8,128)(2,1)S(1)} %collective-permute-done.11.refs_3_, ...), custom_call_target="tpu_custom_call" | custom-call | flops 1024 | bytes 1024 | tf_op jit(solution)/shard_map/pallas_call | solution.py:33
  172.8 9.1 %all_to_all.5 = f32[8,2,16,128]{3,2,1,0:T(8,128)S(1)} all-to-all(f32[8,2,16,128]{3,2,1,0:T(8,128)S(1)} %shard_map.47), channel_id=1, replica_groups=mesh['vir'=8,'out'=4] {'vir'}, dimensions={0} | all-to-all | bytes 262144 | tf_op jit(solution)/shard_map/all_to_all | solution.py:335
  181.8 0.6 reduce_sum.9
  (3 shorter events, 0.0 us)
Async XLA Ops:
  1.0 14.7 %collective-permute-start.1 = (bf16[2,64,1536]{2,1,0:T(8,128)(2,1)S(1)}, bf16[2,64,1536]{2,1,0:T(8,128)(2,1)S(1)}, u32[]{:S(2)}, u32[]{:S(2)}) collective-permute-start(bf16[2,64,1536]{2,1,0:T(8,128)(2,1)S(1)} %slice.9), channel_id=1, source_target_pairs={{0,1},{4,5},{8,9},{12,13},{16,17},{20,21},{24,25},{28,29}} | collective-permute-start | bytes 1179656 | tf_op jit(solution)/shard_map/ppermute | solution.py:257
  1.7 21.6 %collective-permute-start.2 = (bf16[2,64,1536]{2,1,0:T(8,128)(2,1)S(1)}, bf16[2,64,1536]{2,1,0:T(8,128)(2,1)S(1)}, u32[]{:S(2)}, u32[]{:S(2)}) collective-permute-start(bf16[2,64,1536]{2,1,0:T(8,128)(2,1)S(1)} %slice.9), channel_id=1, source_target_pairs={{0,2},{4,6},{8,10},{12,14},{16,18},{20,22},{24,26},{28,30}} | collective-permute-start | bytes 1179656 | tf_op jit(solution)/shard_map/ppermute | solution.py:257
  3.0 20.3 %collective-permute-start.3 = (bf16[2,64,1536]{2,1,0:T(8,128)(2,1)S(1)}, bf16[2,64,1536]{2,1,0:T(8,128)(2,1)S(1)}, u32[]{:S(2)}, u32[]{:S(2)}) collective-permute-start(bf16[2,64,1536]{2,1,0:T(8,128)(2,1)S(1)} %slice.9), channel_id=1, source_target_pairs={{0,3},{4,7},{8,11},{12,15},{16,19},{20,23},{24,27},{28,31}} | collective-permute-start | bytes 1179656 | tf_op jit(solution)/shard_map/ppermute | solution.py:257
  7.8 72.4 %collective-permute-start = (bf16[64,32,512]{2,1,0:T(8,128)(2,1)}, bf16[64,32,512]{2,1,0:T(8,128)(2,1)}, u32[]{:S(2)}, u32[]{:S(2)}) collective-permute-start(bf16[64,32,512]{2,1,0:T(8,128)(2,1)} %bitcast.13.refs_2_.refs_0_), channel_id=1, source_target_pairs={{3,1},{1,0},{0,2},{2,3},{7,5},{5,4},{4,6},{6,7},{11,9},{9,8},{8,10... | collective-permute-start | bytes 6291464 | tf_op jit(solution)/shard_map/ppermute | solution.py:288
  9.4 90.0 %collective-permute-start.8 = (bf16[64,32,512]{2,1,0:T(8,128)(2,1)}, bf16[64,32,512]{2,1,0:T(8,128)(2,1)}, u32[]{:S(2)}, u32[]{:S(2)}) collective-permute-start(bf16[64,32,512]{2,1,0:T(8,128)(2,1)} %bitcast.13.refs_2_.refs_0_), channel_id=1, source_target_pairs={{2,0},{1,3},{6,4},{5,7},{10,8},{9,11},{14,12},{13,15},{18,16},{17,... | collective-permute-start | bytes 6291464 | tf_op jit(solution)/shard_map/ppermute | solution.py:288
  24.4 12.1 %collective-permute-start.4 = (bf16[2,64,1536]{2,1,0:T(8,128)(2,1)S(1)}, bf16[2,64,1536]{2,1,0:T(8,128)(2,1)S(1)}, u32[]{:S(2)}, u32[]{:S(2)}) collective-permute-start(bf16[2,64,1536]{2,1,0:T(8,128)(2,1)S(1)} %select_select_fusion.refs_0_), channel_id=1, source_target_pairs={{0,8},{4,12},{8,0},{12,4},{16,24},{20,28},{24,16},{28,20},{1,9},{5... | collective-permute-start | bytes 1179656 | tf_op jit(solution)/shard_map/ppermute | solution.py:267
  26.0 16.9 %collective-permute-start.5 = (bf16[2,64,1536]{2,1,0:T(8,128)(2,1)S(1)}, bf16[2,64,1536]{2,1,0:T(8,128)(2,1)S(1)}, u32[]{:S(2)}, u32[]{:S(2)}) collective-permute-start(bf16[2,64,1536]{2,1,0:T(8,128)(2,1)S(1)} %select_select_fusion.refs_0_), channel_id=1, source_target_pairs={{0,16},{4,20},{8,24},{12,28},{16,0},{20,4},{24,8},{28,12},{1,17},{... | collective-permute-start | bytes 1179656 | tf_op jit(solution)/shard_map/ppermute | solution.py:267
  27.5 15.4 %collective-permute-start.6 = (bf16[2,64,1536]{2,1,0:T(8,128)(2,1)S(1)}, bf16[2,64,1536]{2,1,0:T(8,128)(2,1)S(1)}, u32[]{:S(2)}, u32[]{:S(2)}) collective-permute-start(bf16[2,64,1536]{2,1,0:T(8,128)(2,1)S(1)} %select_select_fusion.refs_0_), channel_id=1, source_target_pairs={{0,24},{4,28},{8,16},{12,20},{16,8},{20,12},{24,0},{28,4},{1,25},{... | collective-permute-start | bytes 1179656 | tf_op jit(solution)/shard_map/ppermute | solution.py:267
  44.2 4.8 %collective-permute-start.7 = (bf16[4,2,64,1536]{3,2,1,0:T(8,128)(2,1)}, bf16[4,2,64,1536]{3,2,1,0:T(8,128)(2,1)S(1)}, u32[]{:S(2)}, u32[]{:S(2)}) collective-permute-start(bf16[4,2,64,1536]{3,2,1,0:T(8,128)(2,1)} %get-tuple-element.20.refs_1_), channel_id=1, source_target_pairs={{0,4},{4,0},{8,12},{12,8},{16,20},{20,16},{24,28},{28,24},{1,5},{5... | collective-permute-start | bytes 4718600 | tf_op jit(solution)/shard_map/ppermute | solution.py:267
  44.2 6.0 %copy-start = (bf16[4,2,64,1536]{3,2,1,0:T(8,128)(2,1)S(1)}, bf16[4,2,64,1536]{3,2,1,0:T(8,128)(2,1)}, u32[]{:S(2)}) copy-start(bf16[4,2,64,1536]{3,2,1,0:T(8,128)(2,1)} %get-tuple-element.20.refs_1_) | copy-start | bytes 4718596
  49.0 1.1 copy-start.3
  85.2 0.6 copy-start.1
  99.4 58.0 %collective-permute-start.10 = (bf16[48,32,512]{2,1,0:T(8,128)(2,1)}, bf16[48,32,512]{2,1,0:T(8,128)(2,1)}, u32[]{:S(2)}, u32[]{:S(2)}) collective-permute-start(bf16[48,32,512]{2,1,0:T(8,128)(2,1)} %get-tuple-element.32), channel_id=1, source_target_pairs={{2,1},{1,2},{6,5},{5,6},{10,9},{9,10},{14,13},{13,14},{18,17},{17,... | collective-permute-start | bytes 4718600 | tf_op jit(solution)/shard_map/ppermute | solution.py:288
  121.9 37.5 %collective-permute-start.9 = (bf16[48,32,512]{2,1,0:T(8,128)(2,1)}, bf16[48,32,512]{2,1,0:T(8,128)(2,1)S(1)}, u32[]{:S(2)}, u32[]{:S(2)}) collective-permute-start(bf16[48,32,512]{2,1,0:T(8,128)(2,1)} %get-tuple-element.31), channel_id=1, source_target_pairs={{1,0},{0,1},{2,3},{3,2},{5,4},{4,5},{6,7},{7,6},{9,8},{8,9},{10,11... | collective-permute-start | bytes 4718600 | tf_op jit(solution)/shard_map/ppermute | solution.py:288
  123.7 44.0 %collective-permute-start.12 = (bf16[16,32,512]{2,1,0:T(8,128)(2,1)}, bf16[16,32,512]{2,1,0:T(8,128)(2,1)S(1)}, u32[]{:S(2)}, u32[]{:S(2)}) collective-permute-start(bf16[16,32,512]{2,1,0:T(8,128)(2,1)} %get-tuple-element.34), channel_id=1, source_target_pairs={{2,1},{1,2},{6,5},{5,6},{10,9},{9,10},{14,13},{13,14},{18,17},{17,... | collective-permute-start | bytes 1572872 | tf_op jit(solution)/shard_map/ppermute | solution.py:288
  125.6 44.0 %collective-permute-start.11 = (bf16[16,32,512]{2,1,0:T(8,128)(2,1)S(1)}, bf16[16,32,512]{2,1,0:T(8,128)(2,1)S(1)}, u32[]{:S(2)}, u32[]{:S(2)}) collective-permute-start(bf16[16,32,512]{2,1,0:T(8,128)(2,1)S(1)} %get-tuple-element.33), channel_id=1, source_target_pairs={{1,0},{0,1},{2,3},{3,2},{5,4},{4,5},{6,7},{7,6},{9,8},{8,9},{10,11... | collective-permute-start | bytes 1572872 | tf_op jit(solution)/shard_map/ppermute | solution.py:288
  126.4 0.7 copy-start.2

commit v4 on v3

--- a/solution.py
+++ b/solution.py
@@ -12,6 +12,7 @@
 NT = (((1,), (1,)), ((), ()))
 NN = (((1,), (0,)), ((), ()))
 LITTLE = pl.CostEstimate(flops=1024, bytes_accessed=1024, transcendentals=0)
+MORE = pl.CostEstimate(flops=24 * 10**9, bytes_accessed=48 * 10**6, transcendentals=0)
 MUCH = pl.CostEstimate(flops=2 * 10**10, bytes_accessed=4 * 10**7, transcendentals=0)
 
 
@@ -205,21 +206,23 @@
                 out_ref[j, b] = all_ref[pl.ds(start, rows), b * a_rows : (b + 1) * a_rows]
 
 
-def ladder_specs(taus, integral, start):
-    _, pairs, d_len = taus[0].shape
+def ladder_specs(taus, integral):
+    _, pairs, d_len = taus[0][0].shape
     c_rows, bb, a_rows, _ = integral.shape
     c_len = largest_part(c_rows, 8)
-    first = start // c_len
-    specs = [pl.BlockSpec((c_len, pairs, d_len), lambda i: (first + i, 0, 0)) for _ in taus]
+    specs = [
+        pl.BlockSpec((c_len, pairs, d_len), lambda i, k=start // c_len: (k + i, 0, 0))
+        for _, start in taus
+    ]
     specs.append(pl.BlockSpec((c_len, bb, a_rows, d_len), lambda i: (i, 0, 0, 0)))
     return specs, (bb * a_rows, len(taus) * pairs), (c_rows // c_len,)
 
 
-def ladder_early(taus, integral, start):
-    specs, shape, grid = ladder_specs(taus, integral, start)
+def ladder_early(taus, integral):
+    specs, shape, grid = ladder_specs(taus, integral)
     return call(
         functools.partial(early_kernel, len(taus)),
-        taus + [integral],
+        [t for t, _ in taus] + [integral],
         specs,
         jax.ShapeDtypeStruct(shape[::-1], jnp.float32),
         pl.BlockSpec(shape[::-1], lambda i: (0, 0)),
@@ -230,14 +233,14 @@
     )[0]
 
 
-def ladder_late(slots, early, added, taus, integral, start, owners):
-    specs, shape, grid = ladder_specs(taus, integral, start)
-    pairs = taus[0].shape[1]
+def ladder_late(slots, early, added, taus, integral, owners):
+    specs, shape, grid = ladder_specs(taus, integral)
+    pairs = taus[0][0].shape[1]
     _, bb, a_rows, _ = integral.shape
     out = (owners, bb, slots.shape[0] * pairs // owners, a_rows)
     return call(
         functools.partial(late_kernel, len(taus)),
-        [slots, early, added] + taus + [integral],
+        [slots, early, added] + [t for t, _ in taus] + [integral],
         [pl.BlockSpec(memory_space=pltpu.SMEM)]
         + [pl.BlockSpec(t.shape, lambda i: (0, 0)) for t in (early, added)]
         + specs,
@@ -254,8 +257,8 @@
 
 
 def spread(rows, n, z):
-    heres = [lax.ppermute(rows, "out", [(0, k)]) for k in range(n - 1, 0, -1)]
-    for k, here in zip(range(n - 1, 0, -1), heres):
+    heres = [lax.ppermute(rows, "out", [(0, k)]) for k in range(1, n)]
+    for k, here in zip(range(1, n), heres):
         rows = jnp.where(z == k, here, rows)
     return rows
 
@@ -303,35 +306,32 @@
     make()
     if n == 4:
         inside = (z == 1) | (z == 2)
+        second = send(own, (2, 0), (1, 3))
         first = send(own, (3, 1), (1, 0), (0, 2), (2, 3))
-        second = send(own, (2, 0), (1, 3))
-        onward = []
-        for span in spans:
-            part, [token] = pick(inside, first, own, *span, [token])
-            onward.append(part)
-        token, second, *kept = fence([token, second] + [own[i:j] for i, j in spans], MUCH)
-        late = []
-        for part, mine in zip(onward, kept):
-            middle = send(mine, (2, 1), (1, 2))
-            late.append([send(part, (1, 0), (0, 1), (2, 3), (3, 2)), middle])
+        onward, [token] = pick(inside, first, own, 0, c_rows, [token])
+        sides = send(onward, (1, 0), (0, 1), (2, 3), (3, 2))
+        token, second, *kept = fence([token, second] + [own[i:j] for i, j in spans], MORE)
+        [sides] = fence([sides], MUCH)
         early = [own, first, second]
+        late = [[(sides, i), (send(t, (2, 1), (1, 2)), 0)] for (i, _), t in zip(spans, kept)]
         slots = jnp.array([[0, 1, 2, 3], [3, 0, 4, 1], [1, 4, 0, 3], [3, 2, 1, 0]], jnp.int32)[z]
     else:
         gathered = lax.all_gather(own, "out")
-        early, late = [own], [[gathered[k, i:j] for k in range(n)] for i, j in spans]
+        early, late = [own], [[(gathered[k], i) for k in range(n)] for i, _ in spans]
         slots = jnp.arange(1, n + 1, dtype=jnp.int32)
     while len(made) < len(spans):
         make()
 
     known, added = None, None
     for part, (start, _) in zip(made, spans):
-        terms = ladder_early(early, part, start)
+        terms = ladder_early([(t, start) for t in early], part)
         known = terms if known is None else known + terms
     for part, taus in zip(made[:-1], late):
-        added = ladder_early(taus, part, 0)
+        added = ladder_early(taus, part)
     if added is None:
-        added = jnp.zeros((sum(t.shape[1] for t in late[-1]), BB * a_rows), jnp.float32)
-    parts = ladder_late(slots, known, added, late[-1], made[-1], 0, vir)
+        rows = sum(t.shape[1] for t, _ in late[-1])
+        added = jnp.zeros((rows, BB * a_rows), jnp.float32)
+    parts = ladder_late(slots, known, added, late[-1], made[-1], vir)
     swapped = lax.all_to_all(parts, "vir", split_axis=0, concat_axis=0)
     return jnp.sum(swapped, axis=0)
 

time: 184 us -> 181 us (0.984)
  starting transfers between devices: 40.4 us -> 33.6 us
  waiting for transfers between devices: 46.3 us -> 50.7 us
    ppermute x6 -> x5, starting transfers between devices: 34.2 us -> 27.4 us  [send(): return lax.ppermute(array, 'out', ways)]
    ppermute x6 -> x5, waiting for transfers between devices: 23.8 us -> 27.3 us  [send(): return lax.ppermute(array, 'out', ways)]
    pallas_call x10 -> x9, Pallas kernels: 71.7 us -> 71.1 us  [call(): pl.pallas_call(run, grid=grid, in_specs=list(in_specs) + [anywhere] * n_t...]
    unnamed x9 -> x11, local copies, waits for them, and re-layouts: 6.53 us -> 6.57 us
  transfers between devices with their start and end apart: 13 -> 12, of which waited for: 7 -> 5; matrix products, arithmetic and copies ran while one was open for 6% -> 6% of each run, Pallas kernels for 38% -> 38%
where the time goes in v4:
time: 181 us; the launch traced here: 179 us
  Pallas kernels  71.1 us (39%)
  waiting for transfers between devices  50.7 us (28%)
  starting transfers between devices  33.6 us (19%)
  local copies, waits for them, and re-layouts  13.1 us (7%)
  blocking collectives  9.05 us (5%)
    pallas_call x9, Pallas kernels, call(): pl.pallas_call(run, grid=grid, in_specs=list(in_specs) + [anywhere] * n_t...  71.1 us
    ppermute x5, starting transfers between devices, send(): return lax.ppermute(array, 'out', ways)  27.4 us
    ppermute x5, waiting for transfers between devices, send(): return lax.ppermute(array, 'out', ways)  27.3 us
    ppermute x4, waiting for transfers between devices, swap(): return lax.ppermute(array, 'vir', [(k, k ^ mask) for k in range(vir)])  15 us
    all_to_all x1, blocking collectives, body(): swapped = lax.all_to_all(parts, 'vir', split_axis=0, concat_axis=0)  9.05 us
    ppermute x3, waiting for transfers between devices, spread(): heres = [lax.ppermute(rows, 'out', [(0, k)]) for k in range(1, n)]  8.37 us
    unnamed x11, local copies, waits for them, and re-layouts  6.57 us
    slice x2, local copies, waits for them, and re-layouts, body(): own[i:j]  4.75 us
  transfers between devices with their start and end apart: 12, of which 5 were waited for; matrix products, arithmetic and copies ran while one was open for 6% of the time, Pallas kernels for 38%

profile of v4, /device:TPU:16, one launch (start us, length us, event | category | flops | bytes accessed | tf_op | source)
XLA Modules:
  0.0 179.4 jit_solution(1496759631312816888)
XLA Ops:
  0.0 1.0 slice.9
  1.0 0.7 collective-permute-start.1
  1.7 1.3 collective-permute-start.2
  3.0 0.7 collective-permute-start.3
  3.7 4.1 %copy.16 = bf16[32,64,512]{2,0,1:T(8,128)(2,1)} copy(bf16[32,64,512]{2,1,0:T(8,128)(2,1)} %param.4) | data formatting | bytes 4194304 | tf_op args[1]
  7.8 1.6 collective-permute-start
  9.4 7.6 %collective-permute-start.8 = (bf16[64,32,512]{2,1,0:T(8,128)(2,1)}, bf16[64,32,512]{2,1,0:T(8,128)(2,1)}, u32[]{:S(2)}, u32[]{:S(2)}) collective-permute-start(bf16[64,32,512]{2,1,0:T(8,128)(2,1)} %bitcast.13.refs_2_.refs_0_), channel_id=1, source_target_pairs={{2,0},{1,3},{6,4},{5,7},{10,8},{9,11},{14,12},{13,15},{18,16},{17,... | collective-permute-start | bytes 6291464 | tf_op jit(solution)/shard_map/ppermute | solution.py:291
  17.0 0.0 collective-permute-done.1
  17.0 8.4 %collective-permute-done.2 = bf16[2,64,1536]{2,1,0:T(8,128)(2,1)S(1)} collective-permute-done((bf16[2,64,1536]{2,1,0:T(8,128)(2,1)S(1)}, bf16[2,64,1536]{2,1,0:T(8,128)(2,1)S(1)}, u32[]{:S(2)}, u32[]{:S(2)}) %collective-permute-start.2) | collective-permute-done | bytes 393248 | tf_op jit(solution)/shard_map/ppermute | solution.py:260
  25.3 0.0 collective-permute-done.3
  25.3 1.1 select_select_fusion.refs_0_
  26.4 1.6 collective-permute-start.4
  28.0 1.5 collective-permute-start.5
  29.5 0.5 collective-permute-start.6
  30.0 8.6 %collective-permute-done.4.refs_1_ = bf16[2,64,1536]{2,1,0:T(8,128)(2,1)S(1)} collective-permute-done((bf16[2,64,1536]{2,1,0:T(8,128)(2,1)S(1)}, bf16[2,64,1536]{2,1,0:T(8,128)(2,1)S(1)}, u32[]{:S(2)}, u32[]{:S(2)}) %collective-permute-start.4) | collective-permute-done | bytes 393248 | tf_op jit(solution)/shard_map/ppermute | solution.py:270
  38.5 6.4 %collective-permute-done.5.refs_2_ = bf16[2,64,1536]{2,1,0:T(8,128)(2,1)S(1)} collective-permute-done((bf16[2,64,1536]{2,1,0:T(8,128)(2,1)S(1)}, bf16[2,64,1536]{2,1,0:T(8,128)(2,1)S(1)}, u32[]{:S(2)}, u32[]{:S(2)}) %collective-permute-start.5) | collective-permute-done | bytes 393248 | tf_op jit(solution)/shard_map/ppermute | solution.py:270
  45.0 0.0 collective-permute-done.6.refs_3_
  45.0 1.2 shard_map.37
  46.2 0.0 collective-permute-start.7
  46.2 0.0 copy-start
  46.2 2.9 %slice.12.refs_2_ = bf16[48,32,512]{2,1,0:T(8,128)(2,1)} slice(bf16[64,32,512]{2,1,0:T(8,128)(2,1)} %bitcast.13.refs_2_.refs_0_), slice={[0:48], [0:32], [0:512]} | slice | bytes 3145728 | tf_op jit(solution)/shard_map/slice | solution.py:313
  49.1 1.9 %slice.13.refs_3_ = bf16[16,32,512]{2,1,0:T(8,128)(2,1)} slice(bf16[64,32,512]{2,1,0:T(8,128)(2,1)} %bitcast.13.refs_2_.refs_0_), slice={[48:64], [0:32], [0:512]} | slice | bytes 1048576 | tf_op jit(solution)/shard_map/slice | solution.py:313
  51.0 0.1 stack.35.refs_0_
  51.0 0.7 dynamic-slice_bitcast_fusion.refs_0_
  51.7 0.0 collective-permute-done.7.refs_2_
  51.7 0.0 copy-start.3
  51.7 1.2 copy-done.3
  52.9 0.0 copy-done
  52.9 4.1 %shard_map.38 = (bf16[2,1536,512]{2,1,0:T(8,128)(2,1)}, f32[8,128]{1,0:T(8,128)S(1)}) custom-call(s32[8]{0:T(128)S(1)} %stack.35.refs_0_, bf16[4,2,64,1536]{3,2,1,0:T(8,128)(2,1)S(1)} %copy-done, bf16[4,2,64,1536]{3,2,1,0:T(8,128)(2,1)} %copy-done.3, f32[8,128]{1,0:T(8,128)S(1)} %get-tuple-element.19.refs_3_), custom_call_target="tpu_custom_call", output_to_operand_aliasing={{1}: (3, {})} | custom-call | flops 1024 | bytes 1024 | tf_op jit(solution)/shard_map/pallas_call | solution.py:34
  57.1 25.9 %shard_map.39 = (bf16[48,2,128,512]{3,2,1,0:T(8,128)(2,1)}, f32[8,128]{1,0:T(8,128)S(1)}) custom-call(bf16[128,64,1536]{2,1,0:T(8,128)(2,1)} %refs_0_.3, bf16[2,1536,512]{2,1,0:T(8,128)(2,1)} %get-tuple-element.20.refs_1_, f32[8,128]{1,0:T(8,128)S(1)} %get-tuple-element.21.refs_2_), custom_call_target="tpu_custom_call", output_to_operand_aliasing={{1}: (2, {})} | custom-call | flops 1024 | bytes 1024 | tf_op jit(solution)/shard_map/pallas_call | solution.py:34
  83.0 0.0 collective-permute-done.refs_1_
  83.0 4.2 %shard_map.40 = (bf16[64,32,512]{2,1,0:T(8,128)(2,1)}, f32[8,128]{1,0:T(8,128)S(1)}) custom-call(s32[1]{0:T(128)} %bitcast.2.refs_0_, bf16[64,32,512]{2,1,0:T(8,128)(2,1)} %collective-permute-done.refs_1_, bf16[64,32,512]{2,1,0:T(8,128)(2,1)} %bitcast.13.refs_2_.refs_0_, f32[8,128]{1,0:T(8,128)S(1)} %get-tuple-element.22.refs_3_), custom_call_target="tpu_custom_call", output_to_operand_aliasing={{1}: (3, {})} | custom-call | flops 1024 | bytes 1024 | tf_op jit(solution)/shard_map/pallas_call | solution.py:34
  87.2 0.0 copy-start.1
  87.2 0.6 copy-done.1
  87.8 0.0 collective-permute-start.9
  87.8 11.6 %collective-permute-done.8.refs_1_ = bf16[64,32,512]{2,1,0:T(8,128)(2,1)} collective-permute-done((bf16[64,32,512]{2,1,0:T(8,128)(2,1)}, bf16[64,32,512]{2,1,0:T(8,128)(2,1)}, u32[]{:S(2)}, u32[]{:S(2)}) %collective-permute-start.8) | collective-permute-done | bytes 2097184 | tf_op jit(solution)/shard_map/ppermute | solution.py:291
  99.4 16.3 %collective-permute-start.10 = (bf16[48,32,512]{2,1,0:T(8,128)(2,1)}, bf16[48,32,512]{2,1,0:T(8,128)(2,1)S(1)}, u32[]{:S(2)}, u32[]{:S(2)}) collective-permute-start(bf16[48,32,512]{2,1,0:T(8,128)(2,1)} %get-tuple-element.29), channel_id=1, source_target_pairs={{2,1},{1,2},{6,5},{5,6},{10,9},{9,10},{14,13},{13,14},{18,17},{17,... | collective-permute-start | bytes 4718600 | tf_op jit(solution)/shard_map/ppermute | solution.py:291
  115.7 0.0 copy-start.2
  115.7 0.7 copy-done.2
  116.4 0.0 copy-start.4
  116.4 11.4 %shard_map.43 = (bf16[16,2,128,512]{3,2,1,0:T(8,128)(2,1)}, f32[8,128]{1,0:T(8,128)S(1)}) custom-call(bf16[128,64,1536]{2,1,0:T(8,128)(2,1)} %refs_0_.3, bf16[2,1536,512]{2,1,0:T(8,128)(2,1)} %get-tuple-element.20.refs_1_, f32[8,128]{1,0:T(8,128)S(1)} %copy-done.2), custom_call_target="tpu_custom_call", output_to_operand_aliasing={{1}: (2, {})} | custom-call | flops 1024 | bytes 1024 | tf_op jit(solution)/shard_map/pallas_call | solution.py:34
  127.8 0.0 copy-done.4
  127.8 1.9 %collective-permute-start.11 = (bf16[16,32,512]{2,1,0:T(8,128)(2,1)S(1)}, bf16[16,32,512]{2,1,0:T(8,128)(2,1)S(1)}, u32[]{:S(2)}, u32[]{:S(2)}) collective-permute-start(bf16[16,32,512]{2,1,0:T(8,128)(2,1)S(1)} %copy-done.4), channel_id=1, source_target_pairs={{2,1},{1,2},{6,5},{5,6},{10,9},{9,10},{14,13},{13,14},{18,17},{17,... | collective-permute-start | bytes 1572872 | tf_op jit(solution)/shard_map/ppermute | solution.py:291
  129.7 3.6 %shard_map.44 = f32[96,256]{1,0:T(8,128)S(1)} custom-call(bf16[64,32,512]{2,1,0:T(8,128)(2,1)} %bitcast.13.refs_2_.refs_0_, bf16[64,32,512]{2,1,0:T(8,128)(2,1)} %collective-permute-done.refs_1_, bf16[64,32,512]{2,1,0:T(8,128)(2,1)} %get-tuple-element.24.refs_2_, bf16[16,2,128,512]{3,2,1,0:T(8,128)(2,1)} %get-tuple-element.27.refs_3_.refs_5_), custom_call_target="tpu_custom_call" | custom-call | flops 1024 | bytes 1024 | tf_op jit(solution)/shard_map/pallas_call | solution.py:34
  133.3 9.0 %shard_map.42 = f32[96,256]{1,0:T(8,128)S(1)} custom-call(bf16[64,32,512]{2,1,0:T(8,128)(2,1)} %bitcast.13.refs_2_.refs_0_, bf16[64,32,512]{2,1,0:T(8,128)(2,1)} %collective-permute-done.refs_1_, bf16[64,32,512]{2,1,0:T(8,128)(2,1)} %get-tuple-element.24.refs_2_, bf16[48,2,128,512]{3,2,1,0:T(8,128)(2,1)} %get-tuple-element.25.refs_3_.refs_2_), custom_call_target="tpu_custom_call" | custom-call | flops 1024 | bytes 1024 | tf_op jit(solution)/shard_map/pallas_call | solution.py:34
  142.4 15.7 %collective-permute-done.9.refs_0_ = bf16[64,32,512]{2,1,0:T(8,128)(2,1)} collective-permute-done((bf16[64,32,512]{2,1,0:T(8,128)(2,1)}, bf16[64,32,512]{2,1,0:T(8,128)(2,1)}, u32[]{:S(2)}, u32[]{:S(2)}) %collective-permute-start.9) | collective-permute-done | bytes 2097184 | tf_op jit(solution)/shard_map/ppermute | solution.py:291
  158.1 0.0 collective-permute-done.10.refs_1_
  158.1 8.3 %shard_map.46.refs_2_ = f32[64,256]{1,0:T(8,128)S(1)} custom-call(bf16[64,32,512]{2,1,0:T(8,128)(2,1)} %shard_map.45.refs_0_.refs_3_, bf16[48,32,512]{2,1,0:T(8,128)(2,1)S(1)} %collective-permute-done.10.refs_1_, bf16[48,2,128,512]{3,2,1,0:T(8,128)(2,1)} %get-tuple-element.25.refs_3_.refs_2_), custom_call_target="tpu_custom_call" | custom-call | flops 1024 | bytes 1024 | tf_op jit(solution)/shard_map/pallas_call | solution.py:34
  166.4 0.0 collective-permute-done.11.refs_4_
  166.4 3.3 %shard_map.47 = f32[8,2,16,128]{3,2,1,0:T(8,128)S(1)} custom-call(s32[4]{0:T(128)S(1)} %dynamic-slice_bitcast_fusion.refs_0_, f32[96,256]{1,0:T(8,128)S(1)} %add.7.refs_1_, f32[64,256]{1,0:T(8,128)S(1)} %shard_map.46.refs_2_, bf16[64,32,512]{2,1,0:T(8,128)(2,1)} %shard_map.45.refs_0_.refs_3_, bf16[16,32,512]{2,1,0:T(8,128)(2,1)S(1)} %collective-permute-done.11.refs_4_, ...), custom_call_target="tpu_custom_call" | custom-call | flops 1024 | bytes 1024 | tf_op jit(solution)/shard_map/pallas_call | solution.py:34
  169.7 9.1 %all_to_all.5 = f32[8,2,16,128]{3,2,1,0:T(8,128)S(1)} all-to-all(f32[8,2,16,128]{3,2,1,0:T(8,128)S(1)} %shard_map.47), channel_id=1, replica_groups=mesh['vir'=8,'out'=4] {'vir'}, dimensions={0} | all-to-all | bytes 262144 | tf_op jit(solution)/shard_map/all_to_all | solution.py:335
  178.7 0.6 reduce_sum.9
  (4 shorter events, 0.0 us)
Async XLA Ops:
  1.0 16.0 %collective-permute-start.1 = (bf16[2,64,1536]{2,1,0:T(8,128)(2,1)S(1)}, bf16[2,64,1536]{2,1,0:T(8,128)(2,1)S(1)}, u32[]{:S(2)}, u32[]{:S(2)}) collective-permute-start(bf16[2,64,1536]{2,1,0:T(8,128)(2,1)S(1)} %slice.9), channel_id=1, source_target_pairs={{0,3},{4,7},{8,11},{12,15},{16,19},{20,23},{24,27},{28,31}} | collective-permute-start | bytes 1179656 | tf_op jit(solution)/shard_map/ppermute | solution.py:260
  1.7 23.6 %collective-permute-start.2 = (bf16[2,64,1536]{2,1,0:T(8,128)(2,1)S(1)}, bf16[2,64,1536]{2,1,0:T(8,128)(2,1)S(1)}, u32[]{:S(2)}, u32[]{:S(2)}) collective-permute-start(bf16[2,64,1536]{2,1,0:T(8,128)(2,1)S(1)} %slice.9), channel_id=1, source_target_pairs={{0,2},{4,6},{8,10},{12,14},{16,18},{20,22},{24,26},{28,30}} | collective-permute-start | bytes 1179656 | tf_op jit(solution)/shard_map/ppermute | solution.py:260
  3.0 22.3 %collective-permute-start.3 = (bf16[2,64,1536]{2,1,0:T(8,128)(2,1)S(1)}, bf16[2,64,1536]{2,1,0:T(8,128)(2,1)S(1)}, u32[]{:S(2)}, u32[]{:S(2)}) collective-permute-start(bf16[2,64,1536]{2,1,0:T(8,128)(2,1)S(1)} %slice.9), channel_id=1, source_target_pairs={{0,1},{4,5},{8,9},{12,13},{16,17},{20,21},{24,25},{28,29}} | collective-permute-start | bytes 1179656 | tf_op jit(solution)/shard_map/ppermute | solution.py:260
  7.8 75.2 %collective-permute-start = (bf16[64,32,512]{2,1,0:T(8,128)(2,1)}, bf16[64,32,512]{2,1,0:T(8,128)(2,1)}, u32[]{:S(2)}, u32[]{:S(2)}) collective-permute-start(bf16[64,32,512]{2,1,0:T(8,128)(2,1)} %bitcast.13.refs_2_.refs_0_), channel_id=1, source_target_pairs={{3,1},{1,0},{0,2},{2,3},{7,5},{5,4},{4,6},{6,7},{11,9},{9,8},{8,10... | collective-permute-start | bytes 6291464 | tf_op jit(solution)/shard_map/ppermute | solution.py:291
  9.4 90.0 %collective-permute-start.8 = (bf16[64,32,512]{2,1,0:T(8,128)(2,1)}, bf16[64,32,512]{2,1,0:T(8,128)(2,1)}, u32[]{:S(2)}, u32[]{:S(2)}) collective-permute-start(bf16[64,32,512]{2,1,0:T(8,128)(2,1)} %bitcast.13.refs_2_.refs_0_), channel_id=1, source_target_pairs={{2,0},{1,3},{6,4},{5,7},{10,8},{9,11},{14,12},{13,15},{18,16},{17,... | collective-permute-start | bytes 6291464 | tf_op jit(solution)/shard_map/ppermute | solution.py:291
  26.4 12.1 %collective-permute-start.4 = (bf16[2,64,1536]{2,1,0:T(8,128)(2,1)S(1)}, bf16[2,64,1536]{2,1,0:T(8,128)(2,1)S(1)}, u32[]{:S(2)}, u32[]{:S(2)}) collective-permute-start(bf16[2,64,1536]{2,1,0:T(8,128)(2,1)S(1)} %select_select_fusion.refs_0_), channel_id=1, source_target_pairs={{0,8},{4,12},{8,0},{12,4},{16,24},{20,28},{24,16},{28,20},{1,9},{5... | collective-permute-start | bytes 1179656 | tf_op jit(solution)/shard_map/ppermute | solution.py:270
  28.0 17.0 %collective-permute-start.5 = (bf16[2,64,1536]{2,1,0:T(8,128)(2,1)S(1)}, bf16[2,64,1536]{2,1,0:T(8,128)(2,1)S(1)}, u32[]{:S(2)}, u32[]{:S(2)}) collective-permute-start(bf16[2,64,1536]{2,1,0:T(8,128)(2,1)S(1)} %select_select_fusion.refs_0_), channel_id=1, source_target_pairs={{0,16},{4,20},{8,24},{12,28},{16,0},{20,4},{24,8},{28,12},{1,17},{... | collective-permute-start | bytes 1179656 | tf_op jit(solution)/shard_map/ppermute | solution.py:270
  29.5 15.5 %collective-permute-start.6 = (bf16[2,64,1536]{2,1,0:T(8,128)(2,1)S(1)}, bf16[2,64,1536]{2,1,0:T(8,128)(2,1)S(1)}, u32[]{:S(2)}, u32[]{:S(2)}) collective-permute-start(bf16[2,64,1536]{2,1,0:T(8,128)(2,1)S(1)} %select_select_fusion.refs_0_), channel_id=1, source_target_pairs={{0,24},{4,28},{8,16},{12,20},{16,8},{20,12},{24,0},{28,4},{1,25},{... | collective-permute-start | bytes 1179656 | tf_op jit(solution)/shard_map/ppermute | solution.py:270
  46.2 5.5 %collective-permute-start.7 = (bf16[4,2,64,1536]{3,2,1,0:T(8,128)(2,1)}, bf16[4,2,64,1536]{3,2,1,0:T(8,128)(2,1)S(1)}, u32[]{:S(2)}, u32[]{:S(2)}) collective-permute-start(bf16[4,2,64,1536]{3,2,1,0:T(8,128)(2,1)} %get-tuple-element.18.refs_1_), channel_id=1, source_target_pairs={{0,4},{4,0},{8,12},{12,8},{16,20},{20,16},{24,28},{28,24},{1,5},{5... | collective-permute-start | bytes 4718600 | tf_op jit(solution)/shard_map/ppermute | solution.py:270
  46.2 6.7 %copy-start = (bf16[4,2,64,1536]{3,2,1,0:T(8,128)(2,1)S(1)}, bf16[4,2,64,1536]{3,2,1,0:T(8,128)(2,1)}, u32[]{:S(2)}) copy-start(bf16[4,2,64,1536]{3,2,1,0:T(8,128)(2,1)} %get-tuple-element.18.refs_1_) | copy-start | bytes 4718596
  51.7 1.2 copy-start.3
  87.2 0.6 copy-start.1
  87.8 70.3 %collective-permute-start.9 = (bf16[64,32,512]{2,1,0:T(8,128)(2,1)}, bf16[64,32,512]{2,1,0:T(8,128)(2,1)}, u32[]{:S(2)}, u32[]{:S(2)}) collective-permute-start(bf16[64,32,512]{2,1,0:T(8,128)(2,1)} %get-tuple-element.28), channel_id=1, source_target_pairs={{1,0},{0,1},{2,3},{3,2},{5,4},{4,5},{6,7},{7,6},{9,8},{8,9},{10,11... | collective-permute-start | bytes 6291464 | tf_op jit(solution)/shard_map/ppermute | solution.py:291
  99.4 58.7 %collective-permute-start.10 = (bf16[48,32,512]{2,1,0:T(8,128)(2,1)}, bf16[48,32,512]{2,1,0:T(8,128)(2,1)S(1)}, u32[]{:S(2)}, u32[]{:S(2)}) collective-permute-start(bf16[48,32,512]{2,1,0:T(8,128)(2,1)} %get-tuple-element.29), channel_id=1, source_target_pairs={{2,1},{1,2},{6,5},{5,6},{10,9},{9,10},{14,13},{13,14},{18,17},{17,... | collective-permute-start | bytes 4718600 | tf_op jit(solution)/shard_map/ppermute | solution.py:291
  115.7 0.7 copy-start.2
  116.4 11.4 %copy-start.4 = (bf16[16,32,512]{2,1,0:T(8,128)(2,1)S(1)}, bf16[16,32,512]{2,1,0:T(8,128)(2,1)}, u32[]{:S(2)}) copy-start(bf16[16,32,512]{2,1,0:T(8,128)(2,1)} %get-tuple-element.30) | copy-start | bytes 1572868
  127.8 38.6 %collective-permute-start.11 = (bf16[16,32,512]{2,1,0:T(8,128)(2,1)S(1)}, bf16[16,32,512]{2,1,0:T(8,128)(2,1)S(1)}, u32[]{:S(2)}, u32[]{:S(2)}) collective-permute-start(bf16[16,32,512]{2,1,0:T(8,128)(2,1)S(1)} %copy-done.4), channel_id=1, source_target_pairs={{2,1},{1,2},{6,5},{5,6},{10,9},{9,10},{14,13},{13,14},{18,17},{17,... | collective-permute-start | bytes 1572872 | tf_op jit(solution)/shard_map/ppermute | solution.py:291

commit v5 on v4

--- a/solution.py
+++ b/solution.py
@@ -12,7 +12,6 @@
 NT = (((1,), (1,)), ((), ()))
 NN = (((1,), (0,)), ((), ()))
 LITTLE = pl.CostEstimate(flops=1024, bytes_accessed=1024, transcendentals=0)
-MORE = pl.CostEstimate(flops=24 * 10**9, bytes_accessed=48 * 10**6, transcendentals=0)
 MUCH = pl.CostEstimate(flops=2 * 10**10, bytes_accessed=4 * 10**7, transcendentals=0)
 
 
@@ -308,12 +307,16 @@
         inside = (z == 1) | (z == 2)
         second = send(own, (2, 0), (1, 3))
         first = send(own, (3, 1), (1, 0), (0, 2), (2, 3))
-        onward, [token] = pick(inside, first, own, 0, c_rows, [token])
-        sides = send(onward, (1, 0), (0, 1), (2, 3), (3, 2))
-        token, second, *kept = fence([token, second] + [own[i:j] for i, j in spans], MORE)
-        [sides] = fence([sides], MUCH)
+        onward = []
+        for span in spans:
+            part, [token] = pick(inside, first, own, *span, [token])
+            onward.append(part)
+        sides = [send(t, (1, 0), (0, 1), (2, 3), (3, 2)) for t in onward]
+        token, second, *kept = fence([token, second] + [own[i:j] for i, j in spans], MUCH)
+        middle = [send(t, (2, 1), (1, 2)) for t in kept]
+        [sides[0]] = fence(sides[:1], MUCH)
+        late = [[(t, 0) for t in pair] for pair in zip(sides, middle)]
         early = [own, first, second]
-        late = [[(sides, i), (send(t, (2, 1), (1, 2)), 0)] for (i, _), t in zip(spans, kept)]
         slots = jnp.array([[0, 1, 2, 3], [3, 0, 4, 1], [1, 4, 0, 3], [3, 2, 1, 0]], jnp.int32)[z]
     else:
         gathered = lax.all_gather(own, "out")

time: 181 us -> 177 us (0.978)
  waiting for transfers between devices: 50.7 us -> 42 us
  local copies, waits for them, and re-layouts: 13.1 us -> 15.6 us
    ppermute x5 -> x6, waiting for transfers between devices: 27.3 us -> 18.6 us  [send(): return lax.ppermute(array, 'out', ways)]
    unnamed x11 -> x13, local copies, waits for them, and re-layouts: 6.57 us -> 9.1 us
    ppermute x5 -> x6, starting transfers between devices: 27.4 us -> 28.1 us  [send(): return lax.ppermute(array, 'out', ways)]
    pallas_call x9 -> x10, Pallas kernels: 71.1 us -> 71.7 us  [call(): pl.pallas_call(run, grid=grid, in_specs=list(in_specs) + [anywhere] * n_t...]
  transfers between devices with their start and end apart: 12 -> 13, of which waited for: 5 -> 7; matrix products, arithmetic and copies ran while one was open for 6% -> 6% of each run, Pallas kernels for 38% -> 39%
where the time goes in v5:
time: 177 us; the launch traced here: 175 us
  Pallas kernels  71.7 us (41%)
  waiting for transfers between devices  42 us (24%)
  starting transfers between devices  34.3 us (19%)
  local copies, waits for them, and re-layouts  15.6 us (9%)
  blocking collectives  9.06 us (5%)
    pallas_call x10, Pallas kernels, call(): pl.pallas_call(run, grid=grid, in_specs=list(in_specs) + [anywhere] * n_t...  71.7 us
    ppermute x6, starting transfers between devices, send(): return lax.ppermute(array, 'out', ways)  28.1 us
    ppermute x6, waiting for transfers between devices, send(): return lax.ppermute(array, 'out', ways)  18.6 us
    ppermute x4, waiting for transfers between devices, swap(): return lax.ppermute(array, 'vir', [(k, k ^ mask) for k in range(vir)])  15 us
    unnamed x13, local copies, waits for them, and re-layouts  9.1 us
    all_to_all x1, blocking collectives, body(): swapped = lax.all_to_all(parts, 'vir', split_axis=0, concat_axis=0)  9.06 us
    ppermute x3, waiting for transfers between devices, spread(): heres = [lax.ppermute(rows, 'out', [(0, k)]) for k in range(1, n)]  8.38 us
    slice x2, local copies, waits for them, and re-layouts, body(): own[i:j]  4.74 us
  transfers between devices with their start and end apart: 13, of which 7 were waited for; matrix products, arithmetic and copies ran while one was open for 6% of the time, Pallas kernels for 39%

profile of v5, /device:TPU:16, one launch (start us, length us, event | category | flops | bytes accessed | tf_op | source)
XLA Modules:
  0.0 174.5 jit_solution(284685982302783130)
XLA Ops:
  0.0 1.0 slice.9
  1.0 0.7 collective-permute-start.1
  1.7 1.3 collective-permute-start.2
  3.0 0.7 collective-permute-start.3
  3.7 4.1 %copy.17 = bf16[32,64,512]{2,0,1:T(8,128)(2,1)} copy(bf16[32,64,512]{2,1,0:T(8,128)(2,1)} %param.4) | data formatting | bytes 4194304 | tf_op args[1]
  7.8 1.6 collective-permute-start
  9.4 7.6 %collective-permute-start.8 = (bf16[64,32,512]{2,1,0:T(8,128)(2,1)}, bf16[64,32,512]{2,1,0:T(8,128)(2,1)}, u32[]{:S(2)}, u32[]{:S(2)}) collective-permute-start(bf16[64,32,512]{2,1,0:T(8,128)(2,1)} %bitcast.13.refs_2_.refs_0_), channel_id=1, source_target_pairs={{2,0},{1,3},{6,4},{5,7},{10,8},{9,11},{14,12},{13,15},{18,16},{17,... | collective-permute-start | bytes 6291464 | tf_op jit(solution)/shard_map/ppermute | solution.py:290
  17.0 0.0 collective-permute-done.1
  17.0 8.4 %collective-permute-done.2 = bf16[2,64,1536]{2,1,0:T(8,128)(2,1)S(1)} collective-permute-done((bf16[2,64,1536]{2,1,0:T(8,128)(2,1)S(1)}, bf16[2,64,1536]{2,1,0:T(8,128)(2,1)S(1)}, u32[]{:S(2)}, u32[]{:S(2)}) %collective-permute-start.2) | collective-permute-done | bytes 393248 | tf_op jit(solution)/shard_map/ppermute | solution.py:259
  25.3 0.0 collective-permute-done.3
  25.3 1.1 select_select_fusion.refs_0_
  26.4 1.6 collective-permute-start.4
  28.0 1.5 collective-permute-start.5
  29.5 0.5 collective-permute-start.6
  30.0 8.6 %collective-permute-done.4.refs_1_ = bf16[2,64,1536]{2,1,0:T(8,128)(2,1)S(1)} collective-permute-done((bf16[2,64,1536]{2,1,0:T(8,128)(2,1)S(1)}, bf16[2,64,1536]{2,1,0:T(8,128)(2,1)S(1)}, u32[]{:S(2)}, u32[]{:S(2)}) %collective-permute-start.4) | collective-permute-done | bytes 393248 | tf_op jit(solution)/shard_map/ppermute | solution.py:269
  38.5 6.4 %collective-permute-done.5.refs_2_ = bf16[2,64,1536]{2,1,0:T(8,128)(2,1)S(1)} collective-permute-done((bf16[2,64,1536]{2,1,0:T(8,128)(2,1)S(1)}, bf16[2,64,1536]{2,1,0:T(8,128)(2,1)S(1)}, u32[]{:S(2)}, u32[]{:S(2)}) %collective-permute-start.5) | collective-permute-done | bytes 393248 | tf_op jit(solution)/shard_map/ppermute | solution.py:269
  45.0 0.0 collective-permute-done.6.refs_3_
  45.0 1.3 shard_map.37
  46.2 0.0 collective-permute-start.7
  46.2 0.0 copy-start
  46.2 2.8 %slice.12.refs_2_ = bf16[48,32,512]{2,1,0:T(8,128)(2,1)} slice(bf16[64,32,512]{2,1,0:T(8,128)(2,1)} %bitcast.13.refs_2_.refs_0_), slice={[0:48], [0:32], [0:512]} | slice | bytes 3145728 | tf_op jit(solution)/shard_map/slice | solution.py:315
  49.1 1.9 %slice.13.refs_3_ = bf16[16,32,512]{2,1,0:T(8,128)(2,1)} slice(bf16[64,32,512]{2,1,0:T(8,128)(2,1)} %bitcast.13.refs_2_.refs_0_), slice={[48:64], [0:32], [0:512]} | slice | bytes 1048576 | tf_op jit(solution)/shard_map/slice | solution.py:315
  51.0 0.1 stack.35.refs_0_
  51.1 0.7 dynamic-slice_bitcast_fusion.refs_0_
  51.7 0.0 collective-permute-done.7.refs_2_
  51.8 0.0 copy-start.5
  51.8 1.1 copy-done.5
  52.9 0.0 copy-done
  52.9 4.1 %shard_map.38 = (bf16[2,1536,512]{2,1,0:T(8,128)(2,1)}, f32[8,128]{1,0:T(8,128)S(1)}) custom-call(s32[8]{0:T(128)S(1)} %stack.35.refs_0_, bf16[4,2,64,1536]{3,2,1,0:T(8,128)(2,1)S(1)} %copy-done, bf16[4,2,64,1536]{3,2,1,0:T(8,128)(2,1)} %copy-done.5, f32[8,128]{1,0:T(8,128)S(1)} %get-tuple-element.21.refs_3_), custom_call_target="tpu_custom_call", output_to_operand_aliasing={{1}: (3, {})} | custom-call | flops 1024 | bytes 1024 | tf_op jit(solution)/shard_map/pallas_call | solution.py:33
  57.0 25.9 %shard_map.39 = (bf16[48,2,128,512]{3,2,1,0:T(8,128)(2,1)}, f32[8,128]{1,0:T(8,128)S(1)}) custom-call(bf16[128,64,1536]{2,1,0:T(8,128)(2,1)} %refs_0_.3, bf16[2,1536,512]{2,1,0:T(8,128)(2,1)} %get-tuple-element.22.refs_1_, f32[8,128]{1,0:T(8,128)S(1)} %get-tuple-element.23.refs_2_), custom_call_target="tpu_custom_call", output_to_operand_aliasing={{1}: (2, {})} | custom-call | flops 1024 | bytes 1024 | tf_op jit(solution)/shard_map/pallas_call | solution.py:33
  82.9 0.0 collective-permute-done.refs_1_
  82.9 3.8 %shard_map.40 = (bf16[48,32,512]{2,1,0:T(8,128)(2,1)}, f32[8,128]{1,0:T(8,128)S(1)}) custom-call(s32[1]{0:T(128)} %bitcast.2.refs_0_, bf16[64,32,512]{2,1,0:T(8,128)(2,1)} %collective-permute-done.refs_1_, bf16[64,32,512]{2,1,0:T(8,128)(2,1)} %bitcast.13.refs_2_.refs_0_, f32[8,128]{1,0:T(8,128)S(1)} %get-tuple-element.24.refs_3_), custom_call_target="tpu_custom_call", output_to_operand_aliasing={{1}: (3, {})} | custom-call | flops 1024 | bytes 1024 | tf_op jit(solution)/shard_map/pallas_call | solution.py:33
  86.7 0.0 collective-permute-start.9
  86.7 1.2 shard_map.41
  88.0 0.0 copy-start.3
  88.0 0.6 copy-done.3
  88.5 10.8 %collective-permute-done.8.refs_1_ = bf16[64,32,512]{2,1,0:T(8,128)(2,1)} collective-permute-done((bf16[64,32,512]{2,1,0:T(8,128)(2,1)}, bf16[64,32,512]{2,1,0:T(8,128)(2,1)}, u32[]{:S(2)}, u32[]{:S(2)}) %collective-permute-start.8) | collective-permute-done | bytes 2097184 | tf_op jit(solution)/shard_map/ppermute | solution.py:290
  99.4 16.3 %collective-permute-start.10 = (bf16[48,32,512]{2,1,0:T(8,128)(2,1)}, bf16[48,32,512]{2,1,0:T(8,128)(2,1)}, u32[]{:S(2)}, u32[]{:S(2)}) collective-permute-start(bf16[48,32,512]{2,1,0:T(8,128)(2,1)} %get-tuple-element.32), channel_id=1, source_target_pairs={{2,1},{1,2},{6,5},{5,6},{10,9},{9,10},{14,13},{13,14},{18,17},{17,... | collective-permute-start | bytes 4718600 | tf_op jit(solution)/shard_map/ppermute | solution.py:290
  115.7 0.0 copy-start.4
  115.7 0.7 copy-done.4
  116.4 11.4 %shard_map.44 = (bf16[16,2,128,512]{3,2,1,0:T(8,128)(2,1)}, f32[8,128]{1,0:T(8,128)S(1)}) custom-call(bf16[128,64,1536]{2,1,0:T(8,128)(2,1)} %refs_0_.3, bf16[2,1536,512]{2,1,0:T(8,128)(2,1)} %get-tuple-element.22.refs_1_, f32[8,128]{1,0:T(8,128)S(1)} %copy-done.4), custom_call_target="tpu_custom_call", output_to_operand_aliasing={{1}: (2, {})} | custom-call | flops 1024 | bytes 1024 | tf_op jit(solution)/shard_map/pallas_call | solution.py:33
  127.8 1.9 %collective-permute-start.12 = (bf16[16,32,512]{2,1,0:T(8,128)(2,1)}, bf16[16,32,512]{2,1,0:T(8,128)(2,1)S(1)}, u32[]{:S(2)}, u32[]{:S(2)}) collective-permute-start(bf16[16,32,512]{2,1,0:T(8,128)(2,1)} %get-tuple-element.34), channel_id=1, source_target_pairs={{2,1},{1,2},{6,5},{5,6},{10,9},{9,10},{14,13},{13,14},{18,17},{17,... | collective-permute-start | bytes 1572872 | tf_op jit(solution)/shard_map/ppermute | solution.py:290
  129.7 0.7 collective-permute-start.11
  130.4 3.5 %shard_map.45 = f32[96,256]{1,0:T(8,128)S(1)} custom-call(bf16[64,32,512]{2,1,0:T(8,128)(2,1)} %bitcast.13.refs_2_.refs_0_, bf16[64,32,512]{2,1,0:T(8,128)(2,1)} %collective-permute-done.refs_1_, bf16[64,32,512]{2,1,0:T(8,128)(2,1)} %get-tuple-element.27.refs_2_, bf16[16,2,128,512]{3,2,1,0:T(8,128)(2,1)} %get-tuple-element.30.refs_3_.refs_5_), custom_call_target="tpu_custom_call" | custom-call | flops 1024 | bytes 1024 | tf_op jit(solution)/shard_map/pallas_call | solution.py:33
  134.0 9.0 %shard_map.43 = f32[96,256]{1,0:T(8,128)S(1)} custom-call(bf16[64,32,512]{2,1,0:T(8,128)(2,1)} %bitcast.13.refs_2_.refs_0_, bf16[64,32,512]{2,1,0:T(8,128)(2,1)} %collective-permute-done.refs_1_, bf16[64,32,512]{2,1,0:T(8,128)(2,1)} %get-tuple-element.27.refs_2_, bf16[48,2,128,512]{3,2,1,0:T(8,128)(2,1)} %get-tuple-element.28.refs_3_.refs_2_), custom_call_target="tpu_custom_call" | custom-call | flops 1024 | bytes 1024 | tf_op jit(solution)/shard_map/pallas_call | solution.py:33
  143.1 3.8 %collective-permute-done.9.refs_0_ = bf16[48,32,512]{2,1,0:T(8,128)(2,1)S(1)} collective-permute-done((bf16[48,32,512]{2,1,0:T(8,128)(2,1)}, bf16[48,32,512]{2,1,0:T(8,128)(2,1)S(1)}, u32[]{:S(2)}, u32[]{:S(2)}) %collective-permute-start.9) | collective-permute-done | bytes 1572896 | tf_op jit(solution)/shard_map/ppermute | solution.py:290
  146.9 0.0 copy-start.1
  146.9 1.2 copy-done.1
  148.1 3.1 %collective-permute-done.10.refs_1_ = bf16[48,32,512]{2,1,0:T(8,128)(2,1)} collective-permute-done((bf16[48,32,512]{2,1,0:T(8,128)(2,1)}, bf16[48,32,512]{2,1,0:T(8,128)(2,1)}, u32[]{:S(2)}, u32[]{:S(2)}) %collective-permute-start.10) | collective-permute-done | bytes 1572896 | tf_op jit(solution)/shard_map/ppermute | solution.py:290
  151.2 0.0 copy-start.2
  151.2 1.4 copy-done.2
  152.6 8.3 %shard_map.47.refs_2_ = f32[64,256]{1,0:T(8,128)S(1)} custom-call(bf16[48,32,512]{2,1,0:T(8,128)(2,1)S(1)} %copy-done.2, bf16[48,32,512]{2,1,0:T(8,128)(2,1)} %collective-permute-done.10.refs_1_, bf16[48,2,128,512]{3,2,1,0:T(8,128)(2,1)} %get-tuple-element.28.refs_3_.refs_2_), custom_call_target="tpu_custom_call" | custom-call | flops 1024 | bytes 1024 | tf_op jit(solution)/shard_map/pallas_call | solution.py:33
  160.9 0.8 collective-permute-done.12.refs_4_
  161.7 0.0 collective-permute-done.11.refs_3_
  161.7 3.1 %shard_map.48 = f32[8,2,16,128]{3,2,1,0:T(8,128)S(1)} custom-call(s32[4]{0:T(128)S(1)} %dynamic-slice_bitcast_fusion.refs_0_, f32[96,256]{1,0:T(8,128)S(1)} %add.7.refs_1_, f32[64,256]{1,0:T(8,128)S(1)} %shard_map.47.refs_2_, bf16[16,32,512]{2,1,0:T(8,128)(2,1)S(1)} %collective-permute-done.11.refs_3_, ...), custom_call_target="tpu_custom_call" | custom-call | flops 1024 | bytes 1024 | tf_op jit(solution)/shard_map/pallas_call | solution.py:33
  164.8 9.1 %all_to_all.5 = f32[8,2,16,128]{3,2,1,0:T(8,128)S(1)} all-to-all(f32[8,2,16,128]{3,2,1,0:T(8,128)S(1)} %shard_map.48), channel_id=1, replica_groups=mesh['vir'=8,'out'=4] {'vir'}, dimensions={0} | all-to-all | bytes 262144 | tf_op jit(solution)/shard_map/all_to_all | solution.py:338
  173.9 0.6 reduce_sum.9
  (4 shorter events, 0.0 us)
Async XLA Ops:
  1.0 15.9 %collective-permute-start.1 = (bf16[2,64,1536]{2,1,0:T(8,128)(2,1)S(1)}, bf16[2,64,1536]{2,1,0:T(8,128)(2,1)S(1)}, u32[]{:S(2)}, u32[]{:S(2)}) collective-permute-start(bf16[2,64,1536]{2,1,0:T(8,128)(2,1)S(1)} %slice.9), channel_id=1, source_target_pairs={{0,3},{4,7},{8,11},{12,15},{16,19},{20,23},{24,27},{28,31}} | collective-permute-start | bytes 1179656 | tf_op jit(solution)/shard_map/ppermute | solution.py:259
  1.7 23.6 %collective-permute-start.2 = (bf16[2,64,1536]{2,1,0:T(8,128)(2,1)S(1)}, bf16[2,64,1536]{2,1,0:T(8,128)(2,1)S(1)}, u32[]{:S(2)}, u32[]{:S(2)}) collective-permute-start(bf16[2,64,1536]{2,1,0:T(8,128)(2,1)S(1)} %slice.9), channel_id=1, source_target_pairs={{0,2},{4,6},{8,10},{12,14},{16,18},{20,22},{24,26},{28,30}} | collective-permute-start | bytes 1179656 | tf_op jit(solution)/shard_map/ppermute | solution.py:259
  3.0 22.3 %collective-permute-start.3 = (bf16[2,64,1536]{2,1,0:T(8,128)(2,1)S(1)}, bf16[2,64,1536]{2,1,0:T(8,128)(2,1)S(1)}, u32[]{:S(2)}, u32[]{:S(2)}) collective-permute-start(bf16[2,64,1536]{2,1,0:T(8,128)(2,1)S(1)} %slice.9), channel_id=1, source_target_pairs={{0,1},{4,5},{8,9},{12,13},{16,17},{20,21},{24,25},{28,29}} | collective-permute-start | bytes 1179656 | tf_op jit(solution)/shard_map/ppermute | solution.py:259
  7.8 75.1 %collective-permute-start = (bf16[64,32,512]{2,1,0:T(8,128)(2,1)}, bf16[64,32,512]{2,1,0:T(8,128)(2,1)}, u32[]{:S(2)}, u32[]{:S(2)}) collective-permute-start(bf16[64,32,512]{2,1,0:T(8,128)(2,1)} %bitcast.13.refs_2_.refs_0_), channel_id=1, source_target_pairs={{3,1},{1,0},{0,2},{2,3},{7,5},{5,4},{4,6},{6,7},{11,9},{9,8},{8,10... | collective-permute-start | bytes 6291464 | tf_op jit(solution)/shard_map/ppermute | solution.py:290
  9.4 90.0 %collective-permute-start.8 = (bf16[64,32,512]{2,1,0:T(8,128)(2,1)}, bf16[64,32,512]{2,1,0:T(8,128)(2,1)}, u32[]{:S(2)}, u32[]{:S(2)}) collective-permute-start(bf16[64,32,512]{2,1,0:T(8,128)(2,1)} %bitcast.13.refs_2_.refs_0_), channel_id=1, source_target_pairs={{2,0},{1,3},{6,4},{5,7},{10,8},{9,11},{14,12},{13,15},{18,16},{17,... | collective-permute-start | bytes 6291464 | tf_op jit(solution)/shard_map/ppermute | solution.py:290
  26.4 12.1 %collective-permute-start.4 = (bf16[2,64,1536]{2,1,0:T(8,128)(2,1)S(1)}, bf16[2,64,1536]{2,1,0:T(8,128)(2,1)S(1)}, u32[]{:S(2)}, u32[]{:S(2)}) collective-permute-start(bf16[2,64,1536]{2,1,0:T(8,128)(2,1)S(1)} %select_select_fusion.refs_0_), channel_id=1, source_target_pairs={{0,8},{4,12},{8,0},{12,4},{16,24},{20,28},{24,16},{28,20},{1,9},{5... | collective-permute-start | bytes 1179656 | tf_op jit(solution)/shard_map/ppermute | solution.py:269
  28.0 17.0 %collective-permute-start.5 = (bf16[2,64,1536]{2,1,0:T(8,128)(2,1)S(1)}, bf16[2,64,1536]{2,1,0:T(8,128)(2,1)S(1)}, u32[]{:S(2)}, u32[]{:S(2)}) collective-permute-start(bf16[2,64,1536]{2,1,0:T(8,128)(2,1)S(1)} %select_select_fusion.refs_0_), channel_id=1, source_target_pairs={{0,16},{4,20},{8,24},{12,28},{16,0},{20,4},{24,8},{28,12},{1,17},{... | collective-permute-start | bytes 1179656 | tf_op jit(solution)/shard_map/ppermute | solution.py:269
  29.5 15.5 %collective-permute-start.6 = (bf16[2,64,1536]{2,1,0:T(8,128)(2,1)S(1)}, bf16[2,64,1536]{2,1,0:T(8,128)(2,1)S(1)}, u32[]{:S(2)}, u32[]{:S(2)}) collective-permute-start(bf16[2,64,1536]{2,1,0:T(8,128)(2,1)S(1)} %select_select_fusion.refs_0_), channel_id=1, source_target_pairs={{0,24},{4,28},{8,16},{12,20},{16,8},{20,12},{24,0},{28,4},{1,25},{... | collective-permute-start | bytes 1179656 | tf_op jit(solution)/shard_map/ppermute | solution.py:269
  46.2 5.5 %collective-permute-start.7 = (bf16[4,2,64,1536]{3,2,1,0:T(8,128)(2,1)}, bf16[4,2,64,1536]{3,2,1,0:T(8,128)(2,1)S(1)}, u32[]{:S(2)}, u32[]{:S(2)}) collective-permute-start(bf16[4,2,64,1536]{3,2,1,0:T(8,128)(2,1)} %get-tuple-element.20.refs_1_), channel_id=1, source_target_pairs={{0,4},{4,0},{8,12},{12,8},{16,20},{20,16},{24,28},{28,24},{1,5},{5... | collective-permute-start | bytes 4718600 | tf_op jit(solution)/shard_map/ppermute | solution.py:269
  46.2 6.7 %copy-start = (bf16[4,2,64,1536]{3,2,1,0:T(8,128)(2,1)S(1)}, bf16[4,2,64,1536]{3,2,1,0:T(8,128)(2,1)}, u32[]{:S(2)}) copy-start(bf16[4,2,64,1536]{3,2,1,0:T(8,128)(2,1)} %get-tuple-element.20.refs_1_) | copy-start | bytes 4718596
  51.8 1.1 copy-start.5
  86.7 60.2 %collective-permute-start.9 = (bf16[48,32,512]{2,1,0:T(8,128)(2,1)}, bf16[48,32,512]{2,1,0:T(8,128)(2,1)S(1)}, u32[]{:S(2)}, u32[]{:S(2)}) collective-permute-start(bf16[48,32,512]{2,1,0:T(8,128)(2,1)} %get-tuple-element.31), channel_id=1, source_target_pairs={{1,0},{0,1},{2,3},{3,2},{5,4},{4,5},{6,7},{7,6},{9,8},{8,9},{10,11... | collective-permute-start | bytes 4718600 | tf_op jit(solution)/shard_map/ppermute | solution.py:290
  88.0 0.6 copy-start.3
  99.4 51.8 %collective-permute-start.10 = (bf16[48,32,512]{2,1,0:T(8,128)(2,1)}, bf16[48,32,512]{2,1,0:T(8,128)(2,1)}, u32[]{:S(2)}, u32[]{:S(2)}) collective-permute-start(bf16[48,32,512]{2,1,0:T(8,128)(2,1)} %get-tuple-element.32), channel_id=1, source_target_pairs={{2,1},{1,2},{6,5},{5,6},{10,9},{9,10},{14,13},{13,14},{18,17},{17,... | collective-permute-start | bytes 4718600 | tf_op jit(solution)/shard_map/ppermute | solution.py:290
  115.7 0.7 copy-start.4
  127.8 33.9 %collective-permute-start.12 = (bf16[16,32,512]{2,1,0:T(8,128)(2,1)}, bf16[16,32,512]{2,1,0:T(8,128)(2,1)S(1)}, u32[]{:S(2)}, u32[]{:S(2)}) collective-permute-start(bf16[16,32,512]{2,1,0:T(8,128)(2,1)} %get-tuple-element.34), channel_id=1, source_target_pairs={{2,1},{1,2},{6,5},{5,6},{10,9},{9,10},{14,13},{13,14},{18,17},{17,... | collective-permute-start | bytes 1572872 | tf_op jit(solution)/shard_map/ppermute | solution.py:290
  129.7 32.0 %collective-permute-start.11 = (bf16[16,32,512]{2,1,0:T(8,128)(2,1)S(1)}, bf16[16,32,512]{2,1,0:T(8,128)(2,1)S(1)}, u32[]{:S(2)}, u32[]{:S(2)}) collective-permute-start(bf16[16,32,512]{2,1,0:T(8,128)(2,1)S(1)} %get-tuple-element.33), channel_id=1, source_target_pairs={{1,0},{0,1},{2,3},{3,2},{5,4},{4,5},{6,7},{7,6},{9,8},{8,9},{10,11... | collective-permute-start | bytes 1572872 | tf_op jit(solution)/shard_map/ppermute | solution.py:290
  146.9 1.2 copy-start.1
  151.2 1.4 copy-start.2

commit v6 on v5

--- a/solution.py
+++ b/solution.py
@@ -152,14 +152,14 @@
     )
 
 
-def sums(tau_of, integral_ref, total_ref):
-    c_len, bb, a_rows, d_len = integral_ref.shape
+def sums(tau_of, integral_refs, total_ref):
+    c_len = integral_refs[0].shape[0]
 
     @pl.when(pl.program_id(0) == 0)
     def _():
         total_ref[...] = jnp.zeros_like(total_ref)
 
-    left = [integral_ref[c].reshape(bb * a_rows, d_len) for c in range(c_len)]
+    left = [jnp.concatenate([r[c, 0] for r in integral_refs], axis=0) for c in range(c_len)]
     right = [tau_of(c) for c in range(c_len)]
     total_ref[...] += lax.dot_general(
         jnp.concatenate(left, axis=1),
@@ -170,10 +170,10 @@
 
 
 def early_kernel(count, *refs):
-    tau_refs, (integral_ref, out_ref, total_ref) = refs[:count], refs[count:]
+    tau_refs, integral_refs, (out_ref, total_ref) = refs[:count], refs[count:-2], refs[-2:]
     sums(
         lambda c: jnp.concatenate([r[c] for r in tau_refs], axis=0),
-        integral_ref,
+        integral_refs,
         total_ref,
     )
 
@@ -184,11 +184,12 @@
 
 def late_kernel(count, *refs):
     (slot_ref, early_ref, added_ref), refs = refs[:3], refs[3:]
-    tau_refs, (integral_ref, out_ref, total_ref, all_ref) = refs[:count], refs[count:]
+    tau_refs, integral_refs = refs[:count], refs[count:-3]
+    out_ref, total_ref, all_ref = refs[-3:]
     pairs = tau_refs[0].shape[1]
     sums(
         lambda c: jnp.concatenate([r[c] for r in tau_refs], axis=0),
-        integral_ref,
+        integral_refs,
         total_ref,
     )
 
@@ -213,7 +214,8 @@
         pl.BlockSpec((c_len, pairs, d_len), lambda i, k=start // c_len: (k + i, 0, 0))
         for _, start in taus
     ]
-    specs.append(pl.BlockSpec((c_len, bb, a_rows, d_len), lambda i: (i, 0, 0, 0)))
+    for b in range(bb):
+        specs.append(pl.BlockSpec((c_len, 1, a_rows, d_len), lambda i, b=b: (i, b, 0, 0)))
     return specs, (bb * a_rows, len(taus) * pairs), (c_rows // c_len,)
 
 
@@ -221,14 +223,14 @@
     specs, shape, grid = ladder_specs(taus, integral)
     return call(
         functools.partial(early_kernel, len(taus)),
-        [t for t, _ in taus] + [integral],
+        [t for t, _ in taus] + [integral] * integral.shape[1],
         specs,
         jax.ShapeDtypeStruct(shape[::-1], jnp.float32),
         pl.BlockSpec(shape[::-1], lambda i: (0, 0)),
         [],
         grid=grid,
         scratch=[pltpu.VMEM(shape, jnp.float32)],
-        vmem=52,
+        vmem=60,
     )[0]
 
 
@@ -239,7 +241,7 @@
     out = (owners, bb, slots.shape[0] * pairs // owners, a_rows)
     return call(
         functools.partial(late_kernel, len(taus)),
-        [slots, early, added] + [t for t, _ in taus] + [integral],
+        [slots, early, added] + [t for t, _ in taus] + [integral] * integral.shape[1],
         [pl.BlockSpec(memory_space=pltpu.SMEM)]
         + [pl.BlockSpec(t.shape, lambda i: (0, 0)) for t in (early, added)]
         + specs,
@@ -251,13 +253,13 @@
             pltpu.VMEM(shape, jnp.float32),
             pltpu.VMEM((early.shape[0] + shape[1], shape[0]), jnp.float32),
         ],
-        vmem=52,
+        vmem=60,
     )[0]
 
 
 def spread(rows, n, z):
-    heres = [lax.ppermute(rows, "out", [(0, k)]) for k in range(1, n)]
-    for k, here in zip(range(1, n), heres):
+    heres = [lax.ppermute(rows, "out", [(0, k)]) for k in range(n - 1, 0, -1)]
+    for k, here in zip(range(n - 1, 0, -1), heres):
         rows = jnp.where(z == k, here, rows)
     return rows
 
@@ -305,8 +307,8 @@
     make()
     if n == 4:
         inside = (z == 1) | (z == 2)
-        second = send(own, (2, 0), (1, 3))
-        first = send(own, (3, 1), (1, 0), (0, 2), (2, 3))
+        second = send(amplitudes, (2, 0), (1, 3))
+        first = send(amplitudes, (3, 1), (1, 0), (0, 2), (2, 3)).transpose(1, 0, 2)
         onward = []
         for span in spans:
             part, [token] = pick(inside, first, own, *span, [token])
@@ -316,7 +318,7 @@
         middle = [send(t, (2, 1), (1, 2)) for t in kept]
         [sides[0]] = fence(sides[:1], MUCH)
         late = [[(t, 0) for t in pair] for pair in zip(sides, middle)]
-        early = [own, first, second]
+        early = [own, first, second.transpose(1, 0, 2)]
         slots = jnp.array([[0, 1, 2, 3], [3, 0, 4, 1], [1, 4, 0, 3], [3, 2, 1, 0]], jnp.int32)[z]
     else:
         gathered = lax.all_gather(own, "out")

time: 177 us -> 181 us (1.023)
  waiting for transfers between devices: 42 us -> 28.7 us
  starting transfers between devices: 34.3 us -> 44.2 us
  local copies, waits for them, and re-layouts: 15.6 us -> 19.4 us
    ppermute x6, waiting for transfers between devices: 18.6 us -> 6.23 us  [send(): return lax.ppermute(array, 'out', ways)]
    ppermute x6, starting transfers between devices: 28.1 us -> 38 us  [send(): return lax.ppermute(array, 'out', ways)]
    pallas_call x0 -> x1, local copies, waits for them, and re-layouts: none -> 4.09 us  [fence(): pl.pallas_call(lambda *refs: None, in_specs=anywhere, out_specs=anywhere,...]
    unnamed x13 -> x15, local copies, waits for them, and re-layouts: 9.1 us -> 8.19 us
  transfers between devices with their start and end apart: 13 -> 13, of which waited for: 7 -> 6; matrix products, arithmetic and copies ran while one was open for 6% -> 9% of each run, Pallas kernels for 39% -> 39%
where the time goes in v6:
time: 181 us; the launch traced here: 178 us
  Pallas kernels  73.2 us (40%)
  starting transfers between devices  44.2 us (24%)
  waiting for transfers between devices  28.7 us (16%)
  local copies, waits for them, and re-layouts  19.4 us (11%)
  blocking collectives  9.25 us (5%)
  other arithmetic  3.23 us (2%)
    pallas_call x10, Pallas kernels, call(): pl.pallas_call(run, grid=grid, in_specs=list(in_specs) + [anywhere] * n_t...  73.2 us
    ppermute x6, starting transfers between devices, send(): return lax.ppermute(array, 'out', ways)  38 us
    ppermute x4, waiting for transfers between devices, swap(): return lax.ppermute(array, 'vir', [(k, k ^ mask) for k in range(vir)])  14.9 us
    all_to_all x1, blocking collectives, body(): swapped = lax.all_to_all(parts, 'vir', split_axis=0, concat_axis=0)  9.25 us
    unnamed x15, local copies, waits for them, and re-layouts  8.19 us
    ppermute x3, waiting for transfers between devices, spread(): heres = [lax.ppermute(rows, 'out', [(0, k)]) for k in range(n - 1, 0, -1)]  7.59 us
    ppermute x6, waiting for transfers between devices, send(): return lax.ppermute(array, 'out', ways)  6.23 us
    slice x2, local copies, waits for them, and re-layouts, body(): own[i:j]  4.75 us
  transfers between devices with their start and end apart: 13, of which 6 were waited for; matrix products, arithmetic and copies ran while one was open for 9% of the time, Pallas kernels for 39%

profile of v6, /device:TPU:16, one launch (start us, length us, event | category | flops | bytes accessed | tf_op | source)
XLA Modules:
  0.0 178.1 jit_solution(15405274133067743283)
XLA Ops:
  0.0 1.0 slice.9
  1.0 0.7 collective-permute-start.1
  1.7 1.3 collective-permute-start.2
  3.0 0.7 collective-permute-start.3
  3.7 7.9 %collective-permute-start.8 = (bf16[32,64,512]{2,1,0:T(8,128)(2,1)}, bf16[32,64,512]{2,1,0:T(8,128)(2,1)}, u32[]{:S(2)}, u32[]{:S(2)}) collective-permute-start(bf16[32,64,512]{2,1,0:T(8,128)(2,1)} %param.4), channel_id=1, source_target_pairs={{2,0},{1,3},{6,4},{5,7},{10,8},{9,11},{14,12},{13,15},{18,16},{17,... | collective-permute-start | bytes 6291464 | tf_op jit(solution)/shard_map/ppermute | solution.py:292
  11.6 4.1 %copy.22 = bf16[32,64,512]{2,0,1:T(8,128)(2,1)} copy(bf16[32,64,512]{2,1,0:T(8,128)(2,1)} %param.4) | data formatting | bytes 4194304 | tf_op args[1]
  15.7 0.0 collective-permute-start
  15.7 0.0 collective-permute-done.1
  15.7 7.6 %collective-permute-done.2 = bf16[2,64,1536]{2,1,0:T(8,128)(2,1)S(1)} collective-permute-done((bf16[2,64,1536]{2,1,0:T(8,128)(2,1)S(1)}, bf16[2,64,1536]{2,1,0:T(8,128)(2,1)S(1)}, u32[]{:S(2)}, u32[]{:S(2)}) %collective-permute-start.2) | collective-permute-done | bytes 393248 | tf_op jit(solution)/shard_map/ppermute | solution.py:261
  23.3 0.0 collective-permute-done.3
  23.3 1.1 select_select_fusion.refs_0_
  24.4 1.6 collective-permute-start.4
  26.0 1.5 collective-permute-start.5
  27.5 0.5 collective-permute-start.6
  28.0 8.6 %collective-permute-done.4.refs_1_ = bf16[2,64,1536]{2,1,0:T(8,128)(2,1)S(1)} collective-permute-done((bf16[2,64,1536]{2,1,0:T(8,128)(2,1)S(1)}, bf16[2,64,1536]{2,1,0:T(8,128)(2,1)S(1)}, u32[]{:S(2)}, u32[]{:S(2)}) %collective-permute-start.4) | collective-permute-done | bytes 393248 | tf_op jit(solution)/shard_map/ppermute | solution.py:271
  36.5 6.4 %collective-permute-done.5.refs_2_ = bf16[2,64,1536]{2,1,0:T(8,128)(2,1)S(1)} collective-permute-done((bf16[2,64,1536]{2,1,0:T(8,128)(2,1)S(1)}, bf16[2,64,1536]{2,1,0:T(8,128)(2,1)S(1)}, u32[]{:S(2)}, u32[]{:S(2)}) %collective-permute-start.5) | collective-permute-done | bytes 393248 | tf_op jit(solution)/shard_map/ppermute | solution.py:271
  42.9 0.0 collective-permute-done.6.refs_3_
  42.9 1.3 shard_map.37
  44.2 0.0 collective-permute-start.7
  44.2 0.0 copy-start
  44.2 2.8 %slice.12.refs_2_ = bf16[48,32,512]{2,1,0:T(8,128)(2,1)} slice(bf16[64,32,512]{2,1,0:T(8,128)(2,1)} %bitcast.15.clone.2.refs_2_.refs_0_), slice={[0:48], [0:32], [0:512]} | slice | bytes 3145728 | tf_op jit(solution)/shard_map/slice | solution.py:317
  47.0 1.9 %slice.13.refs_3_ = bf16[16,32,512]{2,1,0:T(8,128)(2,1)} slice(bf16[64,32,512]{2,1,0:T(8,128)(2,1)} %bitcast.15.clone.2.refs_2_.refs_0_), slice={[48:64], [0:32], [0:512]} | slice | bytes 1048576 | tf_op jit(solution)/shard_map/slice | solution.py:317
  48.9 0.1 stack.35.refs_0_
  49.0 1.2 dynamic-slice_bitcast_fusion.refs_0_
  50.2 0.0 collective-permute-done.7.refs_2_
  50.2 0.0 copy-start.3
  50.2 1.1 copy-done.3
  51.4 0.0 copy-done
  51.4 4.1 %shard_map.38 = (bf16[2,1536,512]{2,1,0:T(8,128)(2,1)}, f32[8,128]{1,0:T(8,128)S(1)}) custom-call(s32[8]{0:T(128)S(1)} %stack.35.refs_0_, bf16[4,2,64,1536]{3,2,1,0:T(8,128)(2,1)S(1)} %copy-done, bf16[4,2,64,1536]{3,2,1,0:T(8,128)(2,1)} %copy-done.3, f32[8,128]{1,0:T(8,128)S(1)} %get-tuple-element.21.refs_3_), custom_call_target="tpu_custom_call", output_to_operand_aliasing={{1}: (3, {})} | custom-call | flops 1024 | bytes 1024 | tf_op jit(solution)/shard_map/pallas_call | solution.py:33
  55.5 25.9 %shard_map.39 = (bf16[48,2,128,512]{3,2,1,0:T(8,128)(2,1)}, f32[8,128]{1,0:T(8,128)S(1)}) custom-call(bf16[128,64,1536]{2,1,0:T(8,128)(2,1)} %refs_0_.3, bf16[2,1536,512]{2,1,0:T(8,128)(2,1)} %get-tuple-element.22.refs_1_, f32[8,128]{1,0:T(8,128)S(1)} %get-tuple-element.23.refs_2_), custom_call_target="tpu_custom_call", output_to_operand_aliasing={{1}: (2, {})} | custom-call | flops 1024 | bytes 1024 | tf_op jit(solution)/shard_map/pallas_call | solution.py:33
  81.4 0.0 collective-permute-done
  81.4 2.6 %shard_map.40 = (bf16[48,32,512]{2,1,0:T(8,128)(2,1)S(1)}, f32[8,128]{1,0:T(8,128)S(1)}) custom-call(s32[1]{0:T(128)} %bitcast.3.refs_0_, bf16[64,32,512]{2,1,0:T(8,128)(2,1)} %bitcast.2.refs_1_, bf16[64,32,512]{2,1,0:T(8,128)(2,1)} %bitcast.15.clone.2.refs_2_.refs_0_, f32[8,128]{1,0:T(8,128)S(1)} %get-tuple-element.24.refs_3_), custom_call_target="tpu_custom_call", output_to_operand_aliasing={{1}: (3, {})} | custom-call | flops 1024 | bytes 1024 | tf_op jit(solution)/shard_map/pallas_call | solution.py:33
  84.0 1.2 shard_map.41
  85.3 0.0 copy-start.1
  85.3 0.6 copy-done.1
  85.9 9.9 %collective-permute-start.9 = (bf16[48,32,512]{2,1,0:T(8,128)(2,1)S(1)}, bf16[48,32,512]{2,1,0:T(8,128)(2,1)}, u32[]{:S(2)}, u32[]{:S(2)}) collective-permute-start(bf16[48,32,512]{2,1,0:T(8,128)(2,1)S(1)} %get-tuple-element.31), channel_id=1, source_target_pairs={{1,0},{0,1},{2,3},{3,2},{5,4},{4,5},{6,7},{7,6},{9,8},{8,9},{10,11... | collective-permute-start | bytes 4718600 | tf_op jit(solution)/shard_map/ppermute | solution.py:292
  95.8 4.4 %collective-permute-done.8.refs_1_ = bf16[32,64,512]{2,1,0:T(8,128)(2,1)} collective-permute-done((bf16[32,64,512]{2,1,0:T(8,128)(2,1)}, bf16[32,64,512]{2,1,0:T(8,128)(2,1)}, u32[]{:S(2)}, u32[]{:S(2)}) %collective-permute-start.8) | collective-permute-done | bytes 2097184 | tf_op jit(solution)/shard_map/ppermute | solution.py:292
  100.1 17.5 %collective-permute-start.10 = (bf16[48,32,512]{2,1,0:T(8,128)(2,1)}, bf16[48,32,512]{2,1,0:T(8,128)(2,1)}, u32[]{:S(2)}, u32[]{:S(2)}) collective-permute-start(bf16[48,32,512]{2,1,0:T(8,128)(2,1)} %get-tuple-element.32), channel_id=1, source_target_pairs={{2,1},{1,2},{6,5},{5,6},{10,9},{9,10},{14,13},{13,14},{18,17},{17,... | collective-permute-start | bytes 4718600 | tf_op jit(solution)/shard_map/ppermute | solution.py:292
  117.6 0.0 copy-start.2
  117.7 0.7 copy-done.2
  118.3 11.4 %shard_map.44 = (bf16[16,2,128,512]{3,2,1,0:T(8,128)(2,1)}, f32[8,128]{1,0:T(8,128)S(1)}) custom-call(bf16[128,64,1536]{2,1,0:T(8,128)(2,1)} %refs_0_.3, bf16[2,1536,512]{2,1,0:T(8,128)(2,1)} %get-tuple-element.22.refs_1_, f32[8,128]{1,0:T(8,128)S(1)} %copy-done.2), custom_call_target="tpu_custom_call", output_to_operand_aliasing={{1}: (2, {})} | custom-call | flops 1024 | bytes 1024 | tf_op jit(solution)/shard_map/pallas_call | solution.py:33
  129.7 4.1 %copy.21 = bf16[32,64,512]{2,0,1:T(8,128)(2,1)} copy(bf16[32,64,512]{2,1,0:T(8,128)(2,1)} %get-tuple-element.27) | data formatting | bytes 4194304 | tf_op jit(solution)/shard_map/pallas_call | solution.py:49
  133.8 4.1 %shard_map.45 = f32[96,256]{1,0:T(8,128)} custom-call(bf16[64,32,512]{2,1,0:T(8,128)(2,1)} %bitcast.15.clone.2.refs_2_.refs_0_, bf16[64,32,512]{2,1,0:T(8,128)(2,1)} %bitcast.2.refs_1_, bf16[64,32,512]{2,1,0:T(8,128)(2,1)} %bitcast.17, bf16[16,2,128,512]{3,2,1,0:T(8,128)(2,1)} %get-tuple-element.30.refs_3_.refs_4_.refs_5_.refs_6_, ...), custom_call_target="tpu_custom_call" | custom-call | flops 1024 | bytes 1024 | tf_op jit(solution)/shard_map/pallas_call | solution.py:33
  137.9 0.0 copy-start.6
  137.9 9.5 %shard_map.43 = f32[96,256]{1,0:T(8,128)} custom-call(bf16[64,32,512]{2,1,0:T(8,128)(2,1)} %bitcast.15.clone.2.refs_2_.refs_0_, bf16[64,32,512]{2,1,0:T(8,128)(2,1)} %bitcast.2.refs_1_, bf16[64,32,512]{2,1,0:T(8,128)(2,1)} %bitcast.18, bf16[48,2,128,512]{3,2,1,0:T(8,128)(2,1)} %get-tuple-element.28.refs_3_.refs_4_.refs_2_, ...), custom_call_target="tpu_custom_call" | custom-call | flops 1024 | bytes 1024 | tf_op jit(solution)/shard_map/pallas_call | solution.py:33
  147.4 1.9 %collective-permute-start.12 = (bf16[16,32,512]{2,1,0:T(8,128)(2,1)}, bf16[16,32,512]{2,1,0:T(8,128)(2,1)S(1)}, u32[]{:S(2)}, u32[]{:S(2)}) collective-permute-start(bf16[16,32,512]{2,1,0:T(8,128)(2,1)} %get-tuple-element.34), channel_id=1, source_target_pairs={{2,1},{1,2},{6,5},{5,6},{10,9},{9,10},{14,13},{13,14},{18,17},{17,... | collective-permute-start | bytes 1572872 | tf_op jit(solution)/shard_map/ppermute | solution.py:292
  149.4 0.7 collective-permute-start.11
  150.1 0.0 copy-done.6
  150.1 1.5 add.7.refs_1_
  151.6 0.0 collective-permute-done.9.refs_0_
  151.7 1.0 collective-permute-done.10.refs_1_
  152.6 9.1 %shard_map.47.refs_2_ = f32[64,256]{1,0:T(8,128)} custom-call(bf16[48,32,512]{2,1,0:T(8,128)(2,1)} %shard_map.46.refs_0_, bf16[48,32,512]{2,1,0:T(8,128)(2,1)} %collective-permute-done.10.refs_1_, bf16[48,2,128,512]{3,2,1,0:T(8,128)(2,1)} %get-tuple-element.28.refs_3_.refs_4_.refs_2_, bf16[48,2,128,512]{3,2,1,0:T(8,128)(2,1)} %get-tuple-element.28.refs_3_.refs_4_.refs_2_), custom_call_target="tpu_custom_call" | custom-call | flops 1024 | bytes 1024 | tf_op jit(solution)/shard_map/pallas_call | solution.py:33
  161.7 0.9 collective-permute-done.12.refs_4_
  162.6 0.0 copy-start.4
  162.6 0.0 collective-permute-done.11.refs_3_
  162.6 0.8 copy-done.4
  163.4 0.0 copy-start.5
  163.4 0.8 copy-done.5
  164.2 4.0 %shard_map.48 = f32[8,2,16,128]{3,2,1,0:T(8,128)} custom-call(s32[4]{0:T(128)} %dynamic-slice_bitcast_fusion.refs_0_, f32[96,256]{1,0:T(8,128)} %add.7.refs_1_, f32[64,256]{1,0:T(8,128)} %shard_map.47.refs_2_, bf16[16,32,512]{2,1,0:T(8,128)(2,1)} %copy-done.5, bf16[16,32,512]{2,1,0:T(8,128)(2,1)} %copy-done.4, ...), custom_call_target="tpu_custom_call" | custom-call | flops 1024 | bytes 1024 | tf_op jit(solution)/shard_map/pallas_call | solution.py:33
  168.2 9.3 %all_to_all.5 = f32[8,2,16,128]{3,2,1,0:T(8,128)S(1)} all-to-all(f32[8,2,16,128]{3,2,1,0:T(8,128)} %shard_map.48), channel_id=1, replica_groups=mesh['vir'=8,'out'=4] {'vir'}, dimensions={0} | all-to-all | bytes 262144 | tf_op jit(solution)/shard_map/all_to_all | solution.py:340
  177.5 0.6 reduce_sum.9
  (3 shorter events, 0.0 us)
Async XLA Ops:
  1.0 14.7 %collective-permute-start.1 = (bf16[2,64,1536]{2,1,0:T(8,128)(2,1)S(1)}, bf16[2,64,1536]{2,1,0:T(8,128)(2,1)S(1)}, u32[]{:S(2)}, u32[]{:S(2)}) collective-permute-start(bf16[2,64,1536]{2,1,0:T(8,128)(2,1)S(1)} %slice.9), channel_id=1, source_target_pairs={{0,1},{4,5},{8,9},{12,13},{16,17},{20,21},{24,25},{28,29}} | collective-permute-start | bytes 1179656 | tf_op jit(solution)/shard_map/ppermute | solution.py:261
  1.7 21.6 %collective-permute-start.2 = (bf16[2,64,1536]{2,1,0:T(8,128)(2,1)S(1)}, bf16[2,64,1536]{2,1,0:T(8,128)(2,1)S(1)}, u32[]{:S(2)}, u32[]{:S(2)}) collective-permute-start(bf16[2,64,1536]{2,1,0:T(8,128)(2,1)S(1)} %slice.9), channel_id=1, source_target_pairs={{0,2},{4,6},{8,10},{12,14},{16,18},{20,22},{24,26},{28,30}} | collective-permute-start | bytes 1179656 | tf_op jit(solution)/shard_map/ppermute | solution.py:261
  3.0 20.3 %collective-permute-start.3 = (bf16[2,64,1536]{2,1,0:T(8,128)(2,1)S(1)}, bf16[2,64,1536]{2,1,0:T(8,128)(2,1)S(1)}, u32[]{:S(2)}, u32[]{:S(2)}) collective-permute-start(bf16[2,64,1536]{2,1,0:T(8,128)(2,1)S(1)} %slice.9), channel_id=1, source_target_pairs={{0,3},{4,7},{8,11},{12,15},{16,19},{20,23},{24,27},{28,31}} | collective-permute-start | bytes 1179656 | tf_op jit(solution)/shard_map/ppermute | solution.py:261
  3.7 96.4 %collective-permute-start.8 = (bf16[32,64,512]{2,1,0:T(8,128)(2,1)}, bf16[32,64,512]{2,1,0:T(8,128)(2,1)}, u32[]{:S(2)}, u32[]{:S(2)}) collective-permute-start(bf16[32,64,512]{2,1,0:T(8,128)(2,1)} %param.4), channel_id=1, source_target_pairs={{2,0},{1,3},{6,4},{5,7},{10,8},{9,11},{14,12},{13,15},{18,16},{17,... | collective-permute-start | bytes 6291464 | tf_op jit(solution)/shard_map/ppermute | solution.py:292
  15.7 65.7 %collective-permute-start = (bf16[32,64,512]{2,0,1:T(8,128)(2,1)}, bf16[32,64,512]{2,0,1:T(8,128)(2,1)}, u32[]{:S(2)}, u32[]{:S(2)}) collective-permute-start(bf16[32,64,512]{2,0,1:T(8,128)(2,1)} %copy.22), channel_id=1, source_target_pairs={{3,1},{1,0},{0,2},{2,3},{7,5},{5,4},{4,6},{6,7},{11,9},{9,8},{8,10... | collective-permute-start | bytes 6291464 | tf_op jit(solution)/shard_map/ppermute | solution.py:292
  24.4 12.1 %collective-permute-start.4 = (bf16[2,64,1536]{2,1,0:T(8,128)(2,1)S(1)}, bf16[2,64,1536]{2,1,0:T(8,128)(2,1)S(1)}, u32[]{:S(2)}, u32[]{:S(2)}) collective-permute-start(bf16[2,64,1536]{2,1,0:T(8,128)(2,1)S(1)} %select_select_fusion.refs_0_), channel_id=1, source_target_pairs={{0,8},{4,12},{8,0},{12,4},{16,24},{20,28},{24,16},{28,20},{1,9},{5... | collective-permute-start | bytes 1179656 | tf_op jit(solution)/shard_map/ppermute | solution.py:271
  26.0 16.9 %collective-permute-start.5 = (bf16[2,64,1536]{2,1,0:T(8,128)(2,1)S(1)}, bf16[2,64,1536]{2,1,0:T(8,128)(2,1)S(1)}, u32[]{:S(2)}, u32[]{:S(2)}) collective-permute-start(bf16[2,64,1536]{2,1,0:T(8,128)(2,1)S(1)} %select_select_fusion.refs_0_), channel_id=1, source_target_pairs={{0,16},{4,20},{8,24},{12,28},{16,0},{20,4},{24,8},{28,12},{1,17},{... | collective-permute-start | bytes 1179656 | tf_op jit(solution)/shard_map/ppermute | solution.py:271
  27.5 15.4 %collective-permute-start.6 = (bf16[2,64,1536]{2,1,0:T(8,128)(2,1)S(1)}, bf16[2,64,1536]{2,1,0:T(8,128)(2,1)S(1)}, u32[]{:S(2)}, u32[]{:S(2)}) collective-permute-start(bf16[2,64,1536]{2,1,0:T(8,128)(2,1)S(1)} %select_select_fusion.refs_0_), channel_id=1, source_target_pairs={{0,24},{4,28},{8,16},{12,20},{16,8},{20,12},{24,0},{28,4},{1,25},{... | collective-permute-start | bytes 1179656 | tf_op jit(solution)/shard_map/ppermute | solution.py:271
  44.2 6.1 %collective-permute-start.7 = (bf16[4,2,64,1536]{3,2,1,0:T(8,128)(2,1)}, bf16[4,2,64,1536]{3,2,1,0:T(8,128)(2,1)S(1)}, u32[]{:S(2)}, u32[]{:S(2)}) collective-permute-start(bf16[4,2,64,1536]{3,2,1,0:T(8,128)(2,1)} %get-tuple-element.20.refs_1_), channel_id=1, source_target_pairs={{0,4},{4,0},{8,12},{12,8},{16,20},{20,16},{24,28},{28,24},{1,5},{5... | collective-permute-start | bytes 4718600 | tf_op jit(solution)/shard_map/ppermute | solution.py:271
  44.2 7.2 %copy-start = (bf16[4,2,64,1536]{3,2,1,0:T(8,128)(2,1)S(1)}, bf16[4,2,64,1536]{3,2,1,0:T(8,128)(2,1)}, u32[]{:S(2)}) copy-start(bf16[4,2,64,1536]{3,2,1,0:T(8,128)(2,1)} %get-tuple-element.20.refs_1_) | copy-start | bytes 4718596
  50.2 1.1 copy-start.3
  85.3 0.6 copy-start.1
  85.9 65.8 %collective-permute-start.9 = (bf16[48,32,512]{2,1,0:T(8,128)(2,1)S(1)}, bf16[48,32,512]{2,1,0:T(8,128)(2,1)}, u32[]{:S(2)}, u32[]{:S(2)}) collective-permute-start(bf16[48,32,512]{2,1,0:T(8,128)(2,1)S(1)} %get-tuple-element.31), channel_id=1, source_target_pairs={{1,0},{0,1},{2,3},{3,2},{5,4},{4,5},{6,7},{7,6},{9,8},{8,9},{10,11... | collective-permute-start | bytes 4718600 | tf_op jit(solution)/shard_map/ppermute | solution.py:292
  100.1 52.5 %collective-permute-start.10 = (bf16[48,32,512]{2,1,0:T(8,128)(2,1)}, bf16[48,32,512]{2,1,0:T(8,128)(2,1)}, u32[]{:S(2)}, u32[]{:S(2)}) collective-permute-start(bf16[48,32,512]{2,1,0:T(8,128)(2,1)} %get-tuple-element.32), channel_id=1, source_target_pairs={{2,1},{1,2},{6,5},{5,6},{10,9},{9,10},{14,13},{13,14},{18,17},{17,... | collective-permute-start | bytes 4718600 | tf_op jit(solution)/shard_map/ppermute | solution.py:292
  117.6 0.7 copy-start.2
  137.9 12.2 %copy-start.6 = (f32[96,256]{1,0:T(8,128)S(1)}, f32[96,256]{1,0:T(8,128)}, u32[]{:S(2)}) copy-start(f32[96,256]{1,0:T(8,128)} %shard_map.45) | copy-start | bytes 294916
  147.4 15.2 %collective-permute-start.12 = (bf16[16,32,512]{2,1,0:T(8,128)(2,1)}, bf16[16,32,512]{2,1,0:T(8,128)(2,1)S(1)}, u32[]{:S(2)}, u32[]{:S(2)}) collective-permute-start(bf16[16,32,512]{2,1,0:T(8,128)(2,1)} %get-tuple-element.34), channel_id=1, source_target_pairs={{2,1},{1,2},{6,5},{5,6},{10,9},{9,10},{14,13},{13,14},{18,17},{17,... | collective-permute-start | bytes 1572872 | tf_op jit(solution)/shard_map/ppermute | solution.py:292
  149.4 13.2 %collective-permute-start.11 = (bf16[16,32,512]{2,1,0:T(8,128)(2,1)S(1)}, bf16[16,32,512]{2,1,0:T(8,128)(2,1)S(1)}, u32[]{:S(2)}, u32[]{:S(2)}) collective-permute-start(bf16[16,32,512]{2,1,0:T(8,128)(2,1)S(1)} %get-tuple-element.33), channel_id=1, source_target_pairs={{1,0},{0,1},{2,3},{3,2},{5,4},{4,5},{6,7},{7,6},{9,8},{8,9},{10,11... | collective-permute-start | bytes 1572872 | tf_op jit(solution)/shard_map/ppermute | solution.py:292
  162.6 0.8 copy-start.4
  163.4 0.8 copy-start.5

commit v7 on v5

--- a/solution.py
+++ b/solution.py
@@ -91,6 +91,25 @@
     vmem = pl.BlockSpec(memory_space=pltpu.VMEM)
     shape = jax.ShapeDtypeStruct((len(slabs),) + slabs[0].shape, slabs[0].dtype)
     return call(pack_kernel, slabs, [vmem] * len(slabs), shape, vmem, through)
+
+
+def turn_kernel(in_ref, out_ref):
+    whole = in_ref[...].astype(jnp.float32)
+    out_ref[...] = jnp.swapaxes(whole, 0, 1).astype(out_ref.dtype)
+
+
+def turn(array, through):
+    pairs, c_rows, d_len = array.shape
+    c_len = largest_part(c_rows, 16)
+    return call(
+        turn_kernel,
+        [array],
+        [pl.BlockSpec((pairs, c_len, d_len), lambda i: (0, i, 0))],
+        jax.ShapeDtypeStruct((c_rows, pairs, d_len), array.dtype),
+        pl.BlockSpec((c_len, pairs, d_len), lambda i: (i, 0, 0)),
+        through,
+        grid=(c_rows // c_len,),
+    )
 
 
 def assemble_kernel(*refs):
@@ -305,16 +324,22 @@
     make()
     if n == 4:
         inside = (z == 1) | (z == 2)
-        second = send(own, (2, 0), (1, 3))
+        second = send(amplitudes, (2, 0), (1, 3))
         first = send(own, (3, 1), (1, 0), (0, 2), (2, 3))
-        onward = []
+        onward, kept = [], [own[i:j] for i, j in spans]
         for span in spans:
             part, [token] = pick(inside, first, own, *span, [token])
             onward.append(part)
-        sides = [send(t, (1, 0), (0, 1), (2, 3), (3, 2)) for t in onward]
-        token, second, *kept = fence([token, second] + [own[i:j] for i, j in spans], MUCH)
-        middle = [send(t, (2, 1), (1, 2)) for t in kept]
+        sides, middle = [], []
+        for k in range(len(spans)):
+            if k:
+                make()
+            token, onward[k], kept[k] = fence([token, onward[k], kept[k]])
+            middle.append(send(kept[k], (2, 1), (1, 2)))
+            sides.append(send(onward[k], (1, 0), (0, 1), (2, 3), (3, 2)))
+        token, second = fence([token, second], MUCH)
         [sides[0]] = fence(sides[:1], MUCH)
+        second, [token] = turn(second, [token])
         late = [[(t, 0) for t in pair] for pair in zip(sides, middle)]
         early = [own, first, second]
         slots = jnp.array([[0, 1, 2, 3], [3, 0, 4, 1], [1, 4, 0, 3], [3, 2, 1, 0]], jnp.int32)[z]

time: 177 us -> 173 us (0.977)
  waiting for transfers between devices: 42 us -> 36.9 us
  starting transfers between devices: 34.3 us -> 30.2 us
  local copies, waits for them, and re-layouts: 15.6 us -> 18.9 us
  Pallas kernels: 71.7 us -> 74.9 us
    ppermute x6, waiting for transfers between devices: 18.6 us -> 13.6 us  [send(): return lax.ppermute(array, 'out', ways)]
    ppermute x6, starting transfers between devices: 28.1 us -> 24 us  [send(): return lax.ppermute(array, 'out', ways)]
    unnamed x13 -> x21, local copies, waits for them, and re-layouts: 9.1 us -> 12.4 us
    pallas_call x10 -> x11, Pallas kernels: 71.7 us -> 74.9 us  [call(): pl.pallas_call(run, grid=grid, in_specs=list(in_specs) + [anywhere] * n_t...]
  transfers between devices with their start and end apart: 13 -> 13, of which waited for: 7 -> 6; matrix products, arithmetic and copies ran while one was open for 6% -> 6% of each run, Pallas kernels for 39% -> 42%
where the time goes in v7:
time: 173 us; the launch traced here: 172 us
  Pallas kernels  74.9 us (43%)
  waiting for transfers between devices  36.9 us (21%)
  starting transfers between devices  30.2 us (17%)
  local copies, waits for them, and re-layouts  18.9 us (11%)
  blocking collectives  9.06 us (5%)
    pallas_call x11, Pallas kernels, call(): pl.pallas_call(run, grid=grid, in_specs=list(in_specs) + [anywhere] * n_t...  74.9 us
    ppermute x6, starting transfers between devices, send(): return lax.ppermute(array, 'out', ways)  24 us
    ppermute x4, waiting for transfers between devices, swap(): return lax.ppermute(array, 'vir', [(k, k ^ mask) for k in range(vir)])  15 us
    ppermute x6, waiting for transfers between devices, send(): return lax.ppermute(array, 'out', ways)  13.6 us
    unnamed x21, local copies, waits for them, and re-layouts  12.4 us
    all_to_all x1, blocking collectives, body(): swapped = lax.all_to_all(parts, 'vir', split_axis=0, concat_axis=0)  9.06 us
    ppermute x3, waiting for transfers between devices, spread(): heres = [lax.ppermute(rows, 'out', [(0, k)]) for k in range(1, n)]  8.33 us
    slice x2, local copies, waits for them, and re-layouts, body(): onward, kept = ([], [own[i:j] for i, j in spans])  4.76 us
  transfers between devices with their start and end apart: 13, of which 6 were waited for; matrix products, arithmetic and copies ran while one was open for 6% of the time, Pallas kernels for 42%

profile of v7, /device:TPU:16, one launch (start us, length us, event | category | flops | bytes accessed | tf_op | source)
XLA Modules:
  0.0 171.9 jit_solution(7805154821304047921)
XLA Ops:
  0.0 1.0 slice.9
  1.0 0.7 collective-permute-start.1
  1.7 1.3 collective-permute-start.2
  3.0 0.7 collective-permute-start.3
  3.7 9.1 %collective-permute-start.8 = (bf16[32,64,512]{2,1,0:T(8,128)(2,1)}, bf16[32,64,512]{2,1,0:T(8,128)(2,1)}, u32[]{:S(2)}, u32[]{:S(2)}) collective-permute-start(bf16[32,64,512]{2,1,0:T(8,128)(2,1)} %param.4), channel_id=1, source_target_pairs={{2,0},{1,3},{6,4},{5,7},{10,8},{9,11},{14,12},{13,15},{18,16},{17,... | collective-permute-start | bytes 6291464 | tf_op jit(solution)/shard_map/ppermute | solution.py:309
  12.9 4.1 %copy.22 = bf16[32,64,512]{2,0,1:T(8,128)(2,1)} copy(bf16[32,64,512]{2,1,0:T(8,128)(2,1)} %param.4) | data formatting | bytes 4194304 | tf_op args[1]
  17.0 0.0 collective-permute-start
  17.0 0.0 collective-permute-done.1
  17.0 8.3 %collective-permute-done.2 = bf16[2,64,1536]{2,1,0:T(8,128)(2,1)S(1)} collective-permute-done((bf16[2,64,1536]{2,1,0:T(8,128)(2,1)S(1)}, bf16[2,64,1536]{2,1,0:T(8,128)(2,1)S(1)}, u32[]{:S(2)}, u32[]{:S(2)}) %collective-permute-start.2) | collective-permute-done | bytes 393248 | tf_op jit(solution)/shard_map/ppermute | solution.py:278
  25.3 0.0 collective-permute-done.3
  25.3 1.1 select_select_fusion.refs_0_
  26.4 1.6 collective-permute-start.4
  27.9 1.5 collective-permute-start.5
  29.5 0.5 collective-permute-start.6
  29.9 8.6 %collective-permute-done.4.refs_1_ = bf16[2,64,1536]{2,1,0:T(8,128)(2,1)S(1)} collective-permute-done((bf16[2,64,1536]{2,1,0:T(8,128)(2,1)S(1)}, bf16[2,64,1536]{2,1,0:T(8,128)(2,1)S(1)}, u32[]{:S(2)}, u32[]{:S(2)}) %collective-permute-start.4) | collective-permute-done | bytes 393248 | tf_op jit(solution)/shard_map/ppermute | solution.py:288
  38.5 6.4 %collective-permute-done.5.refs_2_ = bf16[2,64,1536]{2,1,0:T(8,128)(2,1)S(1)} collective-permute-done((bf16[2,64,1536]{2,1,0:T(8,128)(2,1)S(1)}, bf16[2,64,1536]{2,1,0:T(8,128)(2,1)S(1)}, u32[]{:S(2)}, u32[]{:S(2)}) %collective-permute-start.5) | collective-permute-done | bytes 393248 | tf_op jit(solution)/shard_map/ppermute | solution.py:288
  44.9 0.0 collective-permute-done.6.refs_3_
  44.9 1.3 shard_map.37
  46.2 0.0 collective-permute-start.7
  46.2 0.0 copy-start.1
  46.2 2.9 %slice.12.refs_2_ = bf16[48,32,512]{2,1,0:T(8,128)(2,1)} slice(bf16[64,32,512]{2,1,0:T(8,128)(2,1)} %bitcast.13.refs_2_.refs_0_), slice={[0:48], [0:32], [0:512]} | slice | bytes 3145728 | tf_op jit(solution)/shard_map/slice | solution.py:329
  49.1 1.9 %slice.13.refs_2_ = bf16[16,32,512]{2,1,0:T(8,128)(2,1)} slice(bf16[64,32,512]{2,1,0:T(8,128)(2,1)} %bitcast.13.refs_2_.refs_0_), slice={[48:64], [0:32], [0:512]} | slice | bytes 1048576 | tf_op jit(solution)/shard_map/slice | solution.py:329
  51.0 0.1 stack.35.refs_0_
  51.1 0.7 dynamic-slice_bitcast_fusion.refs_0_
  51.8 0.0 collective-permute-done.7.refs_2_
  51.8 0.0 copy-start.9
  51.8 1.1 copy-done.9
  52.9 0.0 copy-done.1
  52.9 4.1 %shard_map.38 = (bf16[2,1536,512]{2,1,0:T(8,128)(2,1)}, f32[8,128]{1,0:T(8,128)S(1)}) custom-call(s32[8]{0:T(128)S(1)} %stack.35.refs_0_, bf16[4,2,64,1536]{3,2,1,0:T(8,128)(2,1)S(1)} %copy-done.1, bf16[4,2,64,1536]{3,2,1,0:T(8,128)(2,1)} %copy-done.9, f32[8,128]{1,0:T(8,128)S(1)} %get-tuple-element.27.refs_3_), custom_call_target="tpu_custom_call", output_to_operand_aliasing={{1}: (3, {})} | custom-call | flops 1024 | bytes 1024 | tf_op jit(solution)/shard_map/pallas_call | solution.py:33
  57.0 25.9 %shard_map.39 = (bf16[48,2,128,512]{3,2,1,0:T(8,128)(2,1)}, f32[8,128]{1,0:T(8,128)S(1)}) custom-call(bf16[128,64,1536]{2,1,0:T(8,128)(2,1)} %refs_0_.3, bf16[2,1536,512]{2,1,0:T(8,128)(2,1)} %get-tuple-element.28.refs_1_, f32[8,128]{1,0:T(8,128)S(1)} %get-tuple-element.29.refs_2_), custom_call_target="tpu_custom_call", output_to_operand_aliasing={{1}: (2, {})} | custom-call | flops 1024 | bytes 1024 | tf_op jit(solution)/shard_map/pallas_call | solution.py:33
  83.0 0.0 collective-permute-done.refs_1_
  83.0 2.6 %shard_map.40 = (bf16[48,32,512]{2,1,0:T(8,128)(2,1)S(1)}, f32[8,128]{1,0:T(8,128)S(1)}) custom-call(s32[1]{0:T(128)} %bitcast.10.refs_0_, bf16[64,32,512]{2,1,0:T(8,128)(2,1)} %collective-permute-done.refs_1_, bf16[64,32,512]{2,1,0:T(8,128)(2,1)} %bitcast.13.refs_2_.refs_0_, f32[8,128]{1,0:T(8,128)S(1)} %get-tuple-element.30.refs_3_), custom_call_target="tpu_custom_call", output_to_operand_aliasing={{1}: (3, {})} | custom-call | flops 1024 | bytes 1024 | tf_op jit(solution)/shard_map/pallas_call | solution.py:33
  85.6 0.0 copy-start
  85.6 1.2 copy-done
  86.7 1.2 shard_map.41
  88.0 0.0 copy-start.4
  88.0 0.8 copy-done.4
  88.8 0.0 copy-start.5
  88.8 0.6 copy-done.5
  89.4 0.0 collective-permute-start.9
  89.4 11.0 %collective-permute-start.10 = (bf16[48,32,512]{2,1,0:T(8,128)(2,1)}, bf16[48,32,512]{2,1,0:T(8,128)(2,1)}, u32[]{:S(2)}, u32[]{:S(2)}) collective-permute-start(bf16[48,32,512]{2,1,0:T(8,128)(2,1)} %get-tuple-element.44), channel_id=1, source_target_pairs={{2,1},{1,2},{6,5},{5,6},{10,9},{9,10},{14,13},{13,14},{18,17},{17,... | collective-permute-start | bytes 4718600 | tf_op jit(solution)/shard_map/ppermute | solution.py:309
  100.4 0.0 copy-start.6
  100.4 0.7 copy-done.6
  101.1 11.4 %shard_map.43 = (bf16[16,2,128,512]{3,2,1,0:T(8,128)(2,1)}, f32[8,128]{1,0:T(8,128)S(1)}) custom-call(bf16[128,64,1536]{2,1,0:T(8,128)(2,1)} %refs_0_.3, bf16[2,1536,512]{2,1,0:T(8,128)(2,1)} %get-tuple-element.28.refs_1_, f32[8,128]{1,0:T(8,128)S(1)} %copy-done.6), custom_call_target="tpu_custom_call", output_to_operand_aliasing={{1}: (2, {})} | custom-call | flops 1024 | bytes 1024 | tf_op jit(solution)/shard_map/pallas_call | solution.py:33
  112.5 0.0 copy-start.7
  112.5 0.6 copy-done.7
  113.1 0.0 collective-permute-start.11
  113.1 3.9 %collective-permute-start.12 = (bf16[16,32,512]{2,1,0:T(8,128)(2,1)}, bf16[16,32,512]{2,1,0:T(8,128)(2,1)S(1)}, u32[]{:S(2)}, u32[]{:S(2)}) collective-permute-start(bf16[16,32,512]{2,1,0:T(8,128)(2,1)} %get-tuple-element.46), channel_id=1, source_target_pairs={{2,1},{1,2},{6,5},{5,6},{10,9},{9,10},{14,13},{13,14},{18,17},{17,... | collective-permute-start | bytes 1572872 | tf_op jit(solution)/shard_map/ppermute | solution.py:309
  116.9 0.0 collective-permute-done.8.refs_1_
  117.0 0.0 copy-start.8
  117.0 0.7 copy-done.8
  117.7 4.3 %shard_map.46 = (bf16[64,32,512]{2,1,0:T(8,128)(2,1)}, f32[8,128]{1,0:T(8,128)S(1)}) custom-call(bf16[32,64,512]{2,1,0:T(8,128)(2,1)} %get-tuple-element.38.refs_0_, f32[8,128]{1,0:T(8,128)S(1)} %copy-done.8), custom_call_target="tpu_custom_call", output_to_operand_aliasing={{1}: (1, {})} | custom-call | flops 1024 | bytes 1024 | tf_op jit(solution)/shard_map/pallas_call | solution.py:33
  121.9 3.5 %shard_map.48 = f32[96,256]{1,0:T(8,128)S(1)} custom-call(bf16[64,32,512]{2,1,0:T(8,128)(2,1)} %bitcast.13.refs_2_.refs_0_, bf16[64,32,512]{2,1,0:T(8,128)(2,1)} %collective-permute-done.refs_1_, bf16[64,32,512]{2,1,0:T(8,128)(2,1)} %get-tuple-element.40.refs_2_, bf16[16,2,128,512]{3,2,1,0:T(8,128)(2,1)} %get-tuple-element.42.refs_3_.refs_5_), custom_call_target="tpu_custom_call" | custom-call | flops 1024 | bytes 1024 | tf_op jit(solution)/shard_map/pallas_call | solution.py:33
  125.5 9.0 %shard_map.47 = f32[96,256]{1,0:T(8,128)S(1)} custom-call(bf16[64,32,512]{2,1,0:T(8,128)(2,1)} %bitcast.13.refs_2_.refs_0_, bf16[64,32,512]{2,1,0:T(8,128)(2,1)} %collective-permute-done.refs_1_, bf16[64,32,512]{2,1,0:T(8,128)(2,1)} %get-tuple-element.40.refs_2_, bf16[48,2,128,512]{3,2,1,0:T(8,128)(2,1)} %get-tuple-element.41.refs_3_.refs_2_), custom_call_target="tpu_custom_call" | custom-call | flops 1024 | bytes 1024 | tf_op jit(solution)/shard_map/pallas_call | solution.py:33
  134.6 12.3 %collective-permute-done.9.refs_0_ = bf16[48,32,512]{2,1,0:T(8,128)(2,1)S(1)} collective-permute-done((bf16[48,32,512]{2,1,0:T(8,128)(2,1)}, bf16[48,32,512]{2,1,0:T(8,128)(2,1)S(1)}, u32[]{:S(2)}, u32[]{:S(2)}) %collective-permute-start.9) | collective-permute-done | bytes 1572896 | tf_op jit(solution)/shard_map/ppermute | solution.py:309
  146.8 1.2 copy-done.2
  148.0 0.0 collective-permute-done.10.refs_1_
  148.1 1.4 copy-done.3
  149.5 8.3 %shard_map.50.refs_2_ = f32[64,256]{1,0:T(8,128)S(1)} custom-call(bf16[48,32,512]{2,1,0:T(8,128)(2,1)S(1)} %copy-done.3, bf16[48,32,512]{2,1,0:T(8,128)(2,1)} %collective-permute-done.10.refs_1_, bf16[48,2,128,512]{3,2,1,0:T(8,128)(2,1)} %get-tuple-element.41.refs_3_.refs_2_), custom_call_target="tpu_custom_call" | custom-call | flops 1024 | bytes 1024 | tf_op jit(solution)/shard_map/pallas_call | solution.py:33
  157.8 0.3 collective-permute-done.11.refs_3_
  158.1 1.0 collective-permute-done.12.refs_4_
  159.0 3.1 %shard_map.51 = f32[8,2,16,128]{3,2,1,0:T(8,128)S(1)} custom-call(s32[4]{0:T(128)S(1)} %dynamic-slice_bitcast_fusion.refs_0_, f32[96,256]{1,0:T(8,128)S(1)} %add.7.refs_1_, f32[64,256]{1,0:T(8,128)S(1)} %shard_map.50.refs_2_, bf16[16,32,512]{2,1,0:T(8,128)(2,1)S(1)} %collective-permute-done.11.refs_3_, ...), custom_call_target="tpu_custom_call" | custom-call | flops 1024 | bytes 1024 | tf_op jit(solution)/shard_map/pallas_call | solution.py:33
  162.2 9.1 %all_to_all.5 = f32[8,2,16,128]{3,2,1,0:T(8,128)S(1)} all-to-all(f32[8,2,16,128]{3,2,1,0:T(8,128)S(1)} %shard_map.51), channel_id=1, replica_groups=mesh['vir'=8,'out'=4] {'vir'}, dimensions={0} | all-to-all | bytes 262144 | tf_op jit(solution)/shard_map/all_to_all | solution.py:363
  171.2 0.6 reduce_sum.9
  (8 shorter events, 0.0 us)
Async XLA Ops:
  1.0 15.9 %collective-permute-start.1 = (bf16[2,64,1536]{2,1,0:T(8,128)(2,1)S(1)}, bf16[2,64,1536]{2,1,0:T(8,128)(2,1)S(1)}, u32[]{:S(2)}, u32[]{:S(2)}) collective-permute-start(bf16[2,64,1536]{2,1,0:T(8,128)(2,1)S(1)} %slice.9), channel_id=1, source_target_pairs={{0,3},{4,7},{8,11},{12,15},{16,19},{20,23},{24,27},{28,31}} | collective-permute-start | bytes 1179656 | tf_op jit(solution)/shard_map/ppermute | solution.py:278
  1.7 23.6 %collective-permute-start.2 = (bf16[2,64,1536]{2,1,0:T(8,128)(2,1)S(1)}, bf16[2,64,1536]{2,1,0:T(8,128)(2,1)S(1)}, u32[]{:S(2)}, u32[]{:S(2)}) collective-permute-start(bf16[2,64,1536]{2,1,0:T(8,128)(2,1)S(1)} %slice.9), channel_id=1, source_target_pairs={{0,2},{4,6},{8,10},{12,14},{16,18},{20,22},{24,26},{28,30}} | collective-permute-start | bytes 1179656 | tf_op jit(solution)/shard_map/ppermute | solution.py:278
  3.0 22.3 %collective-permute-start.3 = (bf16[2,64,1536]{2,1,0:T(8,128)(2,1)S(1)}, bf16[2,64,1536]{2,1,0:T(8,128)(2,1)S(1)}, u32[]{:S(2)}, u32[]{:S(2)}) collective-permute-start(bf16[2,64,1536]{2,1,0:T(8,128)(2,1)S(1)} %slice.9), channel_id=1, source_target_pairs={{0,1},{4,5},{8,9},{12,13},{16,17},{20,21},{24,25},{28,29}} | collective-permute-start | bytes 1179656 | tf_op jit(solution)/shard_map/ppermute | solution.py:278
  3.7 113.2 %collective-permute-start.8 = (bf16[32,64,512]{2,1,0:T(8,128)(2,1)}, bf16[32,64,512]{2,1,0:T(8,128)(2,1)}, u32[]{:S(2)}, u32[]{:S(2)}) collective-permute-start(bf16[32,64,512]{2,1,0:T(8,128)(2,1)} %param.4), channel_id=1, source_target_pairs={{2,0},{1,3},{6,4},{5,7},{10,8},{9,11},{14,12},{13,15},{18,16},{17,... | collective-permute-start | bytes 6291464 | tf_op jit(solution)/shard_map/ppermute | solution.py:309
  17.0 66.0 %collective-permute-start = (bf16[64,32,512]{2,1,0:T(8,128)(2,1)}, bf16[64,32,512]{2,1,0:T(8,128)(2,1)}, u32[]{:S(2)}, u32[]{:S(2)}) collective-permute-start(bf16[64,32,512]{2,1,0:T(8,128)(2,1)} %bitcast.13.refs_2_.refs_0_), channel_id=1, source_target_pairs={{3,1},{1,0},{0,2},{2,3},{7,5},{5,4},{4,6},{6,7},{11,9},{9,8},{8,10... | collective-permute-start | bytes 6291464 | tf_op jit(solution)/shard_map/ppermute | solution.py:309
  26.4 12.1 %collective-permute-start.4 = (bf16[2,64,1536]{2,1,0:T(8,128)(2,1)S(1)}, bf16[2,64,1536]{2,1,0:T(8,128)(2,1)S(1)}, u32[]{:S(2)}, u32[]{:S(2)}) collective-permute-start(bf16[2,64,1536]{2,1,0:T(8,128)(2,1)S(1)} %select_select_fusion.refs_0_), channel_id=1, source_target_pairs={{0,8},{4,12},{8,0},{12,4},{16,24},{20,28},{24,16},{28,20},{1,9},{5... | collective-permute-start | bytes 1179656 | tf_op jit(solution)/shard_map/ppermute | solution.py:288
  27.9 17.0 %collective-permute-start.5 = (bf16[2,64,1536]{2,1,0:T(8,128)(2,1)S(1)}, bf16[2,64,1536]{2,1,0:T(8,128)(2,1)S(1)}, u32[]{:S(2)}, u32[]{:S(2)}) collective-permute-start(bf16[2,64,1536]{2,1,0:T(8,128)(2,1)S(1)} %select_select_fusion.refs_0_), channel_id=1, source_target_pairs={{0,16},{4,20},{8,24},{12,28},{16,0},{20,4},{24,8},{28,12},{1,17},{... | collective-permute-start | bytes 1179656 | tf_op jit(solution)/shard_map/ppermute | solution.py:288
  29.5 15.5 %collective-permute-start.6 = (bf16[2,64,1536]{2,1,0:T(8,128)(2,1)S(1)}, bf16[2,64,1536]{2,1,0:T(8,128)(2,1)S(1)}, u32[]{:S(2)}, u32[]{:S(2)}) collective-permute-start(bf16[2,64,1536]{2,1,0:T(8,128)(2,1)S(1)} %select_select_fusion.refs_0_), channel_id=1, source_target_pairs={{0,24},{4,28},{8,16},{12,20},{16,8},{20,12},{24,0},{28,4},{1,25},{... | collective-permute-start | bytes 1179656 | tf_op jit(solution)/shard_map/ppermute | solution.py:288
  46.2 5.5 %collective-permute-start.7 = (bf16[4,2,64,1536]{3,2,1,0:T(8,128)(2,1)}, bf16[4,2,64,1536]{3,2,1,0:T(8,128)(2,1)S(1)}, u32[]{:S(2)}, u32[]{:S(2)}) collective-permute-start(bf16[4,2,64,1536]{3,2,1,0:T(8,128)(2,1)} %get-tuple-element.26.refs_1_), channel_id=1, source_target_pairs={{0,4},{4,0},{8,12},{12,8},{16,20},{20,16},{24,28},{28,24},{1,5},{5... | collective-permute-start | bytes 4718600 | tf_op jit(solution)/shard_map/ppermute | solution.py:288
  46.2 6.7 %copy-start.1 = (bf16[4,2,64,1536]{3,2,1,0:T(8,128)(2,1)S(1)}, bf16[4,2,64,1536]{3,2,1,0:T(8,128)(2,1)}, u32[]{:S(2)}) copy-start(bf16[4,2,64,1536]{3,2,1,0:T(8,128)(2,1)} %get-tuple-element.26.refs_1_) | copy-start | bytes 4718596
  51.8 1.1 copy-start.9
  85.6 1.2 copy-start
  88.0 0.8 copy-start.4
  88.8 0.6 copy-start.5
  89.4 57.5 %collective-permute-start.9 = (bf16[48,32,512]{2,1,0:T(8,128)(2,1)}, bf16[48,32,512]{2,1,0:T(8,128)(2,1)S(1)}, u32[]{:S(2)}, u32[]{:S(2)}) collective-permute-start(bf16[48,32,512]{2,1,0:T(8,128)(2,1)} %get-tuple-element.43), channel_id=1, source_target_pairs={{1,0},{0,1},{2,3},{3,2},{5,4},{4,5},{6,7},{7,6},{9,8},{8,9},{10,11... | collective-permute-start | bytes 4718600 | tf_op jit(solution)/shard_map/ppermute | solution.py:309
  89.4 58.7 %collective-permute-start.10 = (bf16[48,32,512]{2,1,0:T(8,128)(2,1)}, bf16[48,32,512]{2,1,0:T(8,128)(2,1)}, u32[]{:S(2)}, u32[]{:S(2)}) collective-permute-start(bf16[48,32,512]{2,1,0:T(8,128)(2,1)} %get-tuple-element.44), channel_id=1, source_target_pairs={{2,1},{1,2},{6,5},{5,6},{10,9},{9,10},{14,13},{13,14},{18,17},{17,... | collective-permute-start | bytes 4718600 | tf_op jit(solution)/shard_map/ppermute | solution.py:309
  100.4 0.7 copy-start.6
  112.5 0.6 copy-start.7
  113.1 45.0 %collective-permute-start.11 = (bf16[16,32,512]{2,1,0:T(8,128)(2,1)}, bf16[16,32,512]{2,1,0:T(8,128)(2,1)S(1)}, u32[]{:S(2)}, u32[]{:S(2)}) collective-permute-start(bf16[16,32,512]{2,1,0:T(8,128)(2,1)} %get-tuple-element.45), channel_id=1, source_target_pairs={{1,0},{0,1},{2,3},{3,2},{5,4},{4,5},{6,7},{7,6},{9,8},{8,9},{10,11... | collective-permute-start | bytes 1572872 | tf_op jit(solution)/shard_map/ppermute | solution.py:309
  113.1 46.0 %collective-permute-start.12 = (bf16[16,32,512]{2,1,0:T(8,128)(2,1)}, bf16[16,32,512]{2,1,0:T(8,128)(2,1)S(1)}, u32[]{:S(2)}, u32[]{:S(2)}) collective-permute-start(bf16[16,32,512]{2,1,0:T(8,128)(2,1)} %get-tuple-element.46), channel_id=1, source_target_pairs={{2,1},{1,2},{6,5},{5,6},{10,9},{9,10},{14,13},{13,14},{18,17},{17,... | collective-permute-start | bytes 1572872 | tf_op jit(solution)/shard_map/ppermute | solution.py:309
  117.0 0.7 copy-start.8
  146.8 1.2 copy-start.2
  148.0 1.4 copy-start.3

commit v8 on v7

--- a/solution.py
+++ b/solution.py
@@ -275,8 +275,8 @@
 
 
 def spread(rows, n, z):
-    heres = [lax.ppermute(rows, "out", [(0, k)]) for k in range(1, n)]
-    for k, here in zip(range(1, n), heres):
+    heres = [lax.ppermute(rows, "out", [(0, k)]) for k in range(n - 1, 0, -1)]
+    for k, here in zip(range(n - 1, 0, -1), heres):
         rows = jnp.where(z == k, here, rows)
     return rows
 

time: 173 us -> 175 us (1.012)
  waiting for transfers between devices: 36.9 us -> 39.3 us
    ppermute x6, waiting for transfers between devices: 13.6 us -> 16.7 us  [send(): return lax.ppermute(array, 'out', ways)]
  transfers between devices with their start and end apart: 13 -> 13, of which waited for: 6 -> 6; matrix products, arithmetic and copies ran while one was open for 6% -> 6% of each run, Pallas kernels for 42% -> 41%
where the time goes in v8:
time: 175 us; the launch traced here: 174 us
  Pallas kernels  74.9 us (43%)
  waiting for transfers between devices  39.3 us (22%)
  starting transfers between devices  29.8 us (17%)
  local copies, waits for them, and re-layouts  18.9 us (11%)
  blocking collectives  9.07 us (5%)
    pallas_call x11, Pallas kernels, call(): pl.pallas_call(run, grid=grid, in_specs=list(in_specs) + [anywhere] * n_t...  74.9 us
    ppermute x6, starting transfers between devices, send(): return lax.ppermute(array, 'out', ways)  23.6 us
    ppermute x6, waiting for transfers between devices, send(): return lax.ppermute(array, 'out', ways)  16.7 us
    ppermute x4, waiting for transfers between devices, swap(): return lax.ppermute(array, 'vir', [(k, k ^ mask) for k in range(vir)])  14.9 us
    unnamed x21, local copies, waits for them, and re-layouts  12.4 us
    all_to_all x1, blocking collectives, body(): swapped = lax.all_to_all(parts, 'vir', split_axis=0, concat_axis=0)  9.07 us
    ppermute x3, waiting for transfers between devices, spread(): heres = [lax.ppermute(rows, 'out', [(0, k)]) for k in range(n - 1, 0, -1)]  7.62 us
    slice x2, local copies, waits for them, and re-layouts, body(): onward, kept = ([], [own[i:j] for i, j in spans])  4.76 us
  transfers between devices with their start and end apart: 13, of which 6 were waited for; matrix products, arithmetic and copies ran while one was open for 6% of the time, Pallas kernels for 41%

profile of v8, /device:TPU:16, one launch (start us, length us, event | category | flops | bytes accessed | tf_op | source)
XLA Modules:
  0.0 173.9 jit_solution(9124737683563368548)
XLA Ops:
  0.0 1.0 slice.9
  1.0 0.7 collective-permute-start.1
  1.7 1.3 collective-permute-start.2
  3.0 0.7 collective-permute-start.3
  3.7 7.9 %collective-permute-start.8 = (bf16[32,64,512]{2,1,0:T(8,128)(2,1)}, bf16[32,64,512]{2,1,0:T(8,128)(2,1)}, u32[]{:S(2)}, u32[]{:S(2)}) collective-permute-start(bf16[32,64,512]{2,1,0:T(8,128)(2,1)} %param.4), channel_id=1, source_target_pairs={{2,0},{1,3},{6,4},{5,7},{10,8},{9,11},{14,12},{13,15},{18,16},{17,... | collective-permute-start | bytes 6291464 | tf_op jit(solution)/shard_map/ppermute | solution.py:309
  11.6 4.1 %copy.22 = bf16[32,64,512]{2,0,1:T(8,128)(2,1)} copy(bf16[32,64,512]{2,1,0:T(8,128)(2,1)} %param.4) | data formatting | bytes 4194304 | tf_op args[1]
  15.7 0.0 collective-permute-start
  15.7 0.0 collective-permute-done.1
  15.7 7.6 %collective-permute-done.2 = bf16[2,64,1536]{2,1,0:T(8,128)(2,1)S(1)} collective-permute-done((bf16[2,64,1536]{2,1,0:T(8,128)(2,1)S(1)}, bf16[2,64,1536]{2,1,0:T(8,128)(2,1)S(1)}, u32[]{:S(2)}, u32[]{:S(2)}) %collective-permute-start.2) | collective-permute-done | bytes 393248 | tf_op jit(solution)/shard_map/ppermute | solution.py:278
  23.3 0.0 collective-permute-done.3
  23.3 1.1 select_select_fusion.refs_0_
  24.4 1.6 collective-permute-start.4
  26.0 1.5 collective-permute-start.5
  27.5 0.5 collective-permute-start.6
  28.0 8.6 %collective-permute-done.4.refs_1_ = bf16[2,64,1536]{2,1,0:T(8,128)(2,1)S(1)} collective-permute-done((bf16[2,64,1536]{2,1,0:T(8,128)(2,1)S(1)}, bf16[2,64,1536]{2,1,0:T(8,128)(2,1)S(1)}, u32[]{:S(2)}, u32[]{:S(2)}) %collective-permute-start.4) | collective-permute-done | bytes 393248 | tf_op jit(solution)/shard_map/ppermute | solution.py:288
  36.5 6.4 %collective-permute-done.5.refs_2_ = bf16[2,64,1536]{2,1,0:T(8,128)(2,1)S(1)} collective-permute-done((bf16[2,64,1536]{2,1,0:T(8,128)(2,1)S(1)}, bf16[2,64,1536]{2,1,0:T(8,128)(2,1)S(1)}, u32[]{:S(2)}, u32[]{:S(2)}) %collective-permute-start.5) | collective-permute-done | bytes 393248 | tf_op jit(solution)/shard_map/ppermute | solution.py:288
  42.9 0.0 collective-permute-done.6.refs_3_
  42.9 1.3 shard_map.37
  44.2 0.0 collective-permute-start.7
  44.2 0.0 copy-start.1
  44.2 2.9 %slice.12.refs_2_ = bf16[48,32,512]{2,1,0:T(8,128)(2,1)} slice(bf16[64,32,512]{2,1,0:T(8,128)(2,1)} %bitcast.13.refs_2_.refs_0_), slice={[0:48], [0:32], [0:512]} | slice | bytes 3145728 | tf_op jit(solution)/shard_map/slice | solution.py:329
  47.1 1.9 %slice.13.refs_2_ = bf16[16,32,512]{2,1,0:T(8,128)(2,1)} slice(bf16[64,32,512]{2,1,0:T(8,128)(2,1)} %bitcast.13.refs_2_.refs_0_), slice={[48:64], [0:32], [0:512]} | slice | bytes 1048576 | tf_op jit(solution)/shard_map/slice | solution.py:329
  49.0 0.1 stack.35.refs_0_
  49.1 0.7 dynamic-slice_bitcast_fusion.refs_0_
  49.7 0.0 collective-permute-done.7.refs_2_
  49.7 0.0 copy-start.9
  49.7 1.1 copy-done.9
  50.9 0.0 copy-done.1
  50.9 4.1 %shard_map.38 = (bf16[2,1536,512]{2,1,0:T(8,128)(2,1)}, f32[8,128]{1,0:T(8,128)S(1)}) custom-call(s32[8]{0:T(128)S(1)} %stack.35.refs_0_, bf16[4,2,64,1536]{3,2,1,0:T(8,128)(2,1)S(1)} %copy-done.1, bf16[4,2,64,1536]{3,2,1,0:T(8,128)(2,1)} %copy-done.9, f32[8,128]{1,0:T(8,128)S(1)} %get-tuple-element.27.refs_3_), custom_call_target="tpu_custom_call", output_to_operand_aliasing={{1}: (3, {})} | custom-call | flops 1024 | bytes 1024 | tf_op jit(solution)/shard_map/pallas_call | solution.py:33
  55.0 25.9 %shard_map.39 = (bf16[48,2,128,512]{3,2,1,0:T(8,128)(2,1)}, f32[8,128]{1,0:T(8,128)S(1)}) custom-call(bf16[128,64,1536]{2,1,0:T(8,128)(2,1)} %refs_0_.3, bf16[2,1536,512]{2,1,0:T(8,128)(2,1)} %get-tuple-element.28.refs_1_, f32[8,128]{1,0:T(8,128)S(1)} %get-tuple-element.29.refs_2_), custom_call_target="tpu_custom_call", output_to_operand_aliasing={{1}: (2, {})} | custom-call | flops 1024 | bytes 1024 | tf_op jit(solution)/shard_map/pallas_call | solution.py:33
  80.9 0.0 collective-permute-done.refs_1_
  80.9 2.6 %shard_map.40 = (bf16[48,32,512]{2,1,0:T(8,128)(2,1)S(1)}, f32[8,128]{1,0:T(8,128)S(1)}) custom-call(s32[1]{0:T(128)} %bitcast.10.refs_0_, bf16[64,32,512]{2,1,0:T(8,128)(2,1)} %collective-permute-done.refs_1_, bf16[64,32,512]{2,1,0:T(8,128)(2,1)} %bitcast.13.refs_2_.refs_0_, f32[8,128]{1,0:T(8,128)S(1)} %get-tuple-element.30.refs_3_), custom_call_target="tpu_custom_call", output_to_operand_aliasing={{1}: (3, {})} | custom-call | flops 1024 | bytes 1024 | tf_op jit(solution)/shard_map/pallas_call | solution.py:33
  83.5 0.0 copy-start
  83.5 1.2 copy-done
  84.7 1.2 shard_map.41
  85.9 0.0 copy-start.4
  85.9 0.8 copy-done.4
  86.7 0.0 copy-start.5
  86.8 0.6 copy-done.5
  87.3 9.9 %collective-permute-start.9 = (bf16[48,32,512]{2,1,0:T(8,128)(2,1)}, bf16[48,32,512]{2,1,0:T(8,128)(2,1)S(1)}, u32[]{:S(2)}, u32[]{:S(2)}) collective-permute-start(bf16[48,32,512]{2,1,0:T(8,128)(2,1)} %get-tuple-element.43), channel_id=1, source_target_pairs={{1,0},{0,1},{2,3},{3,2},{5,4},{4,5},{6,7},{7,6},{9,8},{8,9},{10,11... | collective-permute-start | bytes 4718600 | tf_op jit(solution)/shard_map/ppermute | solution.py:309
  97.3 1.9 %collective-permute-start.10 = (bf16[48,32,512]{2,1,0:T(8,128)(2,1)}, bf16[48,32,512]{2,1,0:T(8,128)(2,1)}, u32[]{:S(2)}, u32[]{:S(2)}) collective-permute-start(bf16[48,32,512]{2,1,0:T(8,128)(2,1)} %get-tuple-element.44), channel_id=1, source_target_pairs={{2,1},{1,2},{6,5},{5,6},{10,9},{9,10},{14,13},{13,14},{18,17},{17,... | collective-permute-start | bytes 4718600 | tf_op jit(solution)/shard_map/ppermute | solution.py:309
  99.2 0.0 copy-start.6
  99.2 0.7 copy-done.6
  99.9 11.4 %shard_map.43 = (bf16[16,2,128,512]{3,2,1,0:T(8,128)(2,1)}, f32[8,128]{1,0:T(8,128)S(1)}) custom-call(bf16[128,64,1536]{2,1,0:T(8,128)(2,1)} %refs_0_.3, bf16[2,1536,512]{2,1,0:T(8,128)(2,1)} %get-tuple-element.28.refs_1_, f32[8,128]{1,0:T(8,128)S(1)} %copy-done.6), custom_call_target="tpu_custom_call", output_to_operand_aliasing={{1}: (2, {})} | custom-call | flops 1024 | bytes 1024 | tf_op jit(solution)/shard_map/pallas_call | solution.py:33
  111.3 0.0 copy-start.7
  111.3 0.6 copy-done.7
  111.9 0.0 collective-permute-start.11
  111.9 3.9 %collective-permute-start.12 = (bf16[16,32,512]{2,1,0:T(8,128)(2,1)}, bf16[16,32,512]{2,1,0:T(8,128)(2,1)S(1)}, u32[]{:S(2)}, u32[]{:S(2)}) collective-permute-start(bf16[16,32,512]{2,1,0:T(8,128)(2,1)} %get-tuple-element.46), channel_id=1, source_target_pairs={{2,1},{1,2},{6,5},{5,6},{10,9},{9,10},{14,13},{13,14},{18,17},{17,... | collective-permute-start | bytes 1572872 | tf_op jit(solution)/shard_map/ppermute | solution.py:309
  115.8 0.0 collective-permute-done.8.refs_1_
  115.8 0.0 copy-start.8
  115.8 0.7 copy-done.8
  116.5 4.3 %shard_map.46 = (bf16[64,32,512]{2,1,0:T(8,128)(2,1)}, f32[8,128]{1,0:T(8,128)S(1)}) custom-call(bf16[32,64,512]{2,1,0:T(8,128)(2,1)} %get-tuple-element.38.refs_0_, f32[8,128]{1,0:T(8,128)S(1)} %copy-done.8), custom_call_target="tpu_custom_call", output_to_operand_aliasing={{1}: (1, {})} | custom-call | flops 1024 | bytes 1024 | tf_op jit(solution)/shard_map/pallas_call | solution.py:33
  120.8 3.5 %shard_map.48 = f32[96,256]{1,0:T(8,128)S(1)} custom-call(bf16[64,32,512]{2,1,0:T(8,128)(2,1)} %bitcast.13.refs_2_.refs_0_, bf16[64,32,512]{2,1,0:T(8,128)(2,1)} %collective-permute-done.refs_1_, bf16[64,32,512]{2,1,0:T(8,128)(2,1)} %get-tuple-element.40.refs_2_, bf16[16,2,128,512]{3,2,1,0:T(8,128)(2,1)} %get-tuple-element.42.refs_3_.refs_5_), custom_call_target="tpu_custom_call" | custom-call | flops 1024 | bytes 1024 | tf_op jit(solution)/shard_map/pallas_call | solution.py:33
  124.3 9.0 %shard_map.47 = f32[96,256]{1,0:T(8,128)S(1)} custom-call(bf16[64,32,512]{2,1,0:T(8,128)(2,1)} %bitcast.13.refs_2_.refs_0_, bf16[64,32,512]{2,1,0:T(8,128)(2,1)} %collective-permute-done.refs_1_, bf16[64,32,512]{2,1,0:T(8,128)(2,1)} %get-tuple-element.40.refs_2_, bf16[48,2,128,512]{3,2,1,0:T(8,128)(2,1)} %get-tuple-element.41.refs_3_.refs_2_), custom_call_target="tpu_custom_call" | custom-call | flops 1024 | bytes 1024 | tf_op jit(solution)/shard_map/pallas_call | solution.py:33
  133.4 15.5 %collective-permute-done.9.refs_0_ = bf16[48,32,512]{2,1,0:T(8,128)(2,1)S(1)} collective-permute-done((bf16[48,32,512]{2,1,0:T(8,128)(2,1)}, bf16[48,32,512]{2,1,0:T(8,128)(2,1)S(1)}, u32[]{:S(2)}, u32[]{:S(2)}) %collective-permute-start.9) | collective-permute-done | bytes 1572896 | tf_op jit(solution)/shard_map/ppermute | solution.py:309
  148.9 1.2 copy-done.2
  150.1 1.0 collective-permute-done.10.refs_1_
  151.0 1.4 copy-done.3
  152.5 8.3 %shard_map.50.refs_2_ = f32[64,256]{1,0:T(8,128)S(1)} custom-call(bf16[48,32,512]{2,1,0:T(8,128)(2,1)S(1)} %copy-done.3, bf16[48,32,512]{2,1,0:T(8,128)(2,1)} %collective-permute-done.10.refs_1_, bf16[48,2,128,512]{3,2,1,0:T(8,128)(2,1)} %get-tuple-element.41.refs_3_.refs_2_), custom_call_target="tpu_custom_call" | custom-call | flops 1024 | bytes 1024 | tf_op jit(solution)/shard_map/pallas_call | solution.py:33
  160.7 0.0 collective-permute-done.11.refs_3_
  160.8 0.3 collective-permute-done.12.refs_4_
  161.0 3.1 %shard_map.51 = f32[8,2,16,128]{3,2,1,0:T(8,128)S(1)} custom-call(s32[4]{0:T(128)S(1)} %dynamic-slice_bitcast_fusion.refs_0_, f32[96,256]{1,0:T(8,128)S(1)} %add.7.refs_1_, f32[64,256]{1,0:T(8,128)S(1)} %shard_map.50.refs_2_, bf16[16,32,512]{2,1,0:T(8,128)(2,1)S(1)} %collective-permute-done.11.refs_3_, ...), custom_call_target="tpu_custom_call" | custom-call | flops 1024 | bytes 1024 | tf_op jit(solution)/shard_map/pallas_call | solution.py:33
  164.2 9.1 %all_to_all.5 = f32[8,2,16,128]{3,2,1,0:T(8,128)S(1)} all-to-all(f32[8,2,16,128]{3,2,1,0:T(8,128)S(1)} %shard_map.51), channel_id=1, replica_groups=mesh['vir'=8,'out'=4] {'vir'}, dimensions={0} | all-to-all | bytes 262144 | tf_op jit(solution)/shard_map/all_to_all | solution.py:363
  173.2 0.6 reduce_sum.9
  (8 shorter events, 0.0 us)
Async XLA Ops:
  1.0 14.7 %collective-permute-start.1 = (bf16[2,64,1536]{2,1,0:T(8,128)(2,1)S(1)}, bf16[2,64,1536]{2,1,0:T(8,128)(2,1)S(1)}, u32[]{:S(2)}, u32[]{:S(2)}) collective-permute-start(bf16[2,64,1536]{2,1,0:T(8,128)(2,1)S(1)} %slice.9), channel_id=1, source_target_pairs={{0,1},{4,5},{8,9},{12,13},{16,17},{20,21},{24,25},{28,29}} | collective-permute-start | bytes 1179656 | tf_op jit(solution)/shard_map/ppermute | solution.py:278
  1.7 21.6 %collective-permute-start.2 = (bf16[2,64,1536]{2,1,0:T(8,128)(2,1)S(1)}, bf16[2,64,1536]{2,1,0:T(8,128)(2,1)S(1)}, u32[]{:S(2)}, u32[]{:S(2)}) collective-permute-start(bf16[2,64,1536]{2,1,0:T(8,128)(2,1)S(1)} %slice.9), channel_id=1, source_target_pairs={{0,2},{4,6},{8,10},{12,14},{16,18},{20,22},{24,26},{28,30}} | collective-permute-start | bytes 1179656 | tf_op jit(solution)/shard_map/ppermute | solution.py:278
  3.0 20.3 %collective-permute-start.3 = (bf16[2,64,1536]{2,1,0:T(8,128)(2,1)S(1)}, bf16[2,64,1536]{2,1,0:T(8,128)(2,1)S(1)}, u32[]{:S(2)}, u32[]{:S(2)}) collective-permute-start(bf16[2,64,1536]{2,1,0:T(8,128)(2,1)S(1)} %slice.9), channel_id=1, source_target_pairs={{0,3},{4,7},{8,11},{12,15},{16,19},{20,23},{24,27},{28,31}} | collective-permute-start | bytes 1179656 | tf_op jit(solution)/shard_map/ppermute | solution.py:278
  3.7 112.1 %collective-permute-start.8 = (bf16[32,64,512]{2,1,0:T(8,128)(2,1)}, bf16[32,64,512]{2,1,0:T(8,128)(2,1)}, u32[]{:S(2)}, u32[]{:S(2)}) collective-permute-start(bf16[32,64,512]{2,1,0:T(8,128)(2,1)} %param.4), channel_id=1, source_target_pairs={{2,0},{1,3},{6,4},{5,7},{10,8},{9,11},{14,12},{13,15},{18,16},{17,... | collective-permute-start | bytes 6291464 | tf_op jit(solution)/shard_map/ppermute | solution.py:309
  15.7 65.2 %collective-permute-start = (bf16[64,32,512]{2,1,0:T(8,128)(2,1)}, bf16[64,32,512]{2,1,0:T(8,128)(2,1)}, u32[]{:S(2)}, u32[]{:S(2)}) collective-permute-start(bf16[64,32,512]{2,1,0:T(8,128)(2,1)} %bitcast.13.refs_2_.refs_0_), channel_id=1, source_target_pairs={{3,1},{1,0},{0,2},{2,3},{7,5},{5,4},{4,6},{6,7},{11,9},{9,8},{8,10... | collective-permute-start | bytes 6291464 | tf_op jit(solution)/shard_map/ppermute | solution.py:309
  24.4 12.1 %collective-permute-start.4 = (bf16[2,64,1536]{2,1,0:T(8,128)(2,1)S(1)}, bf16[2,64,1536]{2,1,0:T(8,128)(2,1)S(1)}, u32[]{:S(2)}, u32[]{:S(2)}) collective-permute-start(bf16[2,64,1536]{2,1,0:T(8,128)(2,1)S(1)} %select_select_fusion.refs_0_), channel_id=1, source_target_pairs={{0,8},{4,12},{8,0},{12,4},{16,24},{20,28},{24,16},{28,20},{1,9},{5... | collective-permute-start | bytes 1179656 | tf_op jit(solution)/shard_map/ppermute | solution.py:288
  26.0 16.9 %collective-permute-start.5 = (bf16[2,64,1536]{2,1,0:T(8,128)(2,1)S(1)}, bf16[2,64,1536]{2,1,0:T(8,128)(2,1)S(1)}, u32[]{:S(2)}, u32[]{:S(2)}) collective-permute-start(bf16[2,64,1536]{2,1,0:T(8,128)(2,1)S(1)} %select_select_fusion.refs_0_), channel_id=1, source_target_pairs={{0,16},{4,20},{8,24},{12,28},{16,0},{20,4},{24,8},{28,12},{1,17},{... | collective-permute-start | bytes 1179656 | tf_op jit(solution)/shard_map/ppermute | solution.py:288
  27.5 15.4 %collective-permute-start.6 = (bf16[2,64,1536]{2,1,0:T(8,128)(2,1)S(1)}, bf16[2,64,1536]{2,1,0:T(8,128)(2,1)S(1)}, u32[]{:S(2)}, u32[]{:S(2)}) collective-permute-start(bf16[2,64,1536]{2,1,0:T(8,128)(2,1)S(1)} %select_select_fusion.refs_0_), channel_id=1, source_target_pairs={{0,24},{4,28},{8,16},{12,20},{16,8},{20,12},{24,0},{28,4},{1,25},{... | collective-permute-start | bytes 1179656 | tf_op jit(solution)/shard_map/ppermute | solution.py:288
  44.2 5.5 %collective-permute-start.7 = (bf16[4,2,64,1536]{3,2,1,0:T(8,128)(2,1)}, bf16[4,2,64,1536]{3,2,1,0:T(8,128)(2,1)S(1)}, u32[]{:S(2)}, u32[]{:S(2)}) collective-permute-start(bf16[4,2,64,1536]{3,2,1,0:T(8,128)(2,1)} %get-tuple-element.26.refs_1_), channel_id=1, source_target_pairs={{0,4},{4,0},{8,12},{12,8},{16,20},{20,16},{24,28},{28,24},{1,5},{5... | collective-permute-start | bytes 4718600 | tf_op jit(solution)/shard_map/ppermute | solution.py:288
  44.2 6.7 %copy-start.1 = (bf16[4,2,64,1536]{3,2,1,0:T(8,128)(2,1)S(1)}, bf16[4,2,64,1536]{3,2,1,0:T(8,128)(2,1)}, u32[]{:S(2)}) copy-start(bf16[4,2,64,1536]{3,2,1,0:T(8,128)(2,1)} %get-tuple-element.26.refs_1_) | copy-start | bytes 4718596
  49.7 1.1 copy-start.9
  83.5 1.2 copy-start
  85.9 0.8 copy-start.4
  86.7 0.6 copy-start.5
  87.3 61.5 %collective-permute-start.9 = (bf16[48,32,512]{2,1,0:T(8,128)(2,1)}, bf16[48,32,512]{2,1,0:T(8,128)(2,1)S(1)}, u32[]{:S(2)}, u32[]{:S(2)}) collective-permute-start(bf16[48,32,512]{2,1,0:T(8,128)(2,1)} %get-tuple-element.43), channel_id=1, source_target_pairs={{1,0},{0,1},{2,3},{3,2},{5,4},{4,5},{6,7},{7,6},{9,8},{8,9},{10,11... | collective-permute-start | bytes 4718600 | tf_op jit(solution)/shard_map/ppermute | solution.py:309
  97.3 53.8 %collective-permute-start.10 = (bf16[48,32,512]{2,1,0:T(8,128)(2,1)}, bf16[48,32,512]{2,1,0:T(8,128)(2,1)}, u32[]{:S(2)}, u32[]{:S(2)}) collective-permute-start(bf16[48,32,512]{2,1,0:T(8,128)(2,1)} %get-tuple-element.44), channel_id=1, source_target_pairs={{2,1},{1,2},{6,5},{5,6},{10,9},{9,10},{14,13},{13,14},{18,17},{17,... | collective-permute-start | bytes 4718600 | tf_op jit(solution)/shard_map/ppermute | solution.py:309
  99.2 0.7 copy-start.6
  111.3 0.6 copy-start.7
  111.9 48.9 %collective-permute-start.11 = (bf16[16,32,512]{2,1,0:T(8,128)(2,1)}, bf16[16,32,512]{2,1,0:T(8,128)(2,1)S(1)}, u32[]{:S(2)}, u32[]{:S(2)}) collective-permute-start(bf16[16,32,512]{2,1,0:T(8,128)(2,1)} %get-tuple-element.45), channel_id=1, source_target_pairs={{1,0},{0,1},{2,3},{3,2},{5,4},{4,5},{6,7},{7,6},{9,8},{8,9},{10,11... | collective-permute-start | bytes 1572872 | tf_op jit(solution)/shard_map/ppermute | solution.py:309
  111.9 49.1 %collective-permute-start.12 = (bf16[16,32,512]{2,1,0:T(8,128)(2,1)}, bf16[16,32,512]{2,1,0:T(8,128)(2,1)S(1)}, u32[]{:S(2)}, u32[]{:S(2)}) collective-permute-start(bf16[16,32,512]{2,1,0:T(8,128)(2,1)} %get-tuple-element.46), channel_id=1, source_target_pairs={{2,1},{1,2},{6,5},{5,6},{10,9},{9,10},{14,13},{13,14},{18,17},{17,... | collective-permute-start | bytes 1572872 | tf_op jit(solution)/shard_map/ppermute | solution.py:309
  115.8 0.7 copy-start.8
  148.9 1.2 copy-start.2
  151.0 1.4 copy-start.3

commit v9 on v7

--- a/solution.py
+++ b/solution.py
@@ -224,10 +224,10 @@
                 out_ref[j, b] = all_ref[pl.ds(start, rows), b * a_rows : (b + 1) * a_rows]
 
 
-def ladder_specs(taus, integral):
+def ladder_specs(taus, integral, limit=8):
     _, pairs, d_len = taus[0][0].shape
     c_rows, bb, a_rows, _ = integral.shape
-    c_len = largest_part(c_rows, 8)
+    c_len = largest_part(c_rows, limit)
     specs = [
         pl.BlockSpec((c_len, pairs, d_len), lambda i, k=start // c_len: (k + i, 0, 0))
         for _, start in taus
@@ -252,7 +252,7 @@
 
 
 def ladder_late(slots, early, added, taus, integral, owners):
-    specs, shape, grid = ladder_specs(taus, integral)
+    specs, shape, grid = ladder_specs(taus, integral, 4)
     pairs = taus[0][0].shape[1]
     _, bb, a_rows, _ = integral.shape
     out = (owners, bb, slots.shape[0] * pairs // owners, a_rows)

time: 173 us -> 174 us (level)
  no operation moved by 1% of the time
where the time goes in v9:
time: 174 us; the launch traced here: 173 us
  Pallas kernels  75.7 us (44%)
  waiting for transfers between devices  36.9 us (21%)
  starting transfers between devices  30.2 us (17%)
  local copies, waits for them, and re-layouts  18.9 us (11%)
  blocking collectives  9.05 us (5%)
    pallas_call x11, Pallas kernels, call(): pl.pallas_call(run, grid=grid, in_specs=list(in_specs) + [anywhere] * n_t...  75.7 us
    ppermute x6, starting transfers between devices, send(): return lax.ppermute(array, 'out', ways)  24 us
    ppermute x4, waiting for transfers between devices, swap(): return lax.ppermute(array, 'vir', [(k, k ^ mask) for k in range(vir)])  15 us
    ppermute x6, waiting for transfers between devices, send(): return lax.ppermute(array, 'out', ways)  13.6 us
    unnamed x21, local copies, waits for them, and re-layouts  12.4 us
    all_to_all x1, blocking collectives, body(): swapped = lax.all_to_all(parts, 'vir', split_axis=0, concat_axis=0)  9.05 us
    ppermute x3, waiting for transfers between devices, spread(): heres = [lax.ppermute(rows, 'out', [(0, k)]) for k in range(1, n)]  8.33 us
    slice x2, local copies, waits for them, and re-layouts, body(): onward, kept = ([], [own[i:j] for i, j in spans])  4.76 us
  transfers between devices with their start and end apart: 13, of which 6 were waited for; matrix products, arithmetic and copies ran while one was open for 6% of the time, Pallas kernels for 42%

profile of v9, /device:TPU:16, one launch (start us, length us, event | category | flops | bytes accessed | tf_op | source)
XLA Modules:
  0.0 172.7 jit_solution(12640218800477854065)
XLA Ops:
  0.0 1.0 slice.9
  1.0 0.7 collective-permute-start.1
  1.7 1.3 collective-permute-start.2
  3.0 0.7 collective-permute-start.3
  3.7 9.1 %collective-permute-start.8 = (bf16[32,64,512]{2,1,0:T(8,128)(2,1)}, bf16[32,64,512]{2,1,0:T(8,128)(2,1)}, u32[]{:S(2)}, u32[]{:S(2)}) collective-permute-start(bf16[32,64,512]{2,1,0:T(8,128)(2,1)} %param.4), channel_id=1, source_target_pairs={{2,0},{1,3},{6,4},{5,7},{10,8},{9,11},{14,12},{13,15},{18,16},{17,... | collective-permute-start | bytes 6291464 | tf_op jit(solution)/shard_map/ppermute | solution.py:309
  12.9 4.1 %copy.22 = bf16[32,64,512]{2,0,1:T(8,128)(2,1)} copy(bf16[32,64,512]{2,1,0:T(8,128)(2,1)} %param.4) | data formatting | bytes 4194304 | tf_op args[1]
  17.0 0.0 collective-permute-start
  17.0 0.0 collective-permute-done.1
  17.0 8.3 %collective-permute-done.2 = bf16[2,64,1536]{2,1,0:T(8,128)(2,1)S(1)} collective-permute-done((bf16[2,64,1536]{2,1,0:T(8,128)(2,1)S(1)}, bf16[2,64,1536]{2,1,0:T(8,128)(2,1)S(1)}, u32[]{:S(2)}, u32[]{:S(2)}) %collective-permute-start.2) | collective-permute-done | bytes 393248 | tf_op jit(solution)/shard_map/ppermute | solution.py:278
  25.3 0.0 collective-permute-done.3
  25.3 1.1 select_select_fusion.refs_0_
  26.4 1.6 collective-permute-start.4
  27.9 1.5 collective-permute-start.5
  29.5 0.5 collective-permute-start.6
  29.9 8.6 %collective-permute-done.4.refs_1_ = bf16[2,64,1536]{2,1,0:T(8,128)(2,1)S(1)} collective-permute-done((bf16[2,64,1536]{2,1,0:T(8,128)(2,1)S(1)}, bf16[2,64,1536]{2,1,0:T(8,128)(2,1)S(1)}, u32[]{:S(2)}, u32[]{:S(2)}) %collective-permute-start.4) | collective-permute-done | bytes 393248 | tf_op jit(solution)/shard_map/ppermute | solution.py:288
  38.5 6.4 %collective-permute-done.5.refs_2_ = bf16[2,64,1536]{2,1,0:T(8,128)(2,1)S(1)} collective-permute-done((bf16[2,64,1536]{2,1,0:T(8,128)(2,1)S(1)}, bf16[2,64,1536]{2,1,0:T(8,128)(2,1)S(1)}, u32[]{:S(2)}, u32[]{:S(2)}) %collective-permute-start.5) | collective-permute-done | bytes 393248 | tf_op jit(solution)/shard_map/ppermute | solution.py:288
  44.9 0.0 collective-permute-done.6.refs_3_
  44.9 1.3 shard_map.37
  46.2 0.0 collective-permute-start.7
  46.2 0.0 copy-start.1
  46.2 2.9 %slice.12.refs_2_ = bf16[48,32,512]{2,1,0:T(8,128)(2,1)} slice(bf16[64,32,512]{2,1,0:T(8,128)(2,1)} %bitcast.13.refs_2_.refs_0_), slice={[0:48], [0:32], [0:512]} | slice | bytes 3145728 | tf_op jit(solution)/shard_map/slice | solution.py:329
  49.1 1.9 %slice.13.refs_2_ = bf16[16,32,512]{2,1,0:T(8,128)(2,1)} slice(bf16[64,32,512]{2,1,0:T(8,128)(2,1)} %bitcast.13.refs_2_.refs_0_), slice={[48:64], [0:32], [0:512]} | slice | bytes 1048576 | tf_op jit(solution)/shard_map/slice | solution.py:329
  51.0 0.1 stack.35.refs_0_
  51.1 0.7 dynamic-slice_bitcast_fusion.refs_0_
  51.8 0.0 collective-permute-done.7.refs_2_
  51.8 0.0 copy-start.9
  51.8 1.1 copy-done.9
  52.9 0.0 copy-done.1
  52.9 4.1 %shard_map.38 = (bf16[2,1536,512]{2,1,0:T(8,128)(2,1)}, f32[8,128]{1,0:T(8,128)S(1)}) custom-call(s32[8]{0:T(128)S(1)} %stack.35.refs_0_, bf16[4,2,64,1536]{3,2,1,0:T(8,128)(2,1)S(1)} %copy-done.1, bf16[4,2,64,1536]{3,2,1,0:T(8,128)(2,1)} %copy-done.9, f32[8,128]{1,0:T(8,128)S(1)} %get-tuple-element.27.refs_3_), custom_call_target="tpu_custom_call", output_to_operand_aliasing={{1}: (3, {})} | custom-call | flops 1024 | bytes 1024 | tf_op jit(solution)/shard_map/pallas_call | solution.py:33
  57.0 25.9 %shard_map.39 = (bf16[48,2,128,512]{3,2,1,0:T(8,128)(2,1)}, f32[8,128]{1,0:T(8,128)S(1)}) custom-call(bf16[128,64,1536]{2,1,0:T(8,128)(2,1)} %refs_0_.3, bf16[2,1536,512]{2,1,0:T(8,128)(2,1)} %get-tuple-element.28.refs_1_, f32[8,128]{1,0:T(8,128)S(1)} %get-tuple-element.29.refs_2_), custom_call_target="tpu_custom_call", output_to_operand_aliasing={{1}: (2, {})} | custom-call | flops 1024 | bytes 1024 | tf_op jit(solution)/shard_map/pallas_call | solution.py:33
  83.0 0.0 collective-permute-done.refs_1_
  83.0 2.6 %shard_map.40 = (bf16[48,32,512]{2,1,0:T(8,128)(2,1)S(1)}, f32[8,128]{1,0:T(8,128)S(1)}) custom-call(s32[1]{0:T(128)} %bitcast.10.refs_0_, bf16[64,32,512]{2,1,0:T(8,128)(2,1)} %collective-permute-done.refs_1_, bf16[64,32,512]{2,1,0:T(8,128)(2,1)} %bitcast.13.refs_2_.refs_0_, f32[8,128]{1,0:T(8,128)S(1)} %get-tuple-element.30.refs_3_), custom_call_target="tpu_custom_call", output_to_operand_aliasing={{1}: (3, {})} | custom-call | flops 1024 | bytes 1024 | tf_op jit(solution)/shard_map/pallas_call | solution.py:33
  85.6 0.0 copy-start
  85.6 1.2 copy-done
  86.7 1.2 shard_map.41
  88.0 0.0 copy-start.4
  88.0 0.8 copy-done.4
  88.8 0.0 copy-start.5
  88.8 0.6 copy-done.5
  89.4 0.0 collective-permute-start.9
  89.4 11.0 %collective-permute-start.10 = (bf16[48,32,512]{2,1,0:T(8,128)(2,1)}, bf16[48,32,512]{2,1,0:T(8,128)(2,1)}, u32[]{:S(2)}, u32[]{:S(2)}) collective-permute-start(bf16[48,32,512]{2,1,0:T(8,128)(2,1)} %get-tuple-element.44), channel_id=1, source_target_pairs={{2,1},{1,2},{6,5},{5,6},{10,9},{9,10},{14,13},{13,14},{18,17},{17,... | collective-permute-start | bytes 4718600 | tf_op jit(solution)/shard_map/ppermute | solution.py:309
  100.4 0.0 copy-start.6
  100.4 0.7 copy-done.6
  101.1 11.4 %shard_map.43 = (bf16[16,2,128,512]{3,2,1,0:T(8,128)(2,1)}, f32[8,128]{1,0:T(8,128)S(1)}) custom-call(bf16[128,64,1536]{2,1,0:T(8,128)(2,1)} %refs_0_.3, bf16[2,1536,512]{2,1,0:T(8,128)(2,1)} %get-tuple-element.28.refs_1_, f32[8,128]{1,0:T(8,128)S(1)} %copy-done.6), custom_call_target="tpu_custom_call", output_to_operand_aliasing={{1}: (2, {})} | custom-call | flops 1024 | bytes 1024 | tf_op jit(solution)/shard_map/pallas_call | solution.py:33
  112.5 0.0 copy-start.7
  112.5 0.6 copy-done.7
  113.1 0.0 collective-permute-start.11
  113.1 3.9 %collective-permute-start.12 = (bf16[16,32,512]{2,1,0:T(8,128)(2,1)}, bf16[16,32,512]{2,1,0:T(8,128)(2,1)S(1)}, u32[]{:S(2)}, u32[]{:S(2)}) collective-permute-start(bf16[16,32,512]{2,1,0:T(8,128)(2,1)} %get-tuple-element.46), channel_id=1, source_target_pairs={{2,1},{1,2},{6,5},{5,6},{10,9},{9,10},{14,13},{13,14},{18,17},{17,... | collective-permute-start | bytes 1572872 | tf_op jit(solution)/shard_map/ppermute | solution.py:309
  116.9 0.0 collective-permute-done.8.refs_1_
  117.0 0.0 copy-start.8
  117.0 0.7 copy-done.8
  117.7 4.3 %shard_map.46 = (bf16[64,32,512]{2,1,0:T(8,128)(2,1)}, f32[8,128]{1,0:T(8,128)S(1)}) custom-call(bf16[32,64,512]{2,1,0:T(8,128)(2,1)} %get-tuple-element.38.refs_0_, f32[8,128]{1,0:T(8,128)S(1)} %copy-done.8), custom_call_target="tpu_custom_call", output_to_operand_aliasing={{1}: (1, {})} | custom-call | flops 1024 | bytes 1024 | tf_op jit(solution)/shard_map/pallas_call | solution.py:33
  121.9 3.5 %shard_map.48 = f32[96,256]{1,0:T(8,128)S(1)} custom-call(bf16[64,32,512]{2,1,0:T(8,128)(2,1)} %bitcast.13.refs_2_.refs_0_, bf16[64,32,512]{2,1,0:T(8,128)(2,1)} %collective-permute-done.refs_1_, bf16[64,32,512]{2,1,0:T(8,128)(2,1)} %get-tuple-element.40.refs_2_, bf16[16,2,128,512]{3,2,1,0:T(8,128)(2,1)} %get-tuple-element.42.refs_3_.refs_5_), custom_call_target="tpu_custom_call" | custom-call | flops 1024 | bytes 1024 | tf_op jit(solution)/shard_map/pallas_call | solution.py:33
  125.5 9.0 %shard_map.47 = f32[96,256]{1,0:T(8,128)S(1)} custom-call(bf16[64,32,512]{2,1,0:T(8,128)(2,1)} %bitcast.13.refs_2_.refs_0_, bf16[64,32,512]{2,1,0:T(8,128)(2,1)} %collective-permute-done.refs_1_, bf16[64,32,512]{2,1,0:T(8,128)(2,1)} %get-tuple-element.40.refs_2_, bf16[48,2,128,512]{3,2,1,0:T(8,128)(2,1)} %get-tuple-element.41.refs_3_.refs_2_), custom_call_target="tpu_custom_call" | custom-call | flops 1024 | bytes 1024 | tf_op jit(solution)/shard_map/pallas_call | solution.py:33
  134.6 12.3 %collective-permute-done.9.refs_0_ = bf16[48,32,512]{2,1,0:T(8,128)(2,1)S(1)} collective-permute-done((bf16[48,32,512]{2,1,0:T(8,128)(2,1)}, bf16[48,32,512]{2,1,0:T(8,128)(2,1)S(1)}, u32[]{:S(2)}, u32[]{:S(2)}) %collective-permute-start.9) | collective-permute-done | bytes 1572896 | tf_op jit(solution)/shard_map/ppermute | solution.py:309
  146.8 1.2 copy-done.2
  148.0 0.0 collective-permute-done.10.refs_1_
  148.1 1.4 copy-done.3
  149.5 8.3 %shard_map.50.refs_2_ = f32[64,256]{1,0:T(8,128)S(1)} custom-call(bf16[48,32,512]{2,1,0:T(8,128)(2,1)S(1)} %copy-done.3, bf16[48,32,512]{2,1,0:T(8,128)(2,1)} %collective-permute-done.10.refs_1_, bf16[48,2,128,512]{3,2,1,0:T(8,128)(2,1)} %get-tuple-element.41.refs_3_.refs_2_), custom_call_target="tpu_custom_call" | custom-call | flops 1024 | bytes 1024 | tf_op jit(solution)/shard_map/pallas_call | solution.py:33
  157.8 0.3 collective-permute-done.11.refs_3_
  158.1 1.0 collective-permute-done.12.refs_4_
  159.0 4.0 %shard_map.51 = f32[8,2,16,128]{3,2,1,0:T(8,128)S(1)} custom-call(s32[4]{0:T(128)S(1)} %dynamic-slice_bitcast_fusion.refs_0_, f32[96,256]{1,0:T(8,128)S(1)} %add.7.refs_1_, f32[64,256]{1,0:T(8,128)S(1)} %shard_map.50.refs_2_, bf16[16,32,512]{2,1,0:T(8,128)(2,1)S(1)} %collective-permute-done.11.refs_3_, ...), custom_call_target="tpu_custom_call" | custom-call | flops 1024 | bytes 1024 | tf_op jit(solution)/shard_map/pallas_call | solution.py:33
  163.0 9.0 %all_to_all.5 = f32[8,2,16,128]{3,2,1,0:T(8,128)S(1)} all-to-all(f32[8,2,16,128]{3,2,1,0:T(8,128)S(1)} %shard_map.51), channel_id=1, replica_groups=mesh['vir'=8,'out'=4] {'vir'}, dimensions={0} | all-to-all | bytes 262144 | tf_op jit(solution)/shard_map/all_to_all | solution.py:363
  172.1 0.6 reduce_sum.9
  (8 shorter events, 0.0 us)
Async XLA Ops:
  1.0 15.9 %collective-permute-start.1 = (bf16[2,64,1536]{2,1,0:T(8,128)(2,1)S(1)}, bf16[2,64,1536]{2,1,0:T(8,128)(2,1)S(1)}, u32[]{:S(2)}, u32[]{:S(2)}) collective-permute-start(bf16[2,64,1536]{2,1,0:T(8,128)(2,1)S(1)} %slice.9), channel_id=1, source_target_pairs={{0,3},{4,7},{8,11},{12,15},{16,19},{20,23},{24,27},{28,31}} | collective-permute-start | bytes 1179656 | tf_op jit(solution)/shard_map/ppermute | solution.py:278
  1.7 23.6 %collective-permute-start.2 = (bf16[2,64,1536]{2,1,0:T(8,128)(2,1)S(1)}, bf16[2,64,1536]{2,1,0:T(8,128)(2,1)S(1)}, u32[]{:S(2)}, u32[]{:S(2)}) collective-permute-start(bf16[2,64,1536]{2,1,0:T(8,128)(2,1)S(1)} %slice.9), channel_id=1, source_target_pairs={{0,2},{4,6},{8,10},{12,14},{16,18},{20,22},{24,26},{28,30}} | collective-permute-start | bytes 1179656 | tf_op jit(solution)/shard_map/ppermute | solution.py:278
  3.0 22.3 %collective-permute-start.3 = (bf16[2,64,1536]{2,1,0:T(8,128)(2,1)S(1)}, bf16[2,64,1536]{2,1,0:T(8,128)(2,1)S(1)}, u32[]{:S(2)}, u32[]{:S(2)}) collective-permute-start(bf16[2,64,1536]{2,1,0:T(8,128)(2,1)S(1)} %slice.9), channel_id=1, source_target_pairs={{0,1},{4,5},{8,9},{12,13},{16,17},{20,21},{24,25},{28,29}} | collective-permute-start | bytes 1179656 | tf_op jit(solution)/shard_map/ppermute | solution.py:278
  3.7 113.2 %collective-permute-start.8 = (bf16[32,64,512]{2,1,0:T(8,128)(2,1)}, bf16[32,64,512]{2,1,0:T(8,128)(2,1)}, u32[]{:S(2)}, u32[]{:S(2)}) collective-permute-start(bf16[32,64,512]{2,1,0:T(8,128)(2,1)} %param.4), channel_id=1, source_target_pairs={{2,0},{1,3},{6,4},{5,7},{10,8},{9,11},{14,12},{13,15},{18,16},{17,... | collective-permute-start | bytes 6291464 | tf_op jit(solution)/shard_map/ppermute | solution.py:309
  17.0 66.0 %collective-permute-start = (bf16[64,32,512]{2,1,0:T(8,128)(2,1)}, bf16[64,32,512]{2,1,0:T(8,128)(2,1)}, u32[]{:S(2)}, u32[]{:S(2)}) collective-permute-start(bf16[64,32,512]{2,1,0:T(8,128)(2,1)} %bitcast.13.refs_2_.refs_0_), channel_id=1, source_target_pairs={{3,1},{1,0},{0,2},{2,3},{7,5},{5,4},{4,6},{6,7},{11,9},{9,8},{8,10... | collective-permute-start | bytes 6291464 | tf_op jit(solution)/shard_map/ppermute | solution.py:309
  26.4 12.1 %collective-permute-start.4 = (bf16[2,64,1536]{2,1,0:T(8,128)(2,1)S(1)}, bf16[2,64,1536]{2,1,0:T(8,128)(2,1)S(1)}, u32[]{:S(2)}, u32[]{:S(2)}) collective-permute-start(bf16[2,64,1536]{2,1,0:T(8,128)(2,1)S(1)} %select_select_fusion.refs_0_), channel_id=1, source_target_pairs={{0,8},{4,12},{8,0},{12,4},{16,24},{20,28},{24,16},{28,20},{1,9},{5... | collective-permute-start | bytes 1179656 | tf_op jit(solution)/shard_map/ppermute | solution.py:288
  27.9 17.0 %collective-permute-start.5 = (bf16[2,64,1536]{2,1,0:T(8,128)(2,1)S(1)}, bf16[2,64,1536]{2,1,0:T(8,128)(2,1)S(1)}, u32[]{:S(2)}, u32[]{:S(2)}) collective-permute-start(bf16[2,64,1536]{2,1,0:T(8,128)(2,1)S(1)} %select_select_fusion.refs_0_), channel_id=1, source_target_pairs={{0,16},{4,20},{8,24},{12,28},{16,0},{20,4},{24,8},{28,12},{1,17},{... | collective-permute-start | bytes 1179656 | tf_op jit(solution)/shard_map/ppermute | solution.py:288
  29.5 15.5 %collective-permute-start.6 = (bf16[2,64,1536]{2,1,0:T(8,128)(2,1)S(1)}, bf16[2,64,1536]{2,1,0:T(8,128)(2,1)S(1)}, u32[]{:S(2)}, u32[]{:S(2)}) collective-permute-start(bf16[2,64,1536]{2,1,0:T(8,128)(2,1)S(1)} %select_select_fusion.refs_0_), channel_id=1, source_target_pairs={{0,24},{4,28},{8,16},{12,20},{16,8},{20,12},{24,0},{28,4},{1,25},{... | collective-permute-start | bytes 1179656 | tf_op jit(solution)/shard_map/ppermute | solution.py:288
  46.2 5.5 %collective-permute-start.7 = (bf16[4,2,64,1536]{3,2,1,0:T(8,128)(2,1)}, bf16[4,2,64,1536]{3,2,1,0:T(8,128)(2,1)S(1)}, u32[]{:S(2)}, u32[]{:S(2)}) collective-permute-start(bf16[4,2,64,1536]{3,2,1,0:T(8,128)(2,1)} %get-tuple-element.26.refs_1_), channel_id=1, source_target_pairs={{0,4},{4,0},{8,12},{12,8},{16,20},{20,16},{24,28},{28,24},{1,5},{5... | collective-permute-start | bytes 4718600 | tf_op jit(solution)/shard_map/ppermute | solution.py:288
  46.2 6.7 %copy-start.1 = (bf16[4,2,64,1536]{3,2,1,0:T(8,128)(2,1)S(1)}, bf16[4,2,64,1536]{3,2,1,0:T(8,128)(2,1)}, u32[]{:S(2)}) copy-start(bf16[4,2,64,1536]{3,2,1,0:T(8,128)(2,1)} %get-tuple-element.26.refs_1_) | copy-start | bytes 4718596
  51.8 1.1 copy-start.9
  85.6 1.2 copy-start
  88.0 0.8 copy-start.4
  88.8 0.6 copy-start.5
  89.4 57.5 %collective-permute-start.9 = (bf16[48,32,512]{2,1,0:T(8,128)(2,1)}, bf16[48,32,512]{2,1,0:T(8,128)(2,1)S(1)}, u32[]{:S(2)}, u32[]{:S(2)}) collective-permute-start(bf16[48,32,512]{2,1,0:T(8,128)(2,1)} %get-tuple-element.43), channel_id=1, source_target_pairs={{1,0},{0,1},{2,3},{3,2},{5,4},{4,5},{6,7},{7,6},{9,8},{8,9},{10,11... | collective-permute-start | bytes 4718600 | tf_op jit(solution)/shard_map/ppermute | solution.py:309
  89.4 58.7 %collective-permute-start.10 = (bf16[48,32,512]{2,1,0:T(8,128)(2,1)}, bf16[48,32,512]{2,1,0:T(8,128)(2,1)}, u32[]{:S(2)}, u32[]{:S(2)}) collective-permute-start(bf16[48,32,512]{2,1,0:T(8,128)(2,1)} %get-tuple-element.44), channel_id=1, source_target_pairs={{2,1},{1,2},{6,5},{5,6},{10,9},{9,10},{14,13},{13,14},{18,17},{17,... | collective-permute-start | bytes 4718600 | tf_op jit(solution)/shard_map/ppermute | solution.py:309
  100.4 0.7 copy-start.6
  112.5 0.6 copy-start.7
  113.1 45.0 %collective-permute-start.11 = (bf16[16,32,512]{2,1,0:T(8,128)(2,1)}, bf16[16,32,512]{2,1,0:T(8,128)(2,1)S(1)}, u32[]{:S(2)}, u32[]{:S(2)}) collective-permute-start(bf16[16,32,512]{2,1,0:T(8,128)(2,1)} %get-tuple-element.45), channel_id=1, source_target_pairs={{1,0},{0,1},{2,3},{3,2},{5,4},{4,5},{6,7},{7,6},{9,8},{8,9},{10,11... | collective-permute-start | bytes 1572872 | tf_op jit(solution)/shard_map/ppermute | solution.py:309
  113.1 46.0 %collective-permute-start.12 = (bf16[16,32,512]{2,1,0:T(8,128)(2,1)}, bf16[16,32,512]{2,1,0:T(8,128)(2,1)S(1)}, u32[]{:S(2)}, u32[]{:S(2)}) collective-permute-start(bf16[16,32,512]{2,1,0:T(8,128)(2,1)} %get-tuple-element.46), channel_id=1, source_target_pairs={{2,1},{1,2},{6,5},{5,6},{10,9},{9,10},{14,13},{13,14},{18,17},{17,... | collective-permute-start | bytes 1572872 | tf_op jit(solution)/shard_map/ppermute | solution.py:309
  117.0 0.7 copy-start.8
  146.8 1.2 copy-start.2
  148.0 1.4 copy-start.3

commit v10 on v8

--- a/solution.py
+++ b/solution.py
@@ -275,8 +275,9 @@
 
 
 def spread(rows, n, z):
-    heres = [lax.ppermute(rows, "out", [(0, k)]) for k in range(n - 1, 0, -1)]
-    for k, here in zip(range(n - 1, 0, -1), heres):
+    order = [1] + list(range(n - 1, 1, -1))
+    heres = [lax.ppermute(rows, "out", [(0, k)]) for k in order]
+    for k, here in zip(order, heres):
         rows = jnp.where(z == k, here, rows)
     return rows
 

time: 175 us -> 172 us (0.983)
  waiting for transfers between devices: 39.3 us -> 31.2 us
  starting transfers between devices: 29.8 us -> 34.9 us
    ppermute x3, waiting for transfers between devices: 7.62 us -> 0.01 us  [spread(): heres = [lax.ppermute(rows, 'out', [(0, k)]) for k in order]]
    ppermute x6, starting transfers between devices: 23.6 us -> 28.6 us  [send(): return lax.ppermute(array, 'out', ways)]
    ppermute x6, waiting for transfers between devices: 16.7 us -> 14.8 us  [send(): return lax.ppermute(array, 'out', ways)]
  transfers between devices with their start and end apart: 13 -> 13, of which waited for: 6 -> 6; matrix products, arithmetic and copies ran while one was open for 6% -> 6% of each run, Pallas kernels for 41% -> 42%
where the time goes in v10:
time: 172 us; the launch traced here: 171 us
  Pallas kernels  74.9 us (44%)
  starting transfers between devices  34.9 us (20%)
  waiting for transfers between devices  31.2 us (18%)
  local copies, waits for them, and re-layouts  18.9 us (11%)
  blocking collectives  9.03 us (5%)
    pallas_call x11, Pallas kernels, call(): pl.pallas_call(run, grid=grid, in_specs=list(in_specs) + [anywhere] * n_t...  74.9 us
    ppermute x6, starting transfers between devices, send(): return lax.ppermute(array, 'out', ways)  28.6 us
    ppermute x4, waiting for transfers between devices, swap(): return lax.ppermute(array, 'vir', [(k, k ^ mask) for k in range(vir)])  16.4 us
    ppermute x6, waiting for transfers between devices, send(): return lax.ppermute(array, 'out', ways)  14.8 us
    unnamed x21, local copies, waits for them, and re-layouts  12.4 us
    all_to_all x1, blocking collectives, body(): swapped = lax.all_to_all(parts, 'vir', split_axis=0, concat_axis=0)  9.03 us
    slice x2, local copies, waits for them, and re-layouts, body(): onward, kept = ([], [own[i:j] for i, j in spans])  4.76 us
    ppermute x4, starting transfers between devices, swap(): return lax.ppermute(array, 'vir', [(k, k ^ mask) for k in range(vir)])  3.56 us
  transfers between devices with their start and end apart: 13, of which 6 were waited for; matrix products, arithmetic and copies ran while one was open for 6% of the time, Pallas kernels for 42%

profile of v10, /device:TPU:16, one launch (start us, length us, event | category | flops | bytes accessed | tf_op | source)
XLA Modules:
  0.0 170.8 jit_solution(14097521893925604818)
XLA Ops:
  0.0 1.0 slice.9
  1.0 1.3 collective-permute-start.1
  2.3 0.7 collective-permute-start.2
  3.0 0.7 collective-permute-start.3
  3.7 8.5 %collective-permute-start.8 = (bf16[32,64,512]{2,1,0:T(8,128)(2,1)}, bf16[32,64,512]{2,1,0:T(8,128)(2,1)}, u32[]{:S(2)}, u32[]{:S(2)}) collective-permute-start(bf16[32,64,512]{2,1,0:T(8,128)(2,1)} %param.4), channel_id=1, source_target_pairs={{2,0},{1,3},{6,4},{5,7},{10,8},{9,11},{14,12},{13,15},{18,16},{17,... | collective-permute-start | bytes 6291464 | tf_op jit(solution)/shard_map/ppermute | solution.py:310
  12.2 4.1 %copy.22 = bf16[32,64,512]{2,0,1:T(8,128)(2,1)} copy(bf16[32,64,512]{2,1,0:T(8,128)(2,1)} %param.4) | data formatting | bytes 4194304 | tf_op args[1]
  16.3 0.0 collective-permute-start
  16.3 0.0 collective-permute-done.1
  16.3 0.0 collective-permute-done.2
  16.4 0.0 collective-permute-done.3
  16.4 1.1 select_select_fusion.refs_0_
  17.4 1.6 collective-permute-start.4
  19.0 1.5 collective-permute-start.5
  20.5 0.5 collective-permute-start.6
  21.0 8.6 %collective-permute-done.4.refs_1_ = bf16[2,64,1536]{2,1,0:T(8,128)(2,1)S(1)} collective-permute-done((bf16[2,64,1536]{2,1,0:T(8,128)(2,1)S(1)}, bf16[2,64,1536]{2,1,0:T(8,128)(2,1)S(1)}, u32[]{:S(2)}, u32[]{:S(2)}) %collective-permute-start.4) | collective-permute-done | bytes 393248 | tf_op jit(solution)/shard_map/ppermute | solution.py:289
  29.6 7.9 %collective-permute-done.5.refs_2_ = bf16[2,64,1536]{2,1,0:T(8,128)(2,1)S(1)} collective-permute-done((bf16[2,64,1536]{2,1,0:T(8,128)(2,1)S(1)}, bf16[2,64,1536]{2,1,0:T(8,128)(2,1)S(1)}, u32[]{:S(2)}, u32[]{:S(2)}) %collective-permute-start.5) | collective-permute-done | bytes 393248 | tf_op jit(solution)/shard_map/ppermute | solution.py:289
  37.4 0.0 collective-permute-done.6.refs_3_
  37.4 1.3 shard_map.37
  38.7 0.0 collective-permute-start.7
  38.7 0.0 copy-start.1
  38.7 2.9 %slice.12.refs_2_ = bf16[48,32,512]{2,1,0:T(8,128)(2,1)} slice(bf16[64,32,512]{2,1,0:T(8,128)(2,1)} %bitcast.13.refs_2_.refs_0_), slice={[0:48], [0:32], [0:512]} | slice | bytes 3145728 | tf_op jit(solution)/shard_map/slice | solution.py:330
  41.6 1.9 %slice.13.refs_2_ = bf16[16,32,512]{2,1,0:T(8,128)(2,1)} slice(bf16[64,32,512]{2,1,0:T(8,128)(2,1)} %bitcast.13.refs_2_.refs_0_), slice={[48:64], [0:32], [0:512]} | slice | bytes 1048576 | tf_op jit(solution)/shard_map/slice | solution.py:330
  43.5 0.1 stack.35.refs_0_
  43.6 0.7 dynamic-slice_bitcast_fusion.refs_0_
  44.3 0.0 collective-permute-done.7.refs_2_
  44.3 0.0 copy-start.9
  44.3 1.1 copy-done.9
  45.4 0.0 copy-done.1
  45.4 4.1 %shard_map.38 = (bf16[2,1536,512]{2,1,0:T(8,128)(2,1)}, f32[8,128]{1,0:T(8,128)S(1)}) custom-call(s32[8]{0:T(128)S(1)} %stack.35.refs_0_, bf16[4,2,64,1536]{3,2,1,0:T(8,128)(2,1)S(1)} %copy-done.1, bf16[4,2,64,1536]{3,2,1,0:T(8,128)(2,1)} %copy-done.9, f32[8,128]{1,0:T(8,128)S(1)} %get-tuple-element.27.refs_3_), custom_call_target="tpu_custom_call", output_to_operand_aliasing={{1}: (3, {})} | custom-call | flops 1024 | bytes 1024 | tf_op jit(solution)/shard_map/pallas_call | solution.py:33
  49.5 25.9 %shard_map.39 = (bf16[48,2,128,512]{3,2,1,0:T(8,128)(2,1)}, f32[8,128]{1,0:T(8,128)S(1)}) custom-call(bf16[128,64,1536]{2,1,0:T(8,128)(2,1)} %refs_0_.3, bf16[2,1536,512]{2,1,0:T(8,128)(2,1)} %get-tuple-element.28.refs_1_, f32[8,128]{1,0:T(8,128)S(1)} %get-tuple-element.29.refs_2_), custom_call_target="tpu_custom_call", output_to_operand_aliasing={{1}: (2, {})} | custom-call | flops 1024 | bytes 1024 | tf_op jit(solution)/shard_map/pallas_call | solution.py:33
  75.5 1.3 collective-permute-done.refs_1_
  76.8 2.6 %shard_map.40 = (bf16[48,32,512]{2,1,0:T(8,128)(2,1)S(1)}, f32[8,128]{1,0:T(8,128)S(1)}) custom-call(s32[1]{0:T(128)} %bitcast.10.refs_0_, bf16[64,32,512]{2,1,0:T(8,128)(2,1)} %collective-permute-done.refs_1_, bf16[64,32,512]{2,1,0:T(8,128)(2,1)} %bitcast.13.refs_2_.refs_0_, f32[8,128]{1,0:T(8,128)S(1)} %get-tuple-element.30.refs_3_), custom_call_target="tpu_custom_call", output_to_operand_aliasing={{1}: (3, {})} | custom-call | flops 1024 | bytes 1024 | tf_op jit(solution)/shard_map/pallas_call | solution.py:33
  79.3 0.0 copy-start
  79.3 1.2 copy-done
  80.5 1.2 shard_map.41
  81.7 0.0 copy-start.4
  81.8 0.8 copy-done.4
  82.6 0.0 copy-start.5
  82.6 0.6 copy-done.5
  83.2 6.7 %collective-permute-start.9 = (bf16[48,32,512]{2,1,0:T(8,128)(2,1)}, bf16[48,32,512]{2,1,0:T(8,128)(2,1)S(1)}, u32[]{:S(2)}, u32[]{:S(2)}) collective-permute-start(bf16[48,32,512]{2,1,0:T(8,128)(2,1)} %get-tuple-element.43), channel_id=1, source_target_pairs={{1,0},{0,1},{2,3},{3,2},{5,4},{4,5},{6,7},{7,6},{9,8},{8,9},{10,11... | collective-permute-start | bytes 4718600 | tf_op jit(solution)/shard_map/ppermute | solution.py:310
  89.8 9.6 %collective-permute-start.10 = (bf16[48,32,512]{2,1,0:T(8,128)(2,1)}, bf16[48,32,512]{2,1,0:T(8,128)(2,1)}, u32[]{:S(2)}, u32[]{:S(2)}) collective-permute-start(bf16[48,32,512]{2,1,0:T(8,128)(2,1)} %get-tuple-element.44), channel_id=1, source_target_pairs={{2,1},{1,2},{6,5},{5,6},{10,9},{9,10},{14,13},{13,14},{18,17},{17,... | collective-permute-start | bytes 4718600 | tf_op jit(solution)/shard_map/ppermute | solution.py:310
  99.4 0.0 copy-start.6
  99.4 0.7 copy-done.6
  100.1 11.4 %shard_map.43 = (bf16[16,2,128,512]{3,2,1,0:T(8,128)(2,1)}, f32[8,128]{1,0:T(8,128)S(1)}) custom-call(bf16[128,64,1536]{2,1,0:T(8,128)(2,1)} %refs_0_.3, bf16[2,1536,512]{2,1,0:T(8,128)(2,1)} %get-tuple-element.28.refs_1_, f32[8,128]{1,0:T(8,128)S(1)} %copy-done.6), custom_call_target="tpu_custom_call", output_to_operand_aliasing={{1}: (2, {})} | custom-call | flops 1024 | bytes 1024 | tf_op jit(solution)/shard_map/pallas_call | solution.py:33
  111.5 0.0 copy-start.7
  111.5 0.6 copy-done.7
  112.1 0.0 collective-permute-start.11
  112.1 3.9 %collective-permute-start.12 = (bf16[16,32,512]{2,1,0:T(8,128)(2,1)}, bf16[16,32,512]{2,1,0:T(8,128)(2,1)S(1)}, u32[]{:S(2)}, u32[]{:S(2)}) collective-permute-start(bf16[16,32,512]{2,1,0:T(8,128)(2,1)} %get-tuple-element.46), channel_id=1, source_target_pairs={{2,1},{1,2},{6,5},{5,6},{10,9},{9,10},{14,13},{13,14},{18,17},{17,... | collective-permute-start | bytes 1572872 | tf_op jit(solution)/shard_map/ppermute | solution.py:310
  116.0 0.0 collective-permute-done.8.refs_1_
  116.0 0.0 copy-start.8
  116.0 0.7 copy-done.8
  116.7 4.3 %shard_map.46 = (bf16[64,32,512]{2,1,0:T(8,128)(2,1)}, f32[8,128]{1,0:T(8,128)S(1)}) custom-call(bf16[32,64,512]{2,1,0:T(8,128)(2,1)} %get-tuple-element.38.refs_0_, f32[8,128]{1,0:T(8,128)S(1)} %copy-done.8), custom_call_target="tpu_custom_call", output_to_operand_aliasing={{1}: (1, {})} | custom-call | flops 1024 | bytes 1024 | tf_op jit(solution)/shard_map/pallas_call | solution.py:33
  121.0 3.5 %shard_map.48 = f32[96,256]{1,0:T(8,128)S(1)} custom-call(bf16[64,32,512]{2,1,0:T(8,128)(2,1)} %bitcast.13.refs_2_.refs_0_, bf16[64,32,512]{2,1,0:T(8,128)(2,1)} %collective-permute-done.refs_1_, bf16[64,32,512]{2,1,0:T(8,128)(2,1)} %get-tuple-element.40.refs_2_, bf16[16,2,128,512]{3,2,1,0:T(8,128)(2,1)} %get-tuple-element.42.refs_3_.refs_5_), custom_call_target="tpu_custom_call" | custom-call | flops 1024 | bytes 1024 | tf_op jit(solution)/shard_map/pallas_call | solution.py:33
  124.5 9.0 %shard_map.47 = f32[96,256]{1,0:T(8,128)S(1)} custom-call(bf16[64,32,512]{2,1,0:T(8,128)(2,1)} %bitcast.13.refs_2_.refs_0_, bf16[64,32,512]{2,1,0:T(8,128)(2,1)} %collective-permute-done.refs_1_, bf16[64,32,512]{2,1,0:T(8,128)(2,1)} %get-tuple-element.40.refs_2_, bf16[48,2,128,512]{3,2,1,0:T(8,128)(2,1)} %get-tuple-element.41.refs_3_.refs_2_), custom_call_target="tpu_custom_call" | custom-call | flops 1024 | bytes 1024 | tf_op jit(solution)/shard_map/pallas_call | solution.py:33
  133.6 12.2 %collective-permute-done.9.refs_0_ = bf16[48,32,512]{2,1,0:T(8,128)(2,1)S(1)} collective-permute-done((bf16[48,32,512]{2,1,0:T(8,128)(2,1)}, bf16[48,32,512]{2,1,0:T(8,128)(2,1)S(1)}, u32[]{:S(2)}, u32[]{:S(2)}) %collective-permute-start.9) | collective-permute-done | bytes 1572896 | tf_op jit(solution)/shard_map/ppermute | solution.py:310
  145.9 1.2 copy-done.2
  147.1 0.0 collective-permute-done.10.refs_1_
  147.1 1.4 copy-done.3
  148.5 8.3 %shard_map.50.refs_2_ = f32[64,256]{1,0:T(8,128)S(1)} custom-call(bf16[48,32,512]{2,1,0:T(8,128)(2,1)S(1)} %copy-done.3, bf16[48,32,512]{2,1,0:T(8,128)(2,1)} %collective-permute-done.10.refs_1_, bf16[48,2,128,512]{3,2,1,0:T(8,128)(2,1)} %get-tuple-element.41.refs_3_.refs_2_), custom_call_target="tpu_custom_call" | custom-call | flops 1024 | bytes 1024 | tf_op jit(solution)/shard_map/pallas_call | solution.py:33
  156.8 0.3 collective-permute-done.11.refs_3_
  157.1 1.0 collective-permute-done.12.refs_4_
  158.0 3.1 %shard_map.51 = f32[8,2,16,128]{3,2,1,0:T(8,128)S(1)} custom-call(s32[4]{0:T(128)S(1)} %dynamic-slice_bitcast_fusion.refs_0_, f32[96,256]{1,0:T(8,128)S(1)} %add.7.refs_1_, f32[64,256]{1,0:T(8,128)S(1)} %shard_map.50.refs_2_, bf16[16,32,512]{2,1,0:T(8,128)(2,1)S(1)} %collective-permute-done.11.refs_3_, ...), custom_call_target="tpu_custom_call" | custom-call | flops 1024 | bytes 1024 | tf_op jit(solution)/shard_map/pallas_call | solution.py:33
  161.2 9.0 %all_to_all.5 = f32[8,2,16,128]{3,2,1,0:T(8,128)S(1)} all-to-all(f32[8,2,16,128]{3,2,1,0:T(8,128)S(1)} %shard_map.51), channel_id=1, replica_groups=mesh['vir'=8,'out'=4] {'vir'}, dimensions={0} | all-to-all | bytes 262144 | tf_op jit(solution)/shard_map/all_to_all | solution.py:364
  170.2 0.6 reduce_sum.9
  (8 shorter events, 0.0 us)
Async XLA Ops:
  1.0 15.3 %collective-permute-start.1 = (bf16[2,64,1536]{2,1,0:T(8,128)(2,1)S(1)}, bf16[2,64,1536]{2,1,0:T(8,128)(2,1)S(1)}, u32[]{:S(2)}, u32[]{:S(2)}) collective-permute-start(bf16[2,64,1536]{2,1,0:T(8,128)(2,1)S(1)} %slice.9), channel_id=1, source_target_pairs={{0,2},{4,6},{8,10},{12,14},{16,18},{20,22},{24,26},{28,30}} | collective-permute-start | bytes 1179656 | tf_op jit(solution)/shard_map/ppermute | solution.py:279
  2.3 14.0 %collective-permute-start.2 = (bf16[2,64,1536]{2,1,0:T(8,128)(2,1)S(1)}, bf16[2,64,1536]{2,1,0:T(8,128)(2,1)S(1)}, u32[]{:S(2)}, u32[]{:S(2)}) collective-permute-start(bf16[2,64,1536]{2,1,0:T(8,128)(2,1)S(1)} %slice.9), channel_id=1, source_target_pairs={{0,3},{4,7},{8,11},{12,15},{16,19},{20,23},{24,27},{28,31}} | collective-permute-start | bytes 1179656 | tf_op jit(solution)/shard_map/ppermute | solution.py:279
  3.0 13.3 %collective-permute-start.3 = (bf16[2,64,1536]{2,1,0:T(8,128)(2,1)S(1)}, bf16[2,64,1536]{2,1,0:T(8,128)(2,1)S(1)}, u32[]{:S(2)}, u32[]{:S(2)}) collective-permute-start(bf16[2,64,1536]{2,1,0:T(8,128)(2,1)S(1)} %slice.9), channel_id=1, source_target_pairs={{0,1},{4,5},{8,9},{12,13},{16,17},{20,21},{24,25},{28,29}} | collective-permute-start | bytes 1179656 | tf_op jit(solution)/shard_map/ppermute | solution.py:279
  3.7 112.3 %collective-permute-start.8 = (bf16[32,64,512]{2,1,0:T(8,128)(2,1)}, bf16[32,64,512]{2,1,0:T(8,128)(2,1)}, u32[]{:S(2)}, u32[]{:S(2)}) collective-permute-start(bf16[32,64,512]{2,1,0:T(8,128)(2,1)} %param.4), channel_id=1, source_target_pairs={{2,0},{1,3},{6,4},{5,7},{10,8},{9,11},{14,12},{13,15},{18,16},{17,... | collective-permute-start | bytes 6291464 | tf_op jit(solution)/shard_map/ppermute | solution.py:310
  16.3 60.4 %collective-permute-start = (bf16[64,32,512]{2,1,0:T(8,128)(2,1)}, bf16[64,32,512]{2,1,0:T(8,128)(2,1)}, u32[]{:S(2)}, u32[]{:S(2)}) collective-permute-start(bf16[64,32,512]{2,1,0:T(8,128)(2,1)} %bitcast.13.refs_2_.refs_0_), channel_id=1, source_target_pairs={{3,1},{1,0},{0,2},{2,3},{7,5},{5,4},{4,6},{6,7},{11,9},{9,8},{8,10... | collective-permute-start | bytes 6291464 | tf_op jit(solution)/shard_map/ppermute | solution.py:310
  17.4 12.1 %collective-permute-start.4 = (bf16[2,64,1536]{2,1,0:T(8,128)(2,1)S(1)}, bf16[2,64,1536]{2,1,0:T(8,128)(2,1)S(1)}, u32[]{:S(2)}, u32[]{:S(2)}) collective-permute-start(bf16[2,64,1536]{2,1,0:T(8,128)(2,1)S(1)} %select_select_fusion.refs_0_), channel_id=1, source_target_pairs={{0,8},{4,12},{8,0},{12,4},{16,24},{20,28},{24,16},{28,20},{1,9},{5... | collective-permute-start | bytes 1179656 | tf_op jit(solution)/shard_map/ppermute | solution.py:289
  19.0 18.4 %collective-permute-start.5 = (bf16[2,64,1536]{2,1,0:T(8,128)(2,1)S(1)}, bf16[2,64,1536]{2,1,0:T(8,128)(2,1)S(1)}, u32[]{:S(2)}, u32[]{:S(2)}) collective-permute-start(bf16[2,64,1536]{2,1,0:T(8,128)(2,1)S(1)} %select_select_fusion.refs_0_), channel_id=1, source_target_pairs={{0,16},{4,20},{8,24},{12,28},{16,0},{20,4},{24,8},{28,12},{1,17},{... | collective-permute-start | bytes 1179656 | tf_op jit(solution)/shard_map/ppermute | solution.py:289
  20.5 16.9 %collective-permute-start.6 = (bf16[2,64,1536]{2,1,0:T(8,128)(2,1)S(1)}, bf16[2,64,1536]{2,1,0:T(8,128)(2,1)S(1)}, u32[]{:S(2)}, u32[]{:S(2)}) collective-permute-start(bf16[2,64,1536]{2,1,0:T(8,128)(2,1)S(1)} %select_select_fusion.refs_0_), channel_id=1, source_target_pairs={{0,24},{4,28},{8,16},{12,20},{16,8},{20,12},{24,0},{28,4},{1,25},{... | collective-permute-start | bytes 1179656 | tf_op jit(solution)/shard_map/ppermute | solution.py:289
  38.7 5.5 %collective-permute-start.7 = (bf16[4,2,64,1536]{3,2,1,0:T(8,128)(2,1)}, bf16[4,2,64,1536]{3,2,1,0:T(8,128)(2,1)S(1)}, u32[]{:S(2)}, u32[]{:S(2)}) collective-permute-start(bf16[4,2,64,1536]{3,2,1,0:T(8,128)(2,1)} %get-tuple-element.26.refs_1_), channel_id=1, source_target_pairs={{0,4},{4,0},{8,12},{12,8},{16,20},{20,16},{24,28},{28,24},{1,5},{5... | collective-permute-start | bytes 4718600 | tf_op jit(solution)/shard_map/ppermute | solution.py:289
  38.7 6.7 %copy-start.1 = (bf16[4,2,64,1536]{3,2,1,0:T(8,128)(2,1)S(1)}, bf16[4,2,64,1536]{3,2,1,0:T(8,128)(2,1)}, u32[]{:S(2)}) copy-start(bf16[4,2,64,1536]{3,2,1,0:T(8,128)(2,1)} %get-tuple-element.26.refs_1_) | copy-start | bytes 4718596
  44.3 1.1 copy-start.9
  79.3 1.2 copy-start
  81.7 0.8 copy-start.4
  82.6 0.6 copy-start.5
  83.2 62.7 %collective-permute-start.9 = (bf16[48,32,512]{2,1,0:T(8,128)(2,1)}, bf16[48,32,512]{2,1,0:T(8,128)(2,1)S(1)}, u32[]{:S(2)}, u32[]{:S(2)}) collective-permute-start(bf16[48,32,512]{2,1,0:T(8,128)(2,1)} %get-tuple-element.43), channel_id=1, source_target_pairs={{1,0},{0,1},{2,3},{3,2},{5,4},{4,5},{6,7},{7,6},{9,8},{8,9},{10,11... | collective-permute-start | bytes 4718600 | tf_op jit(solution)/shard_map/ppermute | solution.py:310
  89.8 57.2 %collective-permute-start.10 = (bf16[48,32,512]{2,1,0:T(8,128)(2,1)}, bf16[48,32,512]{2,1,0:T(8,128)(2,1)}, u32[]{:S(2)}, u32[]{:S(2)}) collective-permute-start(bf16[48,32,512]{2,1,0:T(8,128)(2,1)} %get-tuple-element.44), channel_id=1, source_target_pairs={{2,1},{1,2},{6,5},{5,6},{10,9},{9,10},{14,13},{13,14},{18,17},{17,... | collective-permute-start | bytes 4718600 | tf_op jit(solution)/shard_map/ppermute | solution.py:310
  99.4 0.7 copy-start.6
  111.5 0.6 copy-start.7
  112.1 44.9 %collective-permute-start.11 = (bf16[16,32,512]{2,1,0:T(8,128)(2,1)}, bf16[16,32,512]{2,1,0:T(8,128)(2,1)S(1)}, u32[]{:S(2)}, u32[]{:S(2)}) collective-permute-start(bf16[16,32,512]{2,1,0:T(8,128)(2,1)} %get-tuple-element.45), channel_id=1, source_target_pairs={{1,0},{0,1},{2,3},{3,2},{5,4},{4,5},{6,7},{7,6},{9,8},{8,9},{10,11... | collective-permute-start | bytes 1572872 | tf_op jit(solution)/shard_map/ppermute | solution.py:310
  112.1 45.9 %collective-permute-start.12 = (bf16[16,32,512]{2,1,0:T(8,128)(2,1)}, bf16[16,32,512]{2,1,0:T(8,128)(2,1)S(1)}, u32[]{:S(2)}, u32[]{:S(2)}) collective-permute-start(bf16[16,32,512]{2,1,0:T(8,128)(2,1)} %get-tuple-element.46), channel_id=1, source_target_pairs={{2,1},{1,2},{6,5},{5,6},{10,9},{9,10},{14,13},{13,14},{18,17},{17,... | collective-permute-start | bytes 1572872 | tf_op jit(solution)/shard_map/ppermute | solution.py:310
  116.0 0.7 copy-start.8
  145.9 1.2 copy-start.2
  147.1 1.4 copy-start.3
